TPU v7x, 256 devices: a whole 4x4x8 slice. The times are simulated.
256 devices in a mesh: exp: 32 (over y, x, core), tp: 8 (over z).
Axes of the slice: x: 4, y: 4, z: 8, core: 2. Of those that a mesh axis runs over, the one named last changes fastest.
Arguments:
- activations: bfloat16 [4096, 3584], P('exp'), may hold values from -6 to 6
- out_grad: bfloat16 [4096, 3584], P('exp'), may hold values from -6 to 6
- expert_ids: int32 [4096, 2], P('exp'), may hold values from 0 to 15, all different within a row; in each aligned block of 128 rows (0 to 127, 128 to 255, ...) at most 32 rows name the same one
- gate_values: float32 [4096, 2], P('exp'), may hold values from 0.1 to 0.9
- gate_proj: bfloat16 [32, 1536, 3584], P('exp', 'tp'), may hold values from -0.09375 to 0.09375
- up_proj: bfloat16 [32, 1536, 3584], P('exp', 'tp'), may hold values from -0.09375 to 0.09375
- down_proj: bfloat16 [32, 1536, 3584], P('exp', 'tp'), may hold values from -0.109375 to 0.109375
Outputs:
- in_grad: bfloat16 [4096, 3584], P('exp')
- gate_grad: bfloat16 [32, 1536, 3584], P('exp', 'tp')
- up_grad: bfloat16 [32, 1536, 3584], P('exp', 'tp')
- down_grad: bfloat16 [32, 1536, 3584], P('exp', 'tp')
Inputs may be any that keep to these rules, and one draw needn't show every extreme that they name: `expert_ids`: each row names two different experts. Within the 128 rows of one index of exp no expert is named by more than 32 rows, and in some such block one expert is named by exactly 32 rows.
All inputs are finite; a program needn't handle non-finite values.
Results may differ from a plain program's by a relative error of at most 0.02.
Values may be sent and summed in bfloat16 or wider, within the bound.
No kernel may reach another device: no remote copies, remote signals or barrier semaphores. Data moves between devices by JAX's collectives and lax.ppermute only.
A program may use at most 128 MiB of HBM per device.

v0:
```python
import jax
import jax.numpy as jnp
from jax import lax
from jax.sharding import PartitionSpec as P


def route_tables(expert_ids, gate_values, experts, slot_count):
    tok_count = expert_ids.shape[0]
    flat_ids = expert_ids.reshape(-1)
    onehot = (flat_ids[:, None] == jnp.arange(experts, dtype=jnp.int32)[None, :]).astype(jnp.int32)
    before = jnp.cumsum(onehot, axis=0) - onehot
    ranking = jnp.sum(before * onehot, axis=1)
    slot_hot = (ranking[:, None] == jnp.arange(slot_count, dtype=jnp.int32)[None, :]).astype(
        jnp.float32
    )
    onehot_f = onehot.astype(jnp.float32)
    routing = jnp.einsum("pe,pc->pec", onehot_f, slot_hot).reshape(
        tok_count, 2, experts, slot_count
    )
    routing = jnp.transpose(jnp.sum(routing, axis=1), (1, 2, 0))
    weighted = jnp.sum(onehot_f.reshape(tok_count, 2, experts) * gate_values[:, :, None], axis=1)
    slot_gate = jnp.einsum("ect,te->ec", routing, weighted, precision=lax.Precision.HIGHEST)
    return (routing, slot_gate)


def dispatch(routing, slot_gate, activations, out_grad):
    select = routing.astype(jnp.bfloat16)
    sent_rows = jnp.einsum(
        "ect,td->ecd", select, activations, preferred_element_type=jnp.float32
    ).astype(jnp.bfloat16)
    picked = jnp.einsum("ect,td->ecd", select, out_grad, preferred_element_type=jnp.float32)
    sent_grads = (picked * slot_gate[:, :, None]).astype(jnp.bfloat16)
    return (sent_rows, sent_grads)


def forward_part(rows_in, gate_w, up_w):
    pre_gate = jnp.einsum("sd,ud->su", rows_in, gate_w, preferred_element_type=jnp.float32)
    pre_up = jnp.einsum("sd,ud->su", rows_in, up_w, preferred_element_type=jnp.float32)
    sigmoid_gate = jax.nn.sigmoid(pre_gate)
    silu_gate = pre_gate * sigmoid_gate
    hidden = (silu_gate * pre_up).astype(jnp.bfloat16)
    return (pre_gate, pre_up, sigmoid_gate, silu_gate, hidden)


def backward_part(state, grads_in, gate_w, up_w, down_w):
    pre_gate, pre_up, sigmoid_gate, silu_gate, hidden = state
    back = jnp.einsum("sd,ud->su", grads_in, down_w, preferred_element_type=jnp.float32)
    d_gate = (back * pre_up * sigmoid_gate * (1.0 + pre_gate * (1.0 - sigmoid_gate))).astype(
        jnp.bfloat16
    )
    d_up = (back * silu_gate).astype(jnp.bfloat16)
    partial_value = jnp.einsum("su,ud->sd", d_gate, gate_w, preferred_element_type=jnp.float32)
    partial_value = partial_value + jnp.einsum(
        "su,ud->sd", d_up, up_w, preferred_element_type=jnp.float32
    )
    return (partial_value.astype(jnp.bfloat16), d_gate, d_up)


def weight_grads(rows_in, grads_in, hidden, d_gate, d_up):
    gate_g = jnp.einsum("su,sd->ud", d_gate, rows_in, preferred_element_type=jnp.float32).astype(
        jnp.bfloat16
    )
    up_g = jnp.einsum("su,sd->ud", d_up, rows_in, preferred_element_type=jnp.float32).astype(
        jnp.bfloat16
    )
    down_g = jnp.einsum("su,sd->ud", hidden, grads_in, preferred_element_type=jnp.float32).astype(
        jnp.bfloat16
    )
    return (gate_g[None], up_g[None], down_g[None])


def per_device(activations, out_grad, expert_ids, gate_values, gate_proj, up_proj, down_proj):
    devices = lax.axis_size("exp")
    experts = devices // 2
    tok_count = activations.shape[0]
    model_width = activations.shape[1]
    slot_count = 8 * tok_count // devices
    routing, slot_gate = route_tables(expert_ids, gate_values, experts, slot_count)
    sent_rows, sent_grads = dispatch(routing, slot_gate, activations, out_grad)
    width_now = sent_rows.shape[2]
    gate_w = gate_proj[0]
    up_w = up_proj[0]
    down_w = down_proj[0]
    received = lax.all_to_all(
        jnp.repeat(sent_rows, 2, axis=0), "exp", split_axis=0, concat_axis=0, tiled=True
    )
    got_grads = lax.all_to_all(
        jnp.repeat(sent_grads, 2, axis=0), "exp", split_axis=0, concat_axis=0, tiled=True
    )
    rows_now = received.reshape(-1, width_now)
    grads_now = got_grads.reshape(-1, width_now)
    state = forward_part(rows_now, gate_w, up_w)
    partial_value, d_gate, d_up = backward_part(state, grads_now, gate_w, up_w, down_w)
    grads_out = weight_grads(rows_now, grads_now, state[4], d_gate, d_up)
    returned = lax.all_to_all(
        partial_value.reshape(devices, slot_count, model_width),
        "exp",
        split_axis=0,
        concat_axis=0,
        tiled=True,
    )
    summed = jnp.sum(
        returned.reshape(experts, 2, slot_count, model_width).astype(jnp.float32), axis=1
    )
    combined = jnp.einsum("ect,ecd->td", routing, summed, precision=lax.Precision.HIGHEST)
    in_grad = lax.psum(combined.astype(jnp.bfloat16), "tp")
    return (in_grad, grads_out[0], grads_out[1], grads_out[2])


def solution(mesh):
    return jax.shard_map(
        per_device,
        mesh=mesh,
        in_specs=(
            P("exp", None),
            P("exp", None),
            P("exp", None),
            P("exp", None),
            P("exp", "tp", None),
            P("exp", "tp", None),
            P("exp", "tp", None),
        ),
        out_specs=(
            P("exp", None),
            P("exp", "tp", None),
            P("exp", "tp", None),
            P("exp", "tp", None),
        ),
        check_vma=False,
    )
```

profile of v0, /device:TPU:2, one launch (start us, length us, event | category | flops | bytes accessed | tf_op | source)
XLA Modules:
  0.0 429.9 jit_solution(4126296814076332917)
XLA Ops:
  7.2 0.0 copy-start
  7.2 0.9 copy.23
  8.1 0.1 eq.45
  8.2 0.1 eq.49
  8.4 0.6 reduce-window.6
  9.0 0.2 slice_reduce_fusion
  9.2 0.1 fusion.22
  9.3 0.9 broadcast_multiply_fusion
  10.1 2.3 copy.26
  12.5 1.2 bitcast_reduce_fusion
  13.7 1.6 copy.30
  15.3 2.3 convolution_convert_fusion
  17.6 3.9 broadcast_in_dim.21
  21.5 7.8 %all-to-all-start.1 = ((bf16[32,32,3584]{2,1,0:T(8,128)(2,1)}), bf16[32,32,3584]{2,1,0:T(8,128)(2,1)}, u32[]{:S(2)}, u32[]{:S(2)}) async-start(bf16[32,32,3584]{2,1,0:T(8,128)(2,1)} %bitcast.95), calls=%async_computation.1 | async-start | bytes 14680064 | tf_op jit(solution)/shard_map/all_to_all | solution.py:84
  29.3 0.0 copy-done.7
  29.3 0.0 copy-done.8
  29.3 0.5 fusion.17
  29.8 0.0 copy-done.3
  29.9 3.0 multiply_convert_fusion
  32.8 83.8 %all-to-all-done.1 = bf16[32,32,3584]{2,1,0:T(8,128)(2,1)} async-done(((bf16[32,32,3584]{2,1,0:T(8,128)(2,1)}), bf16[32,32,3584]{2,1,0:T(8,128)(2,1)}, u32[]{:S(2)}, u32[]{:S(2)}) %all-to-all-start.1) | async-done | bytes 7340064 | tf_op jit(solution)/shard_map/all_to_all | solution.py:84
  116.6 5.8 %broadcast_in_dim.20 = bf16[16,2,32,3584]{3,2,1,0:T(8,128)(2,1)} broadcast(bf16[16,32,3584]{2,1,0:T(8,128)(2,1)} %multiply_convert_fusion), dimensions={0,2,3} | broadcast | bytes 11010048 | tf_op jit(solution)/shard_map/broadcast_in_dim | solution.py:88
  122.5 9.8 %all-to-all-start = ((bf16[32,32,3584]{2,1,0:T(8,128)(2,1)}), bf16[32,32,3584]{2,1,0:T(8,128)(2,1)}, u32[]{:S(2)}, u32[]{:S(2)}) async-start(bf16[32,32,3584]{2,1,0:T(8,128)(2,1)} %bitcast.97), calls=%async_computation | async-start | bytes 14680064 | tf_op jit(solution)/shard_map/all_to_all | solution.py:87
  132.3 0.0 copy-start.2
  132.3 0.0 copy-done
  132.3 6.6 %fusion.6 = f32[1024,192]{0,1:T(8,128)} fusion(bf16[1024,3584]{1,0:T(8,128)(2,1)} %bitcast.13, bf16[1,192,3584]{2,1,0:T(8,128)(2,1)S(1)} %copy-done), kind=kOutput, calls=%fused_computation.15 | convolution fusion | flops 1409286144 | bytes 9502720 | tf_op jit(solution)/shard_map/sd,ud->su/dot_general | solution.py:37
  138.9 0.0 copy-done.2
  138.9 6.5 %fusion.9 = f32[1024,192]{0,1:T(8,128)} fusion(bf16[1024,3584]{1,0:T(8,128)(2,1)} %bitcast.13, bf16[1,192,3584]{2,1,0:T(8,128)(2,1)S(1)} %copy-done.2), kind=kOutput, calls=%fused_computation.18 | convolution fusion | flops 1409286144 | bytes 9502720 | tf_op jit(solution)/shard_map/sd,ud->su/dot_general | solution.py:38
  145.4 74.3 %all-to-all-done = bf16[32,32,3584]{2,1,0:T(8,128)(2,1)} async-done(((bf16[32,32,3584]{2,1,0:T(8,128)(2,1)}), bf16[32,32,3584]{2,1,0:T(8,128)(2,1)}, u32[]{:S(2)}, u32[]{:S(2)}) %all-to-all-start) | async-done | bytes 7340064 | tf_op jit(solution)/shard_map/all_to_all | solution.py:87
  219.7 7.2 %multiply_convert_fusion.2 = (bf16[1024,192]{0,1:T(8,128)(2,1)}, bf16[1024,192]{0,1:T(8,128)(2,1)S(1)}) fusion(f32[1024,192]{0,1:T(8,128)} %fusion.6, f32[1024,192]{0,1:T(8,128)} %fusion.9, bf16[1024,3584]{1,0:T(8,128)(2,1)} %bitcast.9, bf16[1,192,3584]{2,1,0:T(8,128)(2,1)} %param.13), kind=kOutput, calls=%fused_computation.25 | convolution fusion | flops 1411842048 | bytes 11075584 | tf_op jit(solution)/shard_map/sd,ud->su/dot_general | solution.py:47
  226.8 2.1 fusion.4
  229.0 0.0 copy-done.4
  229.0 6.1 %add_convert_fusion = bf16[1024,3584]{1,0:T(8,128)(2,1)} fusion(f32[1024,3584]{1,0:T(8,128)S(1)} %fusion.4, bf16[1024,192]{0,1:T(8,128)(2,1)} %get-tuple-element.4, bf16[1,192,3584]{2,1,0:T(8,128)(2,1)S(1)} %copy-done.2), kind=kOutput, calls=%fused_computation.1 | convolution fusion | flops 1416626176 | bytes 23789568 | tf_op jit(solution)/shard_map/su,ud->sd/dot_general | solution.py:53
  235.1 9.9 %all-to-all-start.2 = ((bf16[32,32,3584]{2,1,0:T(8,128)(2,1)}), bf16[32,32,3584]{2,1,0:T(8,128)(2,1)}, u32[]{:S(2)}, u32[]{:S(2)}) async-start(bf16[32,32,3584]{2,1,0:T(8,128)(2,1)} %bitcast.96), calls=%async_computation.2 | async-start | bytes 14680064 | tf_op jit(solution)/shard_map/all_to_all | solution.py:95
  245.0 0.3 all-reduce.2.cloned.1.call-start
  245.3 5.8 %fusion.2 = bf16[1,192,3584]{2,1,0:T(8,128)(2,1)} fusion(bf16[1024,192]{0,1:T(8,128)(2,1)S(1)} %copy-done.6, bf16[1024,3584]{1,0:T(8,128)(2,1)} %bitcast.13), kind=kOutput, calls=%fused_computation.10 | convolution fusion | flops 1409974272 | bytes 9109504 | tf_op jit(solution)/shard_map/su,sd->ud/dot_general | solution.py:63
  251.1 81.4 %all-to-all-done.2 = bf16[32,32,3584]{2,1,0:T(8,128)(2,1)} async-done(((bf16[32,32,3584]{2,1,0:T(8,128)(2,1)}), bf16[32,32,3584]{2,1,0:T(8,128)(2,1)}, u32[]{:S(2)}, u32[]{:S(2)}) %all-to-all-start.2) | async-done | bytes 7340064 | tf_op jit(solution)/shard_map/all_to_all | solution.py:95
  332.5 5.4 %convert_reduce_fusion = f32[16,32,3584]{2,1,0:T(8,128)S(1)} fusion(bf16[32,32,3584]{2,1,0:T(8,128)(2,1)} %all-to-all-done.2), kind=kLoop, calls=%fused_computation | loop fusion | flops 5505024 | bytes 14680064 | tf_op jit(solution)/shard_map/reduce_sum | solution.py:102
  337.8 0.0 copy-start.5
  337.9 4.9 %fusion = bf16[128,3584]{1,0:T(8,128)(2,1)} fusion(f32[16,32,3584]{2,1,0:T(8,128)S(1)} %convert_reduce_fusion, f32[128,16,32]{0,2,1:T(8,128)S(1)} %copy.30), kind=kOutput, calls=%fused_computation.8 | convolution fusion | flops 2819031040 | bytes 8519680 | tf_op jit(solution)/shard_map/ect,ecd->td/dot_general | solution.py:105
  342.8 0.0 all-reduce.2.cloned.1.call-update
  342.8 0.0 copy-done.5
  342.8 0.0 copy-start.1
  342.8 5.9 %fusion.1 = bf16[1,192,3584]{2,1,0:T(8,128)(2,1)} fusion(bf16[1024,192]{0,1:T(8,128)(2,1)S(1)} %copy-done.5, bf16[1024,3584]{1,0:T(8,128)(2,1)} %bitcast.13), kind=kOutput, calls=%fused_computation.9 | convolution fusion | flops 1409974272 | bytes 9109504 | tf_op jit(solution)/shard_map/su,sd->ud/dot_general | solution.py:60
  348.7 0.0 copy-done.9
  348.7 5.8 %fusion.3 = bf16[1,192,3584]{2,1,0:T(8,128)(2,1)} fusion(bf16[1024,3584]{1,0:T(8,128)(2,1)} %bitcast.9, f32[1024,192]{0,1:T(8,128)S(1)} %copy-done.10, f32[1024,192]{0,1:T(8,128)S(1)} %copy-done.9), kind=kOutput, calls=%fused_computation.11 | convolution fusion | flops 1411153920 | bytes 10289152 | tf_op jit(solution)/shard_map/su,sd->ud/dot_general | solution.py:66
  354.5 66.4 %all-reduce.2.cloned.1.call-done = bf16[128,3584]{1,0:T(8,128)(2,1)} async-done(((bf16[128,3584]{1,0:T(8,128)(2,1)}), bf16[128,3584]{1,0:T(8,128)(2,1)}) %all-reduce.2.cloned.1.call-update) | async-done | bytes 917520 | tf_op jit(solution)/shard_map/psum | solution.py:106
  420.9 2.2 copy.34
  423.1 0.0 copy-done.1
  (15 shorter events, 0.1 us)
Async XLA Ops:
  7.2 125.1 %copy-start = (bf16[1,192,3584]{2,1,0:T(8,128)(2,1)S(1)}, bf16[1,192,3584]{2,1,0:T(8,128)(2,1)}, u32[]{:S(2)}) copy-start(bf16[1,192,3584]{2,1,0:T(8,128)(2,1)} %param.11) | copy-start | bytes 4128772
  21.5 7.8 %copy-start.7 = (s32[128,2]{0,1:T(2,128)S(1)}, s32[128,2]{0,1:T(2,128)}, u32[]{:S(2)}) copy-start(s32[128,2]{0,1:T(2,128)} %param.9) | copy-start | bytes 3076
  21.5 7.8 %copy-start.8 = (f32[128,2]{0,1:T(2,128)S(1)}, f32[128,2]{0,1:T(2,128)}, u32[]{:S(2)}) copy-start(f32[128,2]{0,1:T(2,128)} %param.10) | copy-start | bytes 3076
  21.5 8.4 %copy-start.3 = (bf16[128,3584]{1,0:T(8,128)(2,1)S(1)}, bf16[128,3584]{1,0:T(8,128)(2,1)}, u32[]{:S(2)}) copy-start(bf16[128,3584]{1,0:T(8,128)(2,1)} %param.8) | copy-start | bytes 2752516
  21.5 95.1 %all-to-all-start.1 = ((bf16[32,32,3584]{2,1,0:T(8,128)(2,1)}), bf16[32,32,3584]{2,1,0:T(8,128)(2,1)}, u32[]{:S(2)}, u32[]{:S(2)}) async-start(bf16[32,32,3584]{2,1,0:T(8,128)(2,1)} %bitcast.95), calls=%async_computation.1 | async-start | bytes 14680064 | tf_op jit(solution)/shard_map/all_to_all | solution.py:84
  122.5 97.2 %all-to-all-start = ((bf16[32,32,3584]{2,1,0:T(8,128)(2,1)}), bf16[32,32,3584]{2,1,0:T(8,128)(2,1)}, u32[]{:S(2)}, u32[]{:S(2)}) async-start(bf16[32,32,3584]{2,1,0:T(8,128)(2,1)} %bitcast.97), calls=%async_computation | async-start | bytes 14680064 | tf_op jit(solution)/shard_map/all_to_all | solution.py:87
  132.3 6.6 %copy-start.2 = (bf16[1,192,3584]{2,1,0:T(8,128)(2,1)S(1)}, bf16[1,192,3584]{2,1,0:T(8,128)(2,1)}, u32[]{:S(2)}) copy-start(bf16[1,192,3584]{2,1,0:T(8,128)(2,1)} %param.12) | copy-start | bytes 4128772
  226.8 2.1 copy-start.4
  235.1 10.2 %copy-start.6 = (bf16[1024,192]{0,1:T(8,128)(2,1)S(1)}, bf16[1024,192]{0,1:T(8,128)(2,1)}, u32[]{:S(2)}) copy-start(bf16[1024,192]{0,1:T(8,128)(2,1)} %get-tuple-element.4) | copy-start | bytes 1179652
  235.1 97.4 %all-to-all-start.2 = ((bf16[32,32,3584]{2,1,0:T(8,128)(2,1)}), bf16[32,32,3584]{2,1,0:T(8,128)(2,1)}, u32[]{:S(2)}, u32[]{:S(2)}) async-start(bf16[32,32,3584]{2,1,0:T(8,128)(2,1)} %bitcast.96), calls=%async_computation.2 | async-start | bytes 14680064 | tf_op jit(solution)/shard_map/all_to_all | solution.py:95
  245.0 175.9 %all-reduce.2.cloned.1.call-start = ((), (), s32[]{:S(2)}) async-start(), calls=%async_computation.3 | async-start | bytes 1835008 | tf_op jit(solution)/shard_map/psum | solution.py:106
  337.8 4.9 %copy-start.5 = (bf16[1024,192]{0,1:T(8,128)(2,1)S(1)}, bf16[1024,192]{0,1:T(8,128)(2,1)}, u32[]{:S(2)}) copy-start(bf16[1024,192]{0,1:T(8,128)(2,1)} %copy-done.4) | copy-start | bytes 1179652
  342.8 6.0 %copy-start.9 = (f32[1024,192]{0,1:T(8,128)S(1)}, f32[1024,192]{0,1:T(8,128)}, u32[]{:S(2)}) copy-start(f32[1024,192]{0,1:T(8,128)} %fusion.6) | copy-start | bytes 2359300
  342.8 6.0 %copy-start.10 = (f32[1024,192]{0,1:T(8,128)S(1)}, f32[1024,192]{0,1:T(8,128)}, u32[]{:S(2)}) copy-start(f32[1024,192]{0,1:T(8,128)} %fusion.9) | copy-start | bytes 2359300
  342.8 80.3 %copy-start.1 = (bf16[1,192,3584]{2,1,0:T(8,128)(2,1)S(1)}, bf16[1,192,3584]{2,1,0:T(8,128)(2,1)}, u32[]{:S(2)}) copy-start(bf16[1,192,3584]{2,1,0:T(8,128)(2,1)} %param.11) | copy-start | bytes 4128772
Sparse Core Ops, SparseCore 0:
  342.9 77.9 all-reduce.1
where the time goes:
time: 431 us; the launch traced here: 430 us
  waiting for transfers between devices  306 us (71%)
  matrix products  56.6 us (13%)
  starting transfers between devices  27.8 us (6%)
  local copies, waits for them, and re-layouts  17.2 us (4%)
  between operations  14.2 us (3%)
  other arithmetic  8.21 us (2%)
    all_to_all x1, waiting for transfers between devices, per_device(): lax.all_to_all(jnp.repeat(sent_rows, 2, axis=0), 'exp', split_axis=0, con...  83.8 us
    all_to_all x1, waiting for transfers between devices, per_device(): lax.all_to_all(partial_value.reshape(devices, slot_count, model_width), '...  81.4 us
    all_to_all x1, waiting for transfers between devices, per_device(): lax.all_to_all(jnp.repeat(sent_grads, 2, axis=0), 'exp', split_axis=0, co...  74.3 us
    psum x1, waiting for transfers between devices, per_device(): in_grad = lax.psum(combined.astype(jnp.bfloat16), 'tp')  66.4 us
    all_to_all x1, starting transfers between devices, per_device(): lax.all_to_all(partial_value.reshape(devices, slot_count, model_width), '...  9.92 us
    all_to_all x1, starting transfers between devices, per_device(): lax.all_to_all(jnp.repeat(sent_grads, 2, axis=0), 'exp', split_axis=0, co...  9.79 us
  transfers between devices with their start and end apart: 4, of which 4 were waited for; matrix products, arithmetic and copies ran while one was open for 8% of the time, Pallas kernels for 0%

commit v1 on v0

v1 whole, which is shorter than its diff:
```python
import functools

import jax
import jax.numpy as jnp
from jax import lax
from jax.experimental import pallas as pl
from jax.experimental.pallas import tpu as pltpu
from jax.sharding import PartitionSpec as P

F32 = jnp.float32
BF16 = jnp.bfloat16
VMEM = pltpu.VMEM
LIMIT = 48 * 1024 * 1024


def table(ids, experts):
    toks = ids.shape[1]
    expert = lax.broadcasted_iota(jnp.int32, (experts, toks), 0)
    first = ids[0:1, :] == expert
    second = ids[1:2, :] == expert
    named = jnp.where(first | second, 1.0, 0.0)
    earlier = lax.broadcasted_iota(jnp.int32, (toks, toks), 0)
    later = lax.broadcasted_iota(jnp.int32, (toks, toks), 1)
    before = jnp.where(earlier < later, 1.0, 0.0).astype(BF16)
    rank = jnp.dot(named.astype(BF16), before, preferred_element_type=F32)
    return first, second, jnp.where(named > 0.0, rank, -1.0)


def send_kernel(half, tp_ref, ids_ref, gate_ref, act_ref, grad_ref, far_ref, near_ref):
    experts = near_ref.shape[1] // 2
    toks = ids_ref.shape[1]
    first, second, rank = table(ids_ref[...], experts)
    gate = jnp.where(first, gate_ref[0:1, :], 0.0) + jnp.where(second, gate_ref[1:2, :], 0.0)
    acts = act_ref[...]
    grads = grad_ref[...]

    def select(slots, count):
        hit = (rank[:, None, :] == slots).reshape(experts * count, toks)
        weight = jnp.broadcast_to(gate[:, None, :], (experts, count, toks)).reshape(
            experts * count, toks
        )
        scale = jnp.sum(jnp.where(hit, weight, 0.0), axis=1, keepdims=True)
        mask = jnp.where(hit, 1.0, 0.0).astype(BF16)
        rows = jnp.dot(mask, acts, preferred_element_type=F32).astype(BF16)
        picked = jnp.dot(mask, grads, preferred_element_type=F32)
        return rows, (picked * scale).astype(BF16)

    slots = lax.broadcasted_iota(jnp.int32, (experts, half, toks), 1).astype(F32)
    rows, weighted = select(slots, half)
    far_ref[:, 0] = rows.reshape(far_ref.shape[0], half // 2, -1)
    far_ref[:, 1] = weighted.reshape(far_ref.shape[0], half // 2, -1)
    inner = lax.broadcasted_iota(jnp.int32, (experts, 8, toks), 1)
    slots = jnp.where(inner < 2, half + 2 * tp_ref[0] + inner, -2).astype(F32)
    rows, weighted = select(slots, 8)
    near_ref[0] = rows.reshape(experts, 8, -1)[:, :2].reshape(2 * experts, -1)
    near_ref[1] = weighted.reshape(experts, 8, -1)[:, :2].reshape(2 * experts, -1)


def make_send(tp_at, ids_t, gate_t, acts, grads, experts, half):
    toks, width = acts.shape
    tile = width // 7 if width % (7 * 128) == 0 else width
    return pl.pallas_call(
        functools.partial(send_kernel, half),
        grid=(width // tile,),
        in_specs=[
            pl.BlockSpec(memory_space=pltpu.SMEM),
            pl.BlockSpec((2, toks), lambda i: (0, 0)),
            pl.BlockSpec((2, toks), lambda i: (0, 0)),
            pl.BlockSpec((toks, tile), lambda i: (0, i)),
            pl.BlockSpec((toks, tile), lambda i: (0, i)),
        ],
        out_specs=[
            pl.BlockSpec((2 * experts, 2, half // 2, tile), lambda i: (0, 0, 0, i)),
            pl.BlockSpec((2, 2 * experts, tile), lambda i: (0, 0, i)),
        ],
        out_shape=[
            jax.ShapeDtypeStruct((2 * experts, 2, half // 2, width), BF16),
            jax.ShapeDtypeStruct((2, 2 * experts, width), BF16),
        ],
        compiler_params=pltpu.CompilerParams(vmem_limit_bytes=LIMIT),
    )(tp_at, ids_t, gate_t, acts, grads)


def expert_kernel(src_ref, pair_ref, down_ref, part_ref, side_ref, pre_acc, back_acc, dgu_ref):
    outer, _, inner, width = src_ref.shape
    rows = outer * inner
    units = down_ref.shape[0]
    quarter = part_ref.shape[2]
    contract = (((1,), (1,)), ((), ()))
    pre = jnp.zeros((rows, 2 * units), F32)
    back = jnp.zeros((rows, units), F32)
    pre_acc[...] = pre
    back_acc[...] = back
    step = quarter

    @pl.loop(0, width // step)
    def _(i):
        at = pl.ds(pl.multiple_of(i * step, step), step)
        x = src_ref[:, 0, :, at].reshape(rows, step)
        g = src_ref[:, 1, :, at].reshape(rows, step)
        pre_acc[...] += lax.dot_general(x, pair_ref[:, at], contract, preferred_element_type=F32)
        back_acc[...] += lax.dot_general(g, down_ref[:, at], contract, preferred_element_type=F32)

    pre_gate = pre_acc[:, :units]
    pre_up = pre_acc[:, units:]
    back = back_acc[...]
    sig = jax.nn.sigmoid(pre_gate)
    silu = pre_gate * sig
    hidden = (silu * pre_up).astype(BF16)
    d_gate = (back * pre_up * sig * (1.0 + pre_gate * (1.0 - sig))).astype(BF16)
    d_up = (back * silu).astype(BF16)
    dgu_ref[:, :units] = d_gate
    dgu_ref[:, units:] = d_up
    side_ref[:units, :] = d_gate.T
    side_ref[units : 2 * units, :] = d_up.T
    side_ref[2 * units :, :] = hidden.T

    @pl.loop(0, part_ref.shape[0])
    def _(q):
        at = pl.ds(pl.multiple_of(q * quarter, quarter), quarter)
        part_ref[q] = jnp.dot(
            dgu_ref[...], pair_ref[:, at], preferred_element_type=F32
        ).astype(BF16)


def expert_part(src, pair_w, down_w, quarters):
    outer, _, inner, width = src.shape
    rows = outer * inner
    units = down_w.shape[0]
    return pl.pallas_call(
        expert_kernel,
        in_specs=[pl.BlockSpec(memory_space=VMEM)] * 3,
        out_specs=[pl.BlockSpec(memory_space=VMEM)] * 2,
        out_shape=[
            jax.ShapeDtypeStruct((quarters, rows, width // quarters), BF16),
            jax.ShapeDtypeStruct((3 * units, rows), BF16),
        ],
        scratch_shapes=[
            VMEM((rows, 2 * units), F32),
            VMEM((rows, units), F32),
            VMEM((rows, 2 * units), BF16),
        ],
        compiler_params=pltpu.CompilerParams(vmem_limit_bytes=LIMIT),
        cost_estimate=pl.CostEstimate(
            flops=10 * rows * width * units,
            bytes_accessed=2 * (3 * rows * width + 3 * units * width),
            transcendentals=rows * units,
        ),
    )(src, pair_w, down_w)


def weight_kernel(count, *refs):
    sources, sides = refs[:count], refs[count : 2 * count]
    gate_ref, up_ref, down_ref = refs[2 * count :]
    units = gate_ref.shape[0]
    pair, down = None, None
    for src_ref, side_ref in zip(sources, sides):
        outer, _, inner, tile = src_ref.shape
        x = src_ref[:, 0].reshape(outer * inner, tile)
        g = src_ref[:, 1].reshape(outer * inner, tile)
        one = jnp.dot(side_ref[: 2 * units, :], x, preferred_element_type=F32)
        two = jnp.dot(side_ref[2 * units :, :], g, preferred_element_type=F32)
        pair = one if pair is None else pair + one
        down = two if down is None else down + two
    gate_ref[...] = pair[:units].astype(BF16)
    up_ref[...] = pair[units:].astype(BF16)
    down_ref[...] = down.astype(BF16)


def weight_grads(sources, sides):
    width = sources[0].shape[3]
    units = sides[0].shape[0] // 3
    rows = sum(side.shape[1] for side in sides)
    tile = 256 if width % 256 == 0 else width
    return pl.pallas_call(
        functools.partial(weight_kernel, len(sources)),
        grid=(width // tile,),
        in_specs=[
            pl.BlockSpec(src.shape[:3] + (tile,), lambda i: (0, 0, 0, i)) for src in sources
        ]
        + [pl.BlockSpec(side.shape, lambda i: (0, 0)) for side in sides],
        out_specs=[pl.BlockSpec((units, tile), lambda i: (0, i))] * 3,
        out_shape=[jax.ShapeDtypeStruct((units, width), BF16)] * 3,
        compiler_params=pltpu.CompilerParams(vmem_limit_bytes=LIMIT),
        cost_estimate=pl.CostEstimate(
            flops=6 * rows * width * units,
            bytes_accessed=2 * (2 * rows * width + 3 * units * width),
            transcendentals=0,
        ),
    )(*sources, *sides)


def combine_kernel(half, tp_ref, ids_ref, back_ref, out_ref):
    experts = back_ref.shape[0] // 2
    per_core = back_ref.shape[1]
    toks = ids_ref.shape[1]
    _, _, rank = table(ids_ref[...], experts)
    shape = (experts, 2 * per_core, toks)
    row = lax.broadcasted_iota(jnp.int32, shape, 1)
    core, inner = row // per_core, row % per_core
    slots = jnp.where(tp_ref[0] % 2 == 0, row, half + 2 * inner + core).astype(F32)
    hit = jnp.where(rank[:, None, :] == slots, 1.0, 0.0).astype(BF16)
    hit = hit.reshape(2 * experts * per_core, toks)
    out_ref[...] = lax.dot_general(
        hit,
        back_ref[...].reshape(2 * experts * per_core, -1),
        (((0,), (0,)), ((), ())),
        preferred_element_type=F32,
    ).astype(BF16)


def combine(tp_at, ids_t, returned, half):
    toks = ids_t.shape[1]
    return pl.pallas_call(
        functools.partial(combine_kernel, half),
        in_specs=[
            pl.BlockSpec(memory_space=pltpu.SMEM),
            pl.BlockSpec(memory_space=VMEM),
            pl.BlockSpec(memory_space=VMEM),
        ],
        out_specs=pl.BlockSpec(memory_space=VMEM),
        out_shape=jax.ShapeDtypeStruct((toks, returned.shape[2]), BF16),
        compiler_params=pltpu.CompilerParams(vmem_limit_bytes=LIMIT),
    )(tp_at, ids_t, returned)


def per_device(activations, out_grad, expert_ids, gate_values, gate_proj, up_proj, down_proj):
    devices = lax.axis_size("exp")
    planes = lax.axis_size("tp")
    experts = devices // 2
    toks, width = activations.shape
    slots = 8 * toks // devices
    half = slots // 2
    quarters = planes // 2
    tp_at = lax.axis_index("tp").astype(jnp.int32)[None]
    ids_t = expert_ids.T
    gate_t = gate_values.T
    swap = [(i, i ^ 1) for i in range(devices)]

    def trade(v):
        return lax.ppermute(v, "exp", swap)

    def spread(v):
        return lax.all_to_all(v, "exp", split_axis=0, concat_axis=0, tiled=True)

    far, near = make_send(tp_at, ids_t, gate_t, activations, out_grad, experts, half)
    near = spread(jnp.transpose(near, (1, 0, 2)))
    near, far = lax.optimization_barrier((near, far))
    near = jnp.transpose(near, (1, 0, 2))
    near = lax.all_gather(near, "tp", axis=0, tiled=False)
    far = spread(far.reshape(devices, half, width)).reshape(far.shape)
    pair_w = jnp.concatenate([gate_proj[0], up_proj[0]], axis=0)
    down_w = down_proj[0]
    far_other = trade(far)
    far_part, far_side = expert_part(far, pair_w, down_w, quarters)
    far_other_part, far_other_side = expert_part(far_other, pair_w, down_w, quarters)
    far_sent = trade(far_other_part)
    near_other = trade(near)
    near_other_part, near_other_side = expert_part(near_other, pair_w, down_w, quarters)
    near_sent = trade(near_other_part)
    near_part, near_side = expert_part(near, pair_w, down_w, quarters)
    far_sum = (far_part.astype(F32) + far_sent.astype(F32)).astype(BF16)
    near_sum = (near_part.astype(F32) + near_sent.astype(F32)).astype(BF16)
    both = jnp.stack([far_sum, near_sum], axis=1)
    both = both.reshape((planes,) + far_sum.shape[1:])
    mine = lax.psum_scatter(both, "tp", scatter_dimension=0, tiled=False)
    straight = mine.reshape(devices, half // 2, -1)
    turned = jnp.transpose(mine.reshape(half // 2, devices, -1), (1, 0, 2))
    returned = spread(jnp.where(tp_at[0] % 2 == 0, straight, turned))
    piece = combine(tp_at, ids_t, returned, half)
    gathered = lax.all_gather(piece, "tp", axis=0, tiled=False)
    gathered = gathered.reshape(quarters, 2, toks, width // quarters).astype(F32)
    in_grad = jnp.transpose((gathered[:, 0] + gathered[:, 1]).astype(BF16), (1, 0, 2))
    in_grad = in_grad.reshape(toks, width)
    gate_g, up_g, down_g = weight_grads(
        [far, far_other, near, near_other],
        [far_side, far_other_side, near_side, near_other_side],
    )
    return (in_grad, gate_g[None], up_g[None], down_g[None])


def solution(mesh):
    return jax.shard_map(
        per_device,
        mesh=mesh,
        in_specs=(
            P("exp", None),
            P("exp", None),
            P("exp", None),
            P("exp", None),
            P("exp", "tp", None),
            P("exp", "tp", None),
            P("exp", "tp", None),
        ),
        out_specs=(
            P("exp", None),
            P("exp", "tp", None),
            P("exp", "tp", None),
            P("exp", "tp", None),
        ),
        check_vma=False,
    )
```

time: 431 us -> 250 us (0.58)
  waiting for transfers between devices: 306 us -> 84.1 us
  blocking collectives: 0 us -> 84.7 us
  matrix products: 56.6 us -> 0 us
  Pallas kernels: 0 us -> 47.4 us
  starting transfers between devices: 27.8 us -> 1.32 us
  local copies, waits for them, and re-layouts: 17.2 us -> 12 us
    all_to_all x3 -> x0, waiting for transfers between devices: 239 us -> none  [the longest x1 83.8 us: per_device(): lax.all_to_all(jnp.repeat(sent_rows, 2, axis=0), 'exp', split_axis=0, con...]
    all_to_all x0 -> x3, blocking collectives: none -> 84.7 us  [spread(): return lax.all_to_all(v, 'exp', split_axis=0, concat_axis=0, tiled=True)]
    psum x1 -> x0, waiting for transfers between devices: 66.4 us -> none  [per_device(): in_grad = lax.psum(combined.astype(jnp.bfloat16), 'tp')]
    dot_general x12 -> x0, matrix products: 56.6 us -> none  [the longest x1 7.16 us: backward_part(): jnp.einsum('sd,ud->su', grads_in, down_w, preferred_element_type=jnp.floa...]
    reduce_scatter x0 -> x1, waiting for transfers between devices: none -> 52.4 us  [per_device(): mine = lax.psum_scatter(both, 'tp', scatter_dimension=0, tiled=False)]
    pallas_call x0 -> x7, Pallas kernels: none -> 47.4 us  [the longest x4 28.5 us: expert_part(): pl.pallas_call(expert_kernel, in_specs=[pl.BlockSpec(memory_space=VMEM)]...]
    all_to_all x3 -> x0, starting transfers between devices: 27.5 us -> none  [the longest x1 9.92 us: per_device(): lax.all_to_all(partial_value.reshape(devices, slot_count, model_width), '...]
    all_gather x0 -> x2, waiting for transfers between devices: none -> 23.4 us  [the longest x1 23.4 us: per_device(): gathered = lax.all_gather(piece, 'tp', axis=0, tiled=False)]
  transfers between devices with their start and end apart: 4 -> 7, of which waited for: 4 -> 3; matrix products, arithmetic and copies ran while one was open for 8% -> 1% of each run, Pallas kernels for 0% -> 17%
where the time goes in v1:
time: 250 us
  blocking collectives  84.7 us (34%)
  waiting for transfers between devices  84.1 us (34%)
  Pallas kernels  47.4 us (19%)
  between operations  13.9 us (6%)
  local copies, waits for them, and re-layouts  12 us (5%)
  other arithmetic  6.18 us (2%)
    all_to_all x3, blocking collectives, spread(): return lax.all_to_all(v, 'exp', split_axis=0, concat_axis=0, tiled=True)  84.7 us
    reduce_scatter x1, waiting for transfers between devices, per_device(): mine = lax.psum_scatter(both, 'tp', scatter_dimension=0, tiled=False)  52.4 us
    pallas_call x4, Pallas kernels, expert_part(): pl.pallas_call(expert_kernel, in_specs=[pl.BlockSpec(memory_space=VMEM)]...  28.5 us
    all_gather x1, waiting for transfers between devices, per_device(): gathered = lax.all_gather(piece, 'tp', axis=0, tiled=False)  23.4 us
    pallas_call x1, Pallas kernels, weight_grads(): pl.pallas_call(functools.partial(weight_kernel, len(sources)), grid=(widt...  14 us
    ppermute x4, waiting for transfers between devices, trade(): return lax.ppermute(v, 'exp', swap)  8.27 us
    unnamed x20, local copies, waits for them, and re-layouts  7.56 us
  transfers between devices with their start and end apart: 7, of which 3 were waited for; matrix products, arithmetic and copies ran while one was open for 1% of the time, Pallas kernels for 17%

profile of v1, /device:TPU:2, one launch (start us, length us, event | category | flops | bytes accessed | tf_op | source)
XLA Modules:
  0.0 249.6 jit_solution(17476971240142637269)
XLA Ops:
  7.2 0.0 all-gather.5.cloned.1.call-start
  7.2 0.0 copy-start.2
  7.2 1.2 copy-done.2
  8.4 1.2 copy-done.3
  9.6 0.7 copy-done.4
  10.3 0.7 copy-done.6
  10.9 3.9 %shard_map.102 = (bf16[32,2,8,3584]{3,2,1,0:T(8,128)(2,1)S(1)}, bf16[2,32,3584]{2,1,0:T(8,128)(2,1)S(1)}) custom-call(s32[1]{0:T(128)} %bitcast.tp_ref, s32[2,128]{1,0:T(2,128)S(1)} %bitcast.38, f32[2,128]{1,0:T(2,128)S(1)} %bitcast.40, bf16[128,3584]{1,0:T(8,128)(2,1)S(1)} %copy-done.2, bf16[128,3584]{1,0:T(8,128)(2,1)S(1)} %copy-done.3), custom_call_target="tpu_custom_call" | custom-call | tf_op jit(solution)/shard_map/pallas_call | solution.py:62
  14.8 1.9 copy-done.1
  16.7 0.5 copy.15
  17.2 17.2 %all_to_all.15 = bf16[32,2,3584]{2,1,0:T(2,128)(2,1)S(1)} all-to-all(bf16[32,2,3584]{2,1,0:T(2,128)(2,1)S(1)} %copy.15), channel_id=1, replica_groups=mesh['exp'=32,'tp'=8] {'exp'}, dimensions={0} | all-to-all | bytes 917504 | tf_op jit(solution)/shard_map/all_to_all | solution.py:244
  34.4 0.8 copy.16
  35.2 0.0 all-gather.5.cloned.1.call-update
  35.3 0.0 reduce-scatter.2.cloned.1.call-start
  35.3 0.0 copy-start.8
  35.3 0.0 copy-start.9
  35.3 50.5 %all_to_all.16 = bf16[32,16,3584]{2,1,0:T(8,128)(2,1)} all-to-all(bf16[32,16,3584]{2,1,0:T(8,128)(2,1)} %bitcast.36), channel_id=1, replica_groups=mesh['exp'=32,'tp'=8] {'exp'}, dimensions={0} | all-to-all | bytes 7340032 | tf_op jit(solution)/shard_map/all_to_all | solution.py:244
  85.8 0.4 collective-permute-start
  86.2 0.1 collective-permute-start.2
  86.4 1.7 pad_maximum_fusion.1.pair_ref
  88.0 8.3 %collective-permute-done.src_ref.refs_1_ = bf16[32,2,8,3584]{3,2,1,0:T(8,128)(2,1)} collective-permute-done((bf16[32,2,8,3584]{3,2,1,0:T(8,128)(2,1)}, bf16[32,2,8,3584]{3,2,1,0:T(8,128)(2,1)}, u32[]{:S(2)}, u32[]{:S(2)}) %collective-permute-start) | collective-permute-done | bytes 3670048 | tf_op jit(solution)/shard_map/ppermute | solution.py:241
  96.3 0.0 copy-done
  96.3 7.1 %shard_map.104 = (bf16[4,256,896]{2,1,0:T(8,128)(2,1)S(1)}, bf16[576,256]{1,0:T(8,128)(2,1)S(1)}) custom-call(bf16[32,2,8,3584]{3,2,1,0:T(8,128)(2,1)} %collective-permute-done.src_ref.refs_1_, bf16[384,3584]{1,0:T(8,128)(2,1)} %pad_maximum_fusion.1.pair_ref, bf16[192,3584]{1,0:T(8,128)(2,1)S(1)} %bitcast.32), custom_call_target="tpu_custom_call" | custom-call | flops 1761607680 | bytes 9633792 | tf_op jit(solution)/shard_map/pallas_call | solution.py:130
  103.4 0.5 collective-permute-start.1
  103.9 0.0 collective-permute-done.2.src_ref.refs_3_
  103.9 1.9 copy-done.7
  105.8 7.1 %shard_map.106 = (bf16[4,256,896]{2,1,0:T(8,128)(2,1)S(1)}, bf16[576,256]{1,0:T(8,128)(2,1)S(1)}) custom-call(bf16[8,2,32,3584]{3,2,1,0:T(8,128)(2,1)} %copy-done.7, bf16[384,3584]{1,0:T(8,128)(2,1)} %pad_maximum_fusion.1.pair_ref, bf16[192,3584]{1,0:T(8,128)(2,1)S(1)} %bitcast.33), custom_call_target="tpu_custom_call" | custom-call | flops 1761607680 | bytes 9633792 | tf_op jit(solution)/shard_map/pallas_call | solution.py:130
  112.9 0.2 collective-permute-start.3
  113.2 7.1 %shard_map.103 = (bf16[4,256,896]{2,1,0:T(8,128)(2,1)S(1)}, bf16[576,256]{1,0:T(8,128)(2,1)S(1)}) custom-call(bf16[32,2,8,3584]{3,2,1,0:T(8,128)(2,1)} %bitcast.5.src_ref.refs_0_, bf16[384,3584]{1,0:T(8,128)(2,1)} %pad_maximum_fusion.1.pair_ref, bf16[192,3584]{1,0:T(8,128)(2,1)S(1)} %bitcast.34), custom_call_target="tpu_custom_call" | custom-call | flops 1761607680 | bytes 9633792 | tf_op jit(solution)/shard_map/pallas_call | solution.py:130
  120.3 7.1 %shard_map.105 = (bf16[4,256,896]{2,1,0:T(8,128)(2,1)S(1)}, bf16[576,256]{1,0:T(8,128)(2,1)S(1)}) custom-call(bf16[8,2,32,3584]{3,2,1,0:T(8,128)(2,1)} %bitcast.43, bf16[384,3584]{1,0:T(8,128)(2,1)} %pad_maximum_fusion.1.pair_ref, bf16[192,3584]{1,0:T(8,128)(2,1)S(1)} %bitcast.35), custom_call_target="tpu_custom_call" | custom-call | flops 1761607680 | bytes 9633792 | tf_op jit(solution)/shard_map/pallas_call | solution.py:130
  127.4 0.0 collective-permute-done.1
  127.4 0.4 fusion
  127.9 0.0 collective-permute-done.3
  127.9 0.4 fusion.1
  128.3 0.4 pad_maximum_fusion
  128.7 2.1 copy.17
  130.9 0.0 reduce-scatter.2.cloned.1.call-update
  130.9 0.0 copy-start.5
  130.9 0.0 all-gather.7.cloned.1.call-start
  131.0 52.4 %reduce-scatter.2.cloned.1.call-done = bf16[1,256,896]{2,1,0:T(8,128)(2,1)} async-done(((bf16[8,256,896]{2,1,0:T(8,128)(2,1)}), bf16[1,256,896]{2,1,0:T(8,128)(2,1)}) %reduce-scatter.2.cloned.1.call-update) | async-done | bytes 458768 | tf_op jit(solution)/shard_map/reduce_scatter | solution.py:266
  183.4 1.3 bitcast_select_fusion
  184.7 17.0 %all_to_all.17.back_ref = bf16[32,8,896]{2,1,0:T(8,128)(2,1)S(1)} all-to-all(bf16[32,8,896]{2,1,0:T(8,128)(2,1)S(1)} %bitcast_select_fusion), channel_id=1, replica_groups=mesh['exp'=32,'tp'=8] {'exp'}, dimensions={0} | all-to-all | bytes 917504 | tf_op jit(solution)/shard_map/all_to_all | solution.py:244
  201.7 1.1 shard_map.107
  202.8 0.0 all-gather.7.cloned.1.call-update
  202.8 14.0 %shard_map.108 = (bf16[192,3584]{1,0:T(8,128)(2,1)}, bf16[192,3584]{1,0:T(8,128)(2,1)}, bf16[192,3584]{1,0:T(8,128)(2,1)}) custom-call(bf16[32,2,8,3584]{3,2,1,0:T(8,128)(2,1)} %bitcast.5.src_ref.refs_0_, bf16[32,2,8,3584]{3,2,1,0:T(8,128)(2,1)} %collective-permute-done.src_ref.refs_1_, bf16[8,2,32,3584]{3,2,1,0:T(8,128)(2,1)} %bitcast.44, ...), custom_call_target="tpu_custom_call" | custom-call | flops 4227858432 | bytes 18808832 | tf_op jit(solution)/shard_map/pallas_call | solution.py:175
  216.8 23.4 %all-gather.7.cloned.1.call-done = bf16[1024,896]{1,0:T(8,128)(2,1)} async-done(((bf16[128,896]{1,0:T(8,128)(2,1)}), bf16[1024,896]{1,0:T(8,128)(2,1)}) %all-gather.7.cloned.1.call-update) | async-done | bytes 1835024 | tf_op jit(solution)/shard_map/all_gather | solution.py:271
  240.1 1.8 convert.1
  241.9 0.2 fusion.3
  242.1 1.0 copy.20
  (10 shorter events, 0.0 us)
Async XLA Ops:
  7.2 79.0 %all-gather.5.cloned.1.call-start = ((), (), s32[]{:S(2)}) async-start(), calls=%async_computation.5 | async-start | bytes 4128768 | tf_op jit(solution)/shard_map/all_gather | solution.py:250
  7.2 1.2 copy-start.2
  8.4 1.2 copy-start.3
  9.6 0.7 copy-start.4
  10.3 0.7 copy-start.6
  14.8 1.9 copy-start.1
  35.3 148.1 %reduce-scatter.2.cloned.1.call-start = ((), (), s32[]{:S(2)}) async-start(), calls=%async_computation.4 | async-start | bytes 4128768 | tf_op jit(solution)/shard_map/reduce_scatter | solution.py:266
  35.3 51.0 %copy-start.8 = (bf16[1,192,3584]{2,1,0:T(8,128)(2,1)S(1)}, bf16[1,192,3584]{2,1,0:T(8,128)(2,1)}, u32[]{:S(2)}) copy-start(bf16[1,192,3584]{2,1,0:T(8,128)(2,1)} %param.12) | copy-start | bytes 4128772
  35.3 51.0 %copy-start.9 = (bf16[1,192,3584]{2,1,0:T(8,128)(2,1)S(1)}, bf16[1,192,3584]{2,1,0:T(8,128)(2,1)}, u32[]{:S(2)}) copy-start(bf16[1,192,3584]{2,1,0:T(8,128)(2,1)} %param.11) | copy-start | bytes 4128772
  85.8 10.5 %collective-permute-start = (bf16[32,2,8,3584]{3,2,1,0:T(8,128)(2,1)}, bf16[32,2,8,3584]{3,2,1,0:T(8,128)(2,1)}, u32[]{:S(2)}, u32[]{:S(2)}) collective-permute-start(bf16[32,2,8,3584]{3,2,1,0:T(8,128)(2,1)} %bitcast.5.src_ref.refs_0_), channel_id=1, source_target_pairs={{0,8},{8,0},{16,24},{24,16},{32,40},{40,32},{48,56},{56,48},{64,72... | collective-permute-start | bytes 11010056 | tf_op jit(solution)/shard_map/ppermute | solution.py:241
  86.2 17.7 %collective-permute-start.2 = (bf16[8,2,32,3584]{3,2,1,0:T(8,128)(2,1)}, bf16[8,2,32,3584]{3,2,1,0:T(8,128)(2,1)S(1)}, u32[]{:S(2)}, u32[]{:S(2)}) collective-permute-start(bf16[8,2,32,3584]{3,2,1,0:T(8,128)(2,1)} %bitcast.42), channel_id=1, source_target_pairs={{0,8},{8,0},{16,24},{24,16},{32,40},{40,32},{48,56},{56,48},{64,72... | collective-permute-start | bytes 11010056 | tf_op jit(solution)/shard_map/ppermute | solution.py:241
  86.4 10.0 %copy-start = (bf16[1,192,3584]{2,1,0:T(8,128)(2,1)S(1)}, bf16[1,192,3584]{2,1,0:T(8,128)(2,1)}, u32[]{:S(2)}) copy-start(bf16[1,192,3584]{2,1,0:T(8,128)(2,1)} %param.13) | copy-start | bytes 4128772
  103.4 24.0 %collective-permute-start.1 = (bf16[4,256,896]{2,1,0:T(8,128)(2,1)S(1)}, bf16[4,256,896]{2,1,0:T(8,128)(2,1)S(1)}, u32[]{:S(2)}, u32[]{:S(2)}) collective-permute-start(bf16[4,256,896]{2,1,0:T(8,128)(2,1)S(1)} %get-tuple-element.23), channel_id=1, source_target_pairs={{0,8},{8,0},{16,24},{24,16},{32,40},{40,32},{48,56},{56,48},{64,72... | collective-permute-start | bytes 5505032 | tf_op jit(solution)/shard_map/ppermute | solution.py:241
  103.9 1.9 copy-start.7
  112.9 15.0 %collective-permute-start.3 = (bf16[4,256,896]{2,1,0:T(8,128)(2,1)S(1)}, bf16[4,256,896]{2,1,0:T(8,128)(2,1)S(1)}, u32[]{:S(2)}, u32[]{:S(2)}) collective-permute-start(bf16[4,256,896]{2,1,0:T(8,128)(2,1)S(1)} %get-tuple-element.26), channel_id=1, source_target_pairs={{0,8},{8,0},{16,24},{24,16},{32,40},{40,32},{48,56},{56,48},{64,72... | collective-permute-start | bytes 5505032 | tf_op jit(solution)/shard_map/ppermute | solution.py:241
  130.9 70.8 %copy-start.5 = (s32[128,2]{0,1:T(2,128)S(1)}, s32[128,2]{0,1:T(2,128)}, u32[]{:S(2)}) copy-start(s32[128,2]{0,1:T(2,128)} %param.9) | copy-start | bytes 3076
  130.9 109.2 %all-gather.7.cloned.1.call-start = ((), (), s32[]{:S(2)}) async-start(), calls=%async_computation.6 | async-start | bytes 2064384 | tf_op jit(solution)/shard_map/all_gather | solution.py:271
Sparse Core Ops, SparseCore 0:
  35.4 50.1 all-gather.4
  131.0 52.3 reduce-scatter.1
  202.9 37.1 all-gather.6

commit v2 on v1

v2 whole, which is shorter than its diff:
```python
import functools

import jax
import jax.numpy as jnp
from jax import lax
from jax.experimental import pallas as pl
from jax.experimental.pallas import tpu as pltpu
from jax.sharding import PartitionSpec as P

F32 = jnp.float32
BF16 = jnp.bfloat16
VMEM = pltpu.VMEM
LIMIT = 48 * 1024 * 1024


def padded(columns):
    return -(-columns // 128) * 128


def fill_pieces(out_ref, total, wide):
    for j in range(out_ref.shape[0]):
        out_ref[j, :, :wide] = total[:, j * wide : (j + 1) * wide]
        if out_ref.shape[2] > wide:
            out_ref[j, :, wide:] = jnp.zeros_like(out_ref[j, :, wide:])


def table(ids, experts):
    toks = ids.shape[1]
    expert = lax.broadcasted_iota(jnp.int32, (experts, toks), 0)
    first = ids[0:1, :] == expert
    second = ids[1:2, :] == expert
    named = jnp.where(first | second, 1.0, 0.0)
    earlier = lax.broadcasted_iota(jnp.int32, (toks, toks), 0)
    later = lax.broadcasted_iota(jnp.int32, (toks, toks), 1)
    before = jnp.where(earlier < later, 1.0, 0.0).astype(BF16)
    rank = jnp.dot(named.astype(BF16), before, preferred_element_type=F32)
    return first, second, jnp.where(named > 0.0, rank, -1.0)


def send_kernel(half, tp_ref, ids_ref, gate_ref, act_ref, grad_ref, far_ref, near_ref):
    experts = near_ref.shape[1] // 2
    toks = ids_ref.shape[1]
    first, second, rank = table(ids_ref[...], experts)
    gate = jnp.where(first, gate_ref[0:1, :], 0.0) + jnp.where(second, gate_ref[1:2, :], 0.0)
    acts = act_ref[...]
    grads = grad_ref[...]

    def select(slots, count):
        hit = (rank[:, None, :] == slots).reshape(experts * count, toks)
        weight = jnp.broadcast_to(gate[:, None, :], (experts, count, toks)).reshape(
            experts * count, toks
        )
        scale = jnp.sum(jnp.where(hit, weight, 0.0), axis=1, keepdims=True)
        mask = jnp.where(hit, 1.0, 0.0).astype(BF16)
        rows = jnp.dot(mask, acts, preferred_element_type=F32).astype(BF16)
        picked = jnp.dot(mask, grads, preferred_element_type=F32)
        return rows, (picked * scale).astype(BF16)

    slots = lax.broadcasted_iota(jnp.int32, (experts, half, toks), 1).astype(F32)
    rows, weighted = select(slots, half)
    far_ref[:, 0] = rows.reshape(far_ref.shape[0], half // 2, -1)
    far_ref[:, 1] = weighted.reshape(far_ref.shape[0], half // 2, -1)
    inner = lax.broadcasted_iota(jnp.int32, (experts, 8, toks), 1)
    slots = jnp.where(inner < 2, half + 2 * tp_ref[0] + inner, -2).astype(F32)
    rows, weighted = select(slots, 8)
    near_ref[0] = rows.reshape(experts, 8, -1)[:, :2].reshape(2 * experts, -1)
    near_ref[1] = weighted.reshape(experts, 8, -1)[:, :2].reshape(2 * experts, -1)


def make_send(tp_at, ids_t, gate_t, acts, grads, experts, half):
    toks, width = acts.shape
    tile = width // 7 if width % (7 * 128) == 0 else width
    return pl.pallas_call(
        functools.partial(send_kernel, half),
        grid=(width // tile,),
        in_specs=[
            pl.BlockSpec(memory_space=pltpu.SMEM),
            pl.BlockSpec((2, toks), lambda i: (0, 0)),
            pl.BlockSpec((2, toks), lambda i: (0, 0)),
            pl.BlockSpec((toks, tile), lambda i: (0, i)),
            pl.BlockSpec((toks, tile), lambda i: (0, i)),
        ],
        out_specs=[
            pl.BlockSpec((2 * experts, 2, half // 2, tile), lambda i: (0, 0, 0, i)),
            pl.BlockSpec((2, 2 * experts, tile), lambda i: (0, 0, i)),
        ],
        out_shape=[
            jax.ShapeDtypeStruct((2 * experts, 2, half // 2, width), BF16),
            jax.ShapeDtypeStruct((2, 2 * experts, width), BF16),
        ],
        compiler_params=pltpu.CompilerParams(vmem_limit_bytes=LIMIT),
    )(tp_at, ids_t, gate_t, acts, grads)


def expert_kernel(turn, src_ref, pair_ref, down_ref, part_ref, side_ref, pre_acc, back_acc, dgu_ref):
    outer, _, inner, width = src_ref.shape
    rows = outer * inner
    units = down_ref.shape[0]
    contract = (((1,), (1,)), ((), ()))
    phase, at = pl.program_id(0), pl.program_id(1)

    @pl.when(phase == 0)
    def _():
        x = src_ref[:, 0].reshape(rows, width)
        g = src_ref[:, 1].reshape(rows, width)
        pre = lax.dot_general(x, pair_ref[...], contract, preferred_element_type=F32)
        back = lax.dot_general(g, down_ref[...], contract, preferred_element_type=F32)

        @pl.when(at == 0)
        def _():
            pre_acc[...] = pre
            back_acc[...] = back

        @pl.when(at > 0)
        def _():
            pre_acc[...] += pre
            back_acc[...] += back

    @pl.when((phase == 0) & (at == pl.num_programs(1) - 1))
    def _():
        pre_gate = pre_acc[:, :units]
        pre_up = pre_acc[:, units:]
        back = back_acc[...]
        sig = jax.nn.sigmoid(pre_gate)
        silu = pre_gate * sig
        hidden = (silu * pre_up).astype(BF16)
        d_gate = (back * pre_up * sig * (1.0 + pre_gate * (1.0 - sig))).astype(BF16)
        d_up = (back * silu).astype(BF16)
        side_ref[:units, :] = d_gate.T
        side_ref[units : 2 * units, :] = d_up.T
        side_ref[2 * units :, :] = hidden.T
        dgu_ref[:, :units] = d_gate
        dgu_ref[:, units:] = d_up
        if turn:
            to = lax.broadcasted_iota(jnp.int32, (rows, rows), 0)
            of = lax.broadcasted_iota(jnp.int32, (rows, rows), 1)
            moved = jnp.where(of == (to % outer) * inner + to // outer, 1.0, 0.0).astype(BF16)
            dgu_ref[...] = jnp.dot(moved, dgu_ref[...], preferred_element_type=F32).astype(BF16)

    @pl.when(phase == 1)
    def _():
        part = jnp.dot(dgu_ref[...], pair_ref[...], preferred_element_type=F32).astype(BF16)
        fill_pieces(part_ref, part, part.shape[1] // part_ref.shape[0])


def expert_part(src, pair_w, down_w, pieces, turn):
    outer, _, inner, width = src.shape
    rows = outer * inner
    units = down_w.shape[0]
    steps = 2
    tile = width // steps
    each = max(1, pieces // steps)
    last = steps - 1
    if pieces > 1:
        wide = padded(width // pieces)
        part_spec = pl.BlockSpec((each, rows, wide), lambda p, i: (p * i, 0, 0))
    else:
        wide = width
        part_spec = pl.BlockSpec((1, rows, tile), lambda p, i: (0, 0, p * i))
    return pl.pallas_call(
        functools.partial(expert_kernel, turn),
        grid=(2, steps),
        in_specs=[
            pl.BlockSpec((outer, 2, inner, tile), lambda p, i: (0, 0, 0, jnp.where(p == 0, i, last))),
            pl.BlockSpec((2 * units, tile), lambda p, i: (0, i)),
            pl.BlockSpec((units, tile), lambda p, i: (0, jnp.where(p == 0, i, last))),
        ],
        out_specs=[part_spec, pl.BlockSpec((3 * units, rows), lambda p, i: (0, 0))],
        out_shape=[
            jax.ShapeDtypeStruct((pieces, rows, wide), BF16),
            jax.ShapeDtypeStruct((3 * units, rows), BF16),
        ],
        scratch_shapes=[
            VMEM((rows, 2 * units), F32),
            VMEM((rows, units), F32),
            VMEM((rows, 2 * units), BF16),
        ],
        compiler_params=pltpu.CompilerParams(vmem_limit_bytes=LIMIT),
        cost_estimate=pl.CostEstimate(
            flops=40 * rows * width * units,
            bytes_accessed=2 * (3 * rows * width + 3 * units * width),
            transcendentals=rows * units,
        ),
    )(src, pair_w, down_w)


def weight_kernel(count, *refs):
    sources, sides = refs[:count], refs[count : 2 * count]
    gate_ref, up_ref, down_ref = refs[2 * count :]
    units = gate_ref.shape[0]
    tile = sources[0].shape[3]

    def stacked(kind):
        return jnp.concatenate([s[:, kind].reshape(-1, tile) for s in sources], axis=0)

    left = jnp.concatenate([s[: 2 * units] for s in sides], axis=1)
    pair = jnp.dot(left, stacked(0), preferred_element_type=F32)
    left = jnp.concatenate([s[2 * units :] for s in sides], axis=1)
    down = jnp.dot(left, stacked(1), preferred_element_type=F32)
    gate_ref[...] = pair[:units].astype(BF16)
    up_ref[...] = pair[units:].astype(BF16)
    down_ref[...] = down.astype(BF16)


def weight_grads(sources, sides):
    width = sources[0].shape[3]
    units = sides[0].shape[0] // 3
    rows = sum(side.shape[1] for side in sides)
    tile = width // 4
    return pl.pallas_call(
        functools.partial(weight_kernel, len(sources)),
        grid=(width // tile,),
        in_specs=[
            pl.BlockSpec(src.shape[:3] + (tile,), lambda i: (0, 0, 0, i)) for src in sources
        ]
        + [pl.BlockSpec(side.shape, lambda i: (0, 0)) for side in sides],
        out_specs=[pl.BlockSpec((units, tile), lambda i: (0, i))] * 3,
        out_shape=[jax.ShapeDtypeStruct((units, width), BF16)] * 3,
        compiler_params=pltpu.CompilerParams(vmem_limit_bytes=LIMIT),
        cost_estimate=pl.CostEstimate(
            flops=24 * rows * width * units,
            bytes_accessed=2 * (2 * rows * width + 3 * units * width),
            transcendentals=0,
        ),
    )(*sources, *sides)


def near_combine_kernel(half, ids_ref, back_ref, out_ref):
    experts, per_core = back_ref.shape[0] // 2, back_ref.shape[1]
    toks = ids_ref.shape[1]
    _, _, rank = table(ids_ref[...], experts)
    row = lax.broadcasted_iota(jnp.int32, (experts, 2 * per_core, toks), 1)
    slots = (half + 2 * (row % per_core) + row // per_core).astype(F32)
    total = gather_slots(rank, slots, back_ref[...])
    fill_pieces(out_ref, total.astype(BF16), total.shape[1] // out_ref.shape[0])


def far_combine_kernel(ids_ref, back_ref, near_ref, out_ref):
    experts, per_core = back_ref.shape[0] // 2, back_ref.shape[1]
    toks = ids_ref.shape[1]
    _, _, rank = table(ids_ref[...], experts)
    slots = lax.broadcasted_iota(jnp.int32, (experts, 2 * per_core, toks), 1).astype(F32)
    total = gather_slots(rank, slots, back_ref[...])
    out_ref[...] = (total + near_ref[...].astype(F32)).astype(BF16)


def gather_slots(rank, slots, rows):
    count = rows.shape[0] * rows.shape[1]
    hit = jnp.where(rank[:, None, :] == slots, 1.0, 0.0).astype(BF16).reshape(count, -1)
    return lax.dot_general(
        hit, rows.reshape(count, -1), (((0,), (0,)), ((), ())), preferred_element_type=F32
    )


def near_combine(ids_t, returned, pieces, half):
    toks = ids_t.shape[1]
    width = returned.shape[2]
    wide = padded(width // pieces)
    steps = 2
    return pl.pallas_call(
        functools.partial(near_combine_kernel, half),
        grid=(steps,),
        in_specs=[
            pl.BlockSpec(ids_t.shape, lambda i: (0, 0)),
            pl.BlockSpec(returned.shape[:2] + (width // steps,), lambda i: (0, 0, i)),
        ],
        out_specs=pl.BlockSpec((pieces // steps, toks, wide), lambda i: (i, 0, 0)),
        out_shape=jax.ShapeDtypeStruct((pieces, toks, wide), BF16),
        compiler_params=pltpu.CompilerParams(vmem_limit_bytes=LIMIT),
    )(ids_t, returned)


def far_combine(ids_t, returned, near):
    return pl.pallas_call(
        far_combine_kernel,
        in_specs=[pl.BlockSpec(memory_space=VMEM)] * 3,
        out_specs=pl.BlockSpec(memory_space=VMEM),
        out_shape=jax.ShapeDtypeStruct(near.shape, BF16),
        compiler_params=pltpu.CompilerParams(vmem_limit_bytes=LIMIT),
    )(ids_t, returned, near)


def per_device(activations, out_grad, expert_ids, gate_values, gate_proj, up_proj, down_proj):
    devices = lax.axis_size("exp")
    planes = lax.axis_size("tp")
    experts = devices // 2
    toks, width = activations.shape
    slots = 8 * toks // devices
    half = slots // 2
    tp_at = lax.axis_index("tp").astype(jnp.int32)[None]
    ids_t = expert_ids.T
    gate_t = gate_values.T
    swap = [(i, i ^ 1) for i in range(devices)]

    def trade(v):
        return lax.ppermute(v, "exp", swap)

    def spread(v):
        return lax.all_to_all(v, "exp", split_axis=0, concat_axis=0, tiled=True)

    far, near = make_send(tp_at, ids_t, gate_t, activations, out_grad, experts, half)
    near = spread(jnp.transpose(near, (1, 0, 2)))
    near, far = lax.optimization_barrier((near, far))
    near = jnp.transpose(near, (1, 0, 2))
    near = lax.all_gather(near, "tp", axis=0, tiled=False)
    far = spread(far.reshape(devices, half, width)).reshape(far.shape)
    pair_w = jnp.concatenate([gate_proj[0], up_proj[0]], axis=0)
    down_w = down_proj[0]
    far_other = trade(far)
    near_other = trade(near)
    far_part, far_side = expert_part(far, pair_w, down_w, planes, False)
    far_other, far_part = lax.optimization_barrier((far_other, far_part))
    far_other_part, far_other_side = expert_part(far_other, pair_w, down_w, planes, False)
    far_sum = (far_part.astype(F32) + trade(far_other_part).astype(F32)).astype(BF16)
    near_other, far_other_part = lax.optimization_barrier((near_other, far_other_part))
    near_other_part, near_other_side = expert_part(near_other, pair_w, down_w, 1, True)
    near_part, near_side = expert_part(near, pair_w, down_w, 1, True)
    near_sum = (near_part.astype(F32) + trade(near_other_part).astype(F32)).astype(BF16)
    far_mine = lax.psum_scatter(far_sum, "tp", scatter_dimension=0, tiled=False)
    near_back = spread(near_sum.reshape(devices, half // 2, width))
    near_mine = near_combine(ids_t, near_back, planes, half)
    near_mine = lax.psum_scatter(near_mine, "tp", scatter_dimension=0, tiled=False)
    far_back = spread(far_mine.reshape(devices, half // 2, -1))
    piece = far_combine(ids_t, far_back, near_mine)
    gathered = lax.all_gather(piece, "tp", axis=0, tiled=False)
    gathered = gathered[:, :, : width // planes]
    in_grad = jnp.transpose(gathered, (1, 0, 2)).reshape(toks, width)
    gate_g, up_g, down_g = weight_grads(
        [far, far_other, near, near_other],
        [far_side, far_other_side, near_side, near_other_side],
    )
    return (in_grad, gate_g[None], up_g[None], down_g[None])


def solution(mesh):
    return jax.shard_map(
        per_device,
        mesh=mesh,
        in_specs=(
            P("exp", None),
            P("exp", None),
            P("exp", None),
            P("exp", None),
            P("exp", "tp", None),
            P("exp", "tp", None),
            P("exp", "tp", None),
        ),
        out_specs=(
            P("exp", None),
            P("exp", "tp", None),
            P("exp", "tp", None),
            P("exp", "tp", None),
        ),
        check_vma=False,
    )
```

time: 250 us -> 248 us (level)
  blocking collectives: 84.7 us -> 113 us
  waiting for transfers between devices: 84.1 us -> 56.2 us
  Pallas kernels: 47.4 us -> 41.7 us
    all_to_all x3 -> x4, blocking collectives: 84.7 us -> 113 us  [spread(): return lax.all_to_all(v, 'exp', split_axis=0, concat_axis=0, tiled=True)]
    reduce_scatter x1 -> x2, waiting for transfers between devices: 52.4 us -> 27.4 us  [the longest x1 25.5 us: per_device(): lax.psum_scatter(near_mine, 'tp', scatter_dimension=0, tiled=False)]
    ppermute x4, waiting for transfers between devices: 8.27 us -> 0.57 us  [trade(): return lax.ppermute(v, 'exp', swap)]
    unnamed x20 -> x34, local copies, waits for them, and re-layouts: 7.56 us -> 12.7 us
    all_gather x1, waiting for transfers between devices: 23.4 us -> 28.1 us  [per_device(): gathered = lax.all_gather(piece, 'tp', axis=0, tiled=False)]
    pallas_call x1, Pallas kernels: 14 us -> 9.52 us  [weight_grads(): pl.pallas_call(functools.partial(weight_kernel, len(sources)), grid=(widt...]
    pallas_call x5 -> x6, Pallas kernels: 29.6 us -> 28.3 us  [the longest x4 25.2 us: expert_part(): pl.pallas_call(functools.partial(expert_kernel, turn), grid=(2, steps), i...]
  transfers between devices with their start and end apart: 7 -> 8, of which waited for: 3 -> 4; matrix products, arithmetic and copies ran while one was open for 1% -> 3% of each run, Pallas kernels for 17% -> 15%
where the time goes in v2:
time: 248 us
  blocking collectives  113 us (46%)
  waiting for transfers between devices  56.2 us (23%)
  Pallas kernels  41.7 us (17%)
  local copies, waits for them, and re-layouts  14 us (6%)
  between operations  13.9 us (6%)
  other arithmetic  7.03 us (3%)
    all_to_all x4, blocking collectives, spread(): return lax.all_to_all(v, 'exp', split_axis=0, concat_axis=0, tiled=True)  113 us
    all_gather x1, waiting for transfers between devices, per_device(): gathered = lax.all_gather(piece, 'tp', axis=0, tiled=False)  28.1 us
    reduce_scatter x1, waiting for transfers between devices, per_device(): lax.psum_scatter(near_mine, 'tp', scatter_dimension=0, tiled=False)  25.5 us
    pallas_call x4, Pallas kernels, expert_part(): pl.pallas_call(functools.partial(expert_kernel, turn), grid=(2, steps), i...  25.2 us
    unnamed x34, local copies, waits for them, and re-layouts  12.7 us
    pallas_call x1, Pallas kernels, weight_grads(): pl.pallas_call(functools.partial(weight_kernel, len(sources)), grid=(widt...  9.52 us
  transfers between devices with their start and end apart: 8, of which 4 were waited for; matrix products, arithmetic and copies ran while one was open for 3% of the time, Pallas kernels for 15%

profile of v2, /device:TPU:2, one launch (start us, length us, event | category | flops | bytes accessed | tf_op | source)
XLA Modules:
  0.0 247.8 jit_solution(1131758945656890025)
XLA Ops:
  7.2 0.0 all-gather.5.cloned.1.call-start
  7.2 1.2 copy-done.1
  8.4 1.2 copy-done.2
  9.6 0.7 copy-done.4
  10.3 0.7 copy-done.6
  10.9 3.9 %shard_map.102 = (bf16[32,2,8,3584]{3,2,1,0:T(8,128)(2,1)S(1)}, bf16[2,32,3584]{2,1,0:T(8,128)(2,1)S(1)}) custom-call(s32[1]{0:T(128)} %bitcast.1.tp_ref, s32[2,128]{1,0:T(2,128)S(1)} %bitcast.26, f32[2,128]{1,0:T(2,128)S(1)} %bitcast.29, bf16[128,3584]{1,0:T(8,128)(2,1)S(1)} %copy-done.1, bf16[128,3584]{1,0:T(8,128)(2,1)S(1)} %copy-done.2), custom_call_target="tpu_custom_call" | custom-call | tf_op jit(solution)/shard_map/pallas_call | solution.py:73
  14.8 1.9 copy-done
  16.8 0.5 copy.14
  17.2 17.2 %all_to_all.20 = bf16[32,2,3584]{2,1,0:T(2,128)(2,1)S(1)} all-to-all(bf16[32,2,3584]{2,1,0:T(2,128)(2,1)S(1)} %copy.14), channel_id=1, replica_groups=mesh['exp'=32,'tp'=8] {'exp'}, dimensions={0} | all-to-all | bytes 917504 | tf_op jit(solution)/shard_map/all_to_all | solution.py:299
  34.5 0.8 copy.15
  35.3 0.0 all-gather.5.cloned.1.call-update
  35.3 0.0 reduce-scatter.3.cloned.1.call-start
  35.3 0.0 copy-start.14
  35.4 50.4 %all_to_all.21 = bf16[32,16,3584]{2,1,0:T(8,128)(2,1)} all-to-all(bf16[32,16,3584]{2,1,0:T(8,128)(2,1)} %bitcast.23), channel_id=1, replica_groups=mesh['exp'=32,'tp'=8] {'exp'}, dimensions={0} | all-to-all | bytes 7340032 | tf_op jit(solution)/shard_map/all_to_all | solution.py:299
  85.7 0.4 collective-permute-start
  86.1 0.1 collective-permute-start.2
  86.2 3.1 %pad_maximum_fusion.pair_ref = bf16[384,3584]{1,0:T(8,128)(2,1)} fusion(bf16[192,3584]{1,0:T(8,128)(2,1)S(1)} %bitcast.36, bf16[192,3584]{1,0:T(8,128)(2,1)} %bitcast.37), kind=kLoop, calls=%fused_computation.2 | loop fusion | flops 5505024 | bytes 5505024 | tf_op jit(solution)/shard_map/concatenate | solution.py:307
  89.4 6.2 %shard_map.103 = (bf16[8,256,512]{2,1,0:T(8,128)(2,1)S(1)}, bf16[576,256]{1,0:T(8,128)(2,1)S(1)}) custom-call(bf16[32,2,8,3584]{3,2,1,0:T(8,128)(2,1)} %bitcast.5.src_ref.refs_0_, bf16[384,3584]{1,0:T(8,128)(2,1)} %pad_maximum_fusion.pair_ref, bf16[192,3584]{1,0:T(8,128)(2,1)S(1)} %bitcast.30), custom_call_target="tpu_custom_call" | custom-call | flops 7046430720 | bytes 9633792 | tf_op jit(solution)/shard_map/pallas_call | solution.py:160
  95.6 0.6 collective-permute-done.src_ref.refs_1_
  96.2 6.3 %shard_map.104 = (bf16[8,256,512]{2,1,0:T(8,128)(2,1)S(1)}, bf16[576,256]{1,0:T(8,128)(2,1)S(1)}) custom-call(bf16[32,2,8,3584]{3,2,1,0:T(8,128)(2,1)} %collective-permute-done.src_ref.refs_1_, bf16[384,3584]{1,0:T(8,128)(2,1)} %pad_maximum_fusion.pair_ref, bf16[192,3584]{1,0:T(8,128)(2,1)S(1)} %bitcast.31), custom_call_target="tpu_custom_call" | custom-call | flops 7046430720 | bytes 9633792 | tf_op jit(solution)/shard_map/pallas_call | solution.py:160
  102.5 0.0 copy-start.8
  102.5 0.5 collective-permute-start.1
  102.9 1.9 copy-done.15
  104.8 6.3 %shard_map.106 = (bf16[1,256,3584]{2,1,0:T(8,128)(2,1)S(1)}, bf16[576,256]{1,0:T(8,128)(2,1)S(1)}) custom-call(bf16[8,2,32,3584]{3,2,1,0:T(8,128)(2,1)} %copy-done.15, bf16[384,3584]{1,0:T(8,128)(2,1)} %pad_maximum_fusion.pair_ref, bf16[192,3584]{1,0:T(8,128)(2,1)S(1)} %bitcast.32), custom_call_target="tpu_custom_call" | custom-call | flops 7046430720 | bytes 9633792 | tf_op jit(solution)/shard_map/pallas_call | solution.py:160
  111.2 0.7 copy-done.10
  111.9 0.1 collective-permute-start.3
  112.0 2.0 add_convert_fusion
  114.0 0.0 reduce-scatter.3.cloned.1.call-update
  114.0 0.2 reduce-scatter.5.cloned.1.call-start
  114.2 6.4 %shard_map.105 = (bf16[1,256,3584]{2,1,0:T(8,128)(2,1)S(1)}, bf16[576,256]{1,0:T(8,128)(2,1)S(1)}) custom-call(bf16[8,2,32,3584]{3,2,1,0:T(8,128)(2,1)} %bitcast.41, bf16[384,3584]{1,0:T(8,128)(2,1)} %pad_maximum_fusion.pair_ref, bf16[192,3584]{1,0:T(8,128)(2,1)S(1)} %bitcast.33), custom_call_target="tpu_custom_call" | custom-call | flops 7046430720 | bytes 9633792 | tf_op jit(solution)/shard_map/pallas_call | solution.py:160
  120.6 0.0 copy-start.12
  120.6 0.7 copy-done.12
  121.3 1.9 fusion
  123.3 0.0 copy-start.5
  123.3 30.7 %all_to_all.22.back_ref = bf16[32,8,3584]{2,1,0:T(8,128)(2,1)S(1)} all-to-all(bf16[32,8,3584]{2,1,0:T(8,128)(2,1)S(1)} %fusion), channel_id=1, replica_groups=mesh['exp'=32,'tp'=8] {'exp'}, dimensions={0} | all-to-all | bytes 3670016 | tf_op jit(solution)/shard_map/all_to_all | solution.py:299
  154.0 2.0 shard_map.107
  156.1 0.0 reduce-scatter.5.cloned.1.call-update
  156.1 0.0 all-gather.7.cloned.1.call-start
  156.1 2.0 reduce-scatter.3.cloned.1.call-done
  158.1 15.2 %all_to_all.23.back_ref = bf16[32,8,512]{2,1,0:T(8,128)(2,1)S(1)} all-to-all(bf16[32,8,512]{2,1,0:T(8,128)(2,1)} %bitcast.39), channel_id=1, replica_groups=mesh['exp'=32,'tp'=8] {'exp'}, dimensions={0} | all-to-all | bytes 524288 | tf_op jit(solution)/shard_map/all_to_all | solution.py:299
  173.3 25.5 %reduce-scatter.5.cloned.1.call-done = bf16[1,128,512]{2,1,0:T(8,128)(2,1)} async-done(((bf16[8,128,512]{2,1,0:T(8,128)(2,1)}), bf16[1,128,512]{2,1,0:T(8,128)(2,1)}) %reduce-scatter.5.cloned.1.call-update) | async-done | bytes 131088 | tf_op jit(solution)/shard_map/reduce_scatter | solution.py:322
  198.8 0.9 copy-done.3
  199.7 1.0 shard_map.108
  200.7 0.0 all-gather.7.cloned.1.call-update
  200.8 9.5 %shard_map.109 = (bf16[192,3584]{1,0:T(8,128)(2,1)}, bf16[192,3584]{1,0:T(8,128)(2,1)}, bf16[192,3584]{1,0:T(8,128)(2,1)}) custom-call(bf16[32,2,8,3584]{3,2,1,0:T(8,128)(2,1)} %bitcast.5.src_ref.refs_0_, bf16[32,2,8,3584]{3,2,1,0:T(8,128)(2,1)} %collective-permute-done.src_ref.refs_1_, bf16[8,2,32,3584]{3,2,1,0:T(8,128)(2,1)} %bitcast.42, ...), custom_call_target="tpu_custom_call" | custom-call | flops 16911433728 | bytes 18808832 | tf_op jit(solution)/shard_map/pallas_call | solution.py:210
  210.3 28.1 %all-gather.7.cloned.1.call-done = bf16[1024,512]{1,0:T(8,128)(2,1)} async-done(((bf16[128,512]{1,0:T(8,128)(2,1)}), bf16[1024,512]{1,0:T(8,128)(2,1)}) %all-gather.7.cloned.1.call-update) | async-done | bytes 1048592 | tf_op jit(solution)/shard_map/all_gather | solution.py:325
  238.4 1.6 copy.18
  240.0 1.3 copy.17
  (23 shorter events, 0.0 us)
Async XLA Ops:
  7.2 78.9 %all-gather.5.cloned.1.call-start = ((), (), s32[]{:S(2)}) async-start(), calls=%async_computation.8 | async-start | bytes 4128768 | tf_op jit(solution)/shard_map/all_gather | solution.py:305
  7.2 1.2 copy-start.1
  8.4 1.2 copy-start.2
  9.6 0.7 copy-start.4
  10.3 0.7 copy-start.6
  14.8 1.9 copy-start
  35.3 122.8 %reduce-scatter.3.cloned.1.call-start = ((), (), s32[]{:S(2)}) async-start(), calls=%async_computation.6 | async-start | bytes 2359296 | tf_op jit(solution)/shard_map/reduce_scatter | solution.py:319
  35.3 50.9 %copy-start.14 = (bf16[1,192,3584]{2,1,0:T(8,128)(2,1)S(1)}, bf16[1,192,3584]{2,1,0:T(8,128)(2,1)}, u32[]{:S(2)}) copy-start(bf16[1,192,3584]{2,1,0:T(8,128)(2,1)} %param.12) | copy-start | bytes 4128772
  85.7 10.5 %collective-permute-start = (bf16[32,2,8,3584]{3,2,1,0:T(8,128)(2,1)}, bf16[32,2,8,3584]{3,2,1,0:T(8,128)(2,1)}, u32[]{:S(2)}, u32[]{:S(2)}) collective-permute-start(bf16[32,2,8,3584]{3,2,1,0:T(8,128)(2,1)} %bitcast.5.src_ref.refs_0_), channel_id=1, source_target_pairs={{0,8},{8,0},{16,24},{24,16},{32,40},{40,32},{48,56},{56,48},{64,72... | collective-permute-start | bytes 11010056 | tf_op jit(solution)/shard_map/ppermute | solution.py:296
  86.1 16.8 %collective-permute-start.2 = (bf16[8,2,32,3584]{3,2,1,0:T(8,128)(2,1)}, bf16[8,2,32,3584]{3,2,1,0:T(8,128)(2,1)S(1)}, u32[]{:S(2)}, u32[]{:S(2)}) collective-permute-start(bf16[8,2,32,3584]{3,2,1,0:T(8,128)(2,1)} %bitcast.40), channel_id=1, source_target_pairs={{0,8},{8,0},{16,24},{24,16},{32,40},{40,32},{48,56},{56,48},{64,72... | collective-permute-start | bytes 11010056 | tf_op jit(solution)/shard_map/ppermute | solution.py:296
  86.2 3.1 %copy-start.7 = (bf16[1,192,3584]{2,1,0:T(8,128)(2,1)S(1)}, bf16[1,192,3584]{2,1,0:T(8,128)(2,1)}, u32[]{:S(2)}) copy-start(bf16[1,192,3584]{2,1,0:T(8,128)(2,1)} %param.13) | copy-start | bytes 4128772
  102.5 8.7 %copy-start.8 = (bf16[576,256]{1,0:T(8,128)(2,1)}, bf16[576,256]{1,0:T(8,128)(2,1)S(1)}, u32[]{:S(2)}) copy-start(bf16[576,256]{1,0:T(8,128)(2,1)S(1)} %get-tuple-element.34.refs_5_) | copy-start | bytes 884740
  102.5 9.5 %collective-permute-start.1 = (bf16[8,256,512]{2,1,0:T(8,128)(2,1)S(1)}, bf16[8,256,512]{2,1,0:T(8,128)(2,1)S(1)}, u32[]{:S(2)}, u32[]{:S(2)}) collective-permute-start(bf16[8,256,512]{2,1,0:T(8,128)(2,1)S(1)} %get-tuple-element.28), channel_id=1, source_target_pairs={{0,8},{8,0},{16,24},{24,16},{32,40},{40,32},{48,56},{56,48},{64,72... | collective-permute-start | bytes 6291464 | tf_op jit(solution)/shard_map/ppermute | solution.py:296
  102.9 1.9 copy-start.15
  111.2 0.7 copy-start.10
  111.9 9.5 %collective-permute-start.3 = (bf16[1,256,3584]{2,1,0:T(8,128)(2,1)S(1)}, bf16[1,256,3584]{2,1,0:T(8,128)(2,1)}, u32[]{:S(2)}, u32[]{:S(2)}) collective-permute-start(bf16[1,256,3584]{2,1,0:T(8,128)(2,1)S(1)} %get-tuple-element.32), channel_id=1, source_target_pairs={{0,8},{8,0},{16,24},{24,16},{32,40},{40,32},{48,56},{56,48},{64,72... | collective-permute-start | bytes 5505032 | tf_op jit(solution)/shard_map/ppermute | solution.py:296
  114.0 84.8 %reduce-scatter.5.cloned.1.call-start = ((), (), s32[]{:S(2)}) async-start(), calls=%async_computation.7 | async-start | bytes 1179648 | tf_op jit(solution)/shard_map/reduce_scatter | solution.py:322
  120.6 0.7 copy-start.12
  123.3 30.7 %copy-start.5 = (s32[128,2]{0,1:T(2,128)S(1)}, s32[128,2]{0,1:T(2,128)}, u32[]{:S(2)}) copy-start(s32[128,2]{0,1:T(2,128)} %param.9) | copy-start | bytes 3076
  154.0 46.7 %copy-start.9 = (bf16[576,256]{1,0:T(8,128)(2,1)S(1)}, bf16[576,256]{1,0:T(8,128)(2,1)}, u32[]{:S(2)}) copy-start(bf16[576,256]{1,0:T(8,128)(2,1)} %copy-done.8) | copy-start | bytes 884740
  154.0 46.7 %copy-start.11 = (bf16[576,256]{1,0:T(8,128)(2,1)S(1)}, bf16[576,256]{1,0:T(8,128)(2,1)}, u32[]{:S(2)}) copy-start(bf16[576,256]{1,0:T(8,128)(2,1)} %copy-done.10) | copy-start | bytes 884740
  154.0 46.7 %copy-start.13 = (bf16[576,256]{1,0:T(8,128)(2,1)S(1)}, bf16[576,256]{1,0:T(8,128)(2,1)}, u32[]{:S(2)}) copy-start(bf16[576,256]{1,0:T(8,128)(2,1)} %copy-done.12) | copy-start | bytes 884740
  156.1 82.3 %all-gather.7.cloned.1.call-start = ((), (), s32[]{:S(2)}) async-start(), calls=%async_computation.9 | async-start | bytes 1179648 | tf_op jit(solution)/shard_map/all_gather | solution.py:325
  198.8 0.9 copy-start.3
Sparse Core Ops, SparseCore 0:
  35.4 50.1 all-gather.4
  114.1 43.9 reduce-scatter.2
  161.2 37.5 reduce-scatter.4
  200.8 37.4 all-gather.6

commit v3 on v2

v3 whole, which is shorter than its diff:
```python
import functools

import jax
import jax.numpy as jnp
from jax import lax
from jax.experimental import pallas as pl
from jax.experimental.pallas import tpu as pltpu
from jax.sharding import PartitionSpec as P

F32 = jnp.float32
BF16 = jnp.bfloat16
VMEM = pltpu.VMEM
LIMIT = 48 * 1024 * 1024


def table(ids, experts):
    toks = ids.shape[1]
    expert = lax.broadcasted_iota(jnp.int32, (experts, toks), 0)
    first = ids[0:1, :] == expert
    second = ids[1:2, :] == expert
    named = jnp.where(first | second, 1.0, 0.0)
    earlier = lax.broadcasted_iota(jnp.int32, (toks, toks), 0)
    later = lax.broadcasted_iota(jnp.int32, (toks, toks), 1)
    before = jnp.where(earlier < later, 1.0, 0.0).astype(BF16)
    rank = jnp.dot(named.astype(BF16), before, preferred_element_type=F32)
    return first, second, jnp.where(named > 0.0, rank, -1.0)


def select(ids_ref, gate_ref, act_ref, grad_ref, slots):
    experts, count, toks = slots.shape
    first, second, rank = table(ids_ref[...], experts)
    gate = jnp.where(first, gate_ref[0:1, :], 0.0) + jnp.where(second, gate_ref[1:2, :], 0.0)
    hit = (rank[:, None, :] == slots.astype(F32)).reshape(experts * count, toks)
    weight = jnp.broadcast_to(gate[:, None, :], slots.shape).reshape(experts * count, toks)
    scale = jnp.sum(jnp.where(hit, weight, 0.0), axis=1, keepdims=True)
    mask = jnp.where(hit, 1.0, 0.0).astype(BF16)
    rows = jnp.dot(mask, act_ref[...], preferred_element_type=F32).astype(BF16)
    picked = jnp.dot(mask, grad_ref[...], preferred_element_type=F32)
    return rows, (picked * scale).astype(BF16)


def far_kernel(ids_ref, gate_ref, act_ref, grad_ref, out_ref):
    experts, count, toks = out_ref.shape[0] // 2, 2 * out_ref.shape[2], ids_ref.shape[1]
    slots = lax.broadcasted_iota(jnp.int32, (experts, count, toks), 1)
    rows, weighted = select(ids_ref, gate_ref, act_ref, grad_ref, slots)
    out_ref[:, 0] = rows.reshape(2 * experts, count // 2, -1)
    out_ref[:, 1] = weighted.reshape(2 * experts, count // 2, -1)


def near_kernel(half, tp_ref, ids_ref, gate_ref, act_ref, grad_ref, out_ref):
    experts, toks = out_ref.shape[1] // 2, ids_ref.shape[1]
    inner = lax.broadcasted_iota(jnp.int32, (experts, 8, toks), 1)
    slots = jnp.where(inner < 2, half + 2 * tp_ref[0] + inner, -2)
    rows, weighted = select(ids_ref, gate_ref, act_ref, grad_ref, slots)
    out_ref[0] = rows.reshape(experts, 8, -1)[:, :2].reshape(2 * experts, -1)
    out_ref[1] = weighted.reshape(experts, 8, -1)[:, :2].reshape(2 * experts, -1)


def send_far(ids_t, gate_t, acts, grads, experts, half):
    toks, width = acts.shape
    tile = width // 4
    return pl.pallas_call(
        far_kernel,
        grid=(width // tile,),
        in_specs=[
            pl.BlockSpec((2, toks), lambda i: (0, 0)),
            pl.BlockSpec((2, toks), lambda i: (0, 0)),
            pl.BlockSpec((toks, tile), lambda i: (0, i)),
            pl.BlockSpec((toks, tile), lambda i: (0, i)),
        ],
        out_specs=pl.BlockSpec((2 * experts, 2, half // 2, tile), lambda i: (0, 0, 0, i)),
        out_shape=jax.ShapeDtypeStruct((2 * experts, 2, half // 2, width), BF16),
        compiler_params=pltpu.CompilerParams(vmem_limit_bytes=LIMIT),
        cost_estimate=pl.CostEstimate(
            flops=16 * experts * half * toks * width,
            bytes_accessed=4 * (toks + experts * half) * width,
            transcendentals=0,
        ),
    )(ids_t, gate_t, acts, grads)


def send_near(tp_at, ids_t, gate_t, acts, grads, experts, half):
    toks, width = acts.shape
    tile = width // 2
    return pl.pallas_call(
        functools.partial(near_kernel, half),
        grid=(width // tile,),
        in_specs=[
            pl.BlockSpec(memory_space=pltpu.SMEM),
            pl.BlockSpec((2, toks), lambda i: (0, 0)),
            pl.BlockSpec((2, toks), lambda i: (0, 0)),
            pl.BlockSpec((toks, tile), lambda i: (0, i)),
            pl.BlockSpec((toks, tile), lambda i: (0, i)),
        ],
        out_specs=pl.BlockSpec((2, 2 * experts, tile), lambda i: (0, 0, i)),
        out_shape=jax.ShapeDtypeStruct((2, 2 * experts, width), BF16),
        compiler_params=pltpu.CompilerParams(vmem_limit_bytes=LIMIT),
    )(tp_at, ids_t, gate_t, acts, grads)


def expert_kernel(
    turn, src_ref, gate_ref, up_ref, down_ref, part_ref, side_ref, pre_acc, back_acc, dgu_ref, kept
):
    outer, _, inner, width = src_ref.shape
    rows = outer * inner
    units = down_ref.shape[0]
    contract = (((1,), (1,)), ((), ()))
    phase, at = pl.program_id(0), pl.program_id(1)

    @pl.when(phase == 0)
    def _():
        x = src_ref[:, 0].reshape(rows, width)
        g = src_ref[:, 1].reshape(rows, width)
        kept[at, :units] = gate_ref[...]
        kept[at, units:] = up_ref[...]
        pre = lax.dot_general(x, kept[at], contract, preferred_element_type=F32)
        back = lax.dot_general(g, down_ref[...], contract, preferred_element_type=F32)

        @pl.when(at == 0)
        def _():
            pre_acc[...] = pre
            back_acc[...] = back

        @pl.when(at > 0)
        def _():
            pre_acc[...] += pre
            back_acc[...] += back

    @pl.when((phase == 0) & (at == pl.num_programs(1) - 1))
    def _():
        pre_gate = pre_acc[:, :units]
        pre_up = pre_acc[:, units:]
        back = back_acc[...]
        sig = jax.nn.sigmoid(pre_gate)
        silu = pre_gate * sig
        hidden = (silu * pre_up).astype(BF16)
        d_gate = (back * pre_up * sig * (1.0 + pre_gate * (1.0 - sig))).astype(BF16)
        d_up = (back * silu).astype(BF16)
        side_ref[:units, :] = d_gate.T
        side_ref[units : 2 * units, :] = d_up.T
        side_ref[2 * units :, :] = hidden.T
        dgu_ref[:, :units] = d_gate
        dgu_ref[:, units:] = d_up
        if turn:
            to = lax.broadcasted_iota(jnp.int32, (rows, rows), 0)
            of = lax.broadcasted_iota(jnp.int32, (rows, rows), 1)
            moved = jnp.where(of == (to % outer) * inner + to // outer, 1.0, 0.0).astype(BF16)
            dgu_ref[...] = jnp.dot(moved, dgu_ref[...], preferred_element_type=F32).astype(BF16)

    @pl.when(phase == 1)
    def _():
        part = jnp.dot(dgu_ref[...], kept[at], preferred_element_type=F32)
        part_ref[...] = part.astype(BF16)


def expert_part(src, gate_w, up_w, down_w, turn):
    outer, _, inner, width = src.shape
    rows = outer * inner
    units = down_w.shape[0]
    steps = 2
    tile = width // steps
    last = steps - 1

    def first_phase(p, i):
        return jnp.where(p == 0, i, last)

    weight_spec = pl.BlockSpec((units, tile), lambda p, i: (0, first_phase(p, i)))
    return pl.pallas_call(
        functools.partial(expert_kernel, turn),
        grid=(2, steps),
        in_specs=[
            pl.BlockSpec((outer, 2, inner, tile), lambda p, i: (0, 0, 0, first_phase(p, i))),
            weight_spec,
            weight_spec,
            weight_spec,
        ],
        out_specs=[
            pl.BlockSpec((rows, tile), lambda p, i: (0, p * i)),
            pl.BlockSpec((3 * units, rows), lambda p, i: (0, 0)),
        ],
        out_shape=[
            jax.ShapeDtypeStruct((rows, width), BF16),
            jax.ShapeDtypeStruct((3 * units, rows), BF16),
        ],
        scratch_shapes=[
            VMEM((rows, 2 * units), F32),
            VMEM((rows, units), F32),
            VMEM((rows, 2 * units), BF16),
            VMEM((steps, 2 * units, tile), BF16),
        ],
        compiler_params=pltpu.CompilerParams(vmem_limit_bytes=LIMIT),
        cost_estimate=pl.CostEstimate(
            flops=40 * rows * width * units,
            bytes_accessed=2 * (3 * rows * width + 3 * units * width),
            transcendentals=rows * units,
        ),
    )(src, gate_w, up_w, down_w)


def merge_kernel(far_ref, far_more_ref, near_ref, near_more_ref, out_ref):
    wide = out_ref.shape[2] // 2
    far = (far_ref[...].astype(F32) + far_more_ref[...].astype(F32)).astype(BF16)
    near = (near_ref[...].astype(F32) + near_more_ref[...].astype(F32)).astype(BF16)
    for j in range(out_ref.shape[0]):
        at = slice(j * wide, (j + 1) * wide)
        out_ref[j] = jnp.concatenate([far[:, at], near[:, at]], axis=1)


def merge(far, far_more, near, near_more, pieces):
    rows, width = far.shape
    steps = pieces // 2
    spec = pl.BlockSpec((rows, width // steps), lambda i: (0, i))
    return pl.pallas_call(
        merge_kernel,
        grid=(steps,),
        in_specs=[spec] * 4,
        out_specs=pl.BlockSpec((2, rows, 2 * width // pieces), lambda i: (i, 0, 0)),
        out_shape=jax.ShapeDtypeStruct((pieces, rows, 2 * width // pieces), BF16),
        compiler_params=pltpu.CompilerParams(vmem_limit_bytes=LIMIT),
    )(far, far_more, near, near_more)


def weight_kernel(count, *refs):
    sources, sides = refs[:count], refs[count : 2 * count]
    gate_ref, up_ref, down_ref = refs[2 * count :]
    units = gate_ref.shape[0]
    tile = sources[0].shape[3]

    def stacked(kind):
        return jnp.concatenate([s[:, kind].reshape(-1, tile) for s in sources], axis=0)

    left = jnp.concatenate([s[: 2 * units] for s in sides], axis=1)
    pair = jnp.dot(left, stacked(0), preferred_element_type=F32)
    left = jnp.concatenate([s[2 * units :] for s in sides], axis=1)
    down = jnp.dot(left, stacked(1), preferred_element_type=F32)
    gate_ref[...] = pair[:units].astype(BF16)
    up_ref[...] = pair[units:].astype(BF16)
    down_ref[...] = down.astype(BF16)


def weight_grads(sources, sides):
    width = sources[0].shape[3]
    units = sides[0].shape[0] // 3
    rows = sum(side.shape[1] for side in sides)
    tile = width // 4
    return pl.pallas_call(
        functools.partial(weight_kernel, len(sources)),
        grid=(width // tile,),
        in_specs=[
            pl.BlockSpec(src.shape[:3] + (tile,), lambda i: (0, 0, 0, i)) for src in sources
        ]
        + [pl.BlockSpec(side.shape, lambda i: (0, 0)) for side in sides],
        out_specs=[pl.BlockSpec((units, tile), lambda i: (0, i))] * 3,
        out_shape=[jax.ShapeDtypeStruct((units, width), BF16)] * 3,
        compiler_params=pltpu.CompilerParams(vmem_limit_bytes=LIMIT),
        cost_estimate=pl.CostEstimate(
            flops=24 * rows * width * units,
            bytes_accessed=2 * (2 * rows * width + 3 * units * width),
            transcendentals=0,
        ),
    )(*sources, *sides)


def combine_kernel(half, ids_ref, back_ref, out_ref):
    experts, per_core = back_ref.shape[0] // 2, back_ref.shape[1]
    toks = ids_ref.shape[1]
    wide = out_ref.shape[1]
    _, _, rank = table(ids_ref[...], experts)
    row = lax.broadcasted_iota(jnp.int32, (experts, 2 * per_core, toks), 1)
    late = half + 2 * (row % per_core) + row // per_core
    rows = back_ref[...].reshape(2 * experts * per_core, 2 * wide)
    total = gather_slots(rank, row.astype(F32), rows)[:, :wide]
    total += gather_slots(rank, late.astype(F32), rows)[:, wide:]
    out_ref[...] = total.astype(BF16)


def gather_slots(rank, slots, rows):
    hit = jnp.where(rank[:, None, :] == slots, 1.0, 0.0).astype(BF16).reshape(rows.shape[0], -1)
    return lax.dot_general(hit, rows, (((0,), (0,)), ((), ())), preferred_element_type=F32)


def combine(ids_t, returned, half):
    toks = ids_t.shape[1]
    return pl.pallas_call(
        functools.partial(combine_kernel, half),
        in_specs=[pl.BlockSpec(memory_space=VMEM)] * 2,
        out_specs=pl.BlockSpec(memory_space=VMEM),
        out_shape=jax.ShapeDtypeStruct((toks, returned.shape[2] // 2), BF16),
        compiler_params=pltpu.CompilerParams(vmem_limit_bytes=LIMIT),
    )(ids_t, returned)


def per_device(activations, out_grad, expert_ids, gate_values, gate_proj, up_proj, down_proj):
    devices = lax.axis_size("exp")
    planes = lax.axis_size("tp")
    experts = devices // 2
    toks, width = activations.shape
    slots = 8 * toks // devices
    half = slots // 2
    tp_at = lax.axis_index("tp").astype(jnp.int32)[None]
    ids_t = expert_ids.T
    gate_t = gate_values.T
    swap = [(i, i ^ 1) for i in range(devices)]

    def trade(v):
        return lax.ppermute(v, "exp", swap)

    def spread(v):
        return lax.all_to_all(v, "exp", split_axis=0, concat_axis=0, tiled=True)

    near = send_near(tp_at, ids_t, gate_t, activations, out_grad, experts, half)
    near = spread(jnp.transpose(near, (1, 0, 2)))
    far = send_far(ids_t, gate_t, activations, out_grad, experts, half)
    near, far = lax.optimization_barrier((near, far))
    near = jnp.transpose(near, (1, 0, 2))
    near = lax.all_gather(near, "tp", axis=0, tiled=False)
    far = spread(far.reshape(devices, half, width)).reshape(far.shape)
    weights = (gate_proj[0], up_proj[0], down_proj[0])
    far_other = trade(far)
    near_other = trade(near)
    far_part, far_side = expert_part(far, *weights, False)
    far_other, far_part = lax.optimization_barrier((far_other, far_part))
    far_other_part, far_other_side = expert_part(far_other, *weights, False)
    far_sent = trade(far_other_part)
    near_other, far_other_part = lax.optimization_barrier((near_other, far_other_part))
    near_other_part, near_other_side = expert_part(near_other, *weights, True)
    near_sent = trade(near_other_part)
    near, near_other_part = lax.optimization_barrier((near, near_other_part))
    near_part, near_side = expert_part(near, *weights, True)
    both = merge(far_part, far_sent, near_part, near_sent, planes)
    mine = lax.psum_scatter(both, "tp", scatter_dimension=0, tiled=False)
    returned = spread(mine.reshape(devices, half // 2, -1))
    piece = combine(ids_t, returned, half)
    gathered = lax.all_gather(piece, "tp", axis=0, tiled=False)
    in_grad = jnp.transpose(gathered, (1, 0, 2)).reshape(toks, width)
    gate_g, up_g, down_g = weight_grads(
        [far, far_other, near, near_other],
        [far_side, far_other_side, near_side, near_other_side],
    )
    return (in_grad, gate_g[None], up_g[None], down_g[None])


def solution(mesh):
    return jax.shard_map(
        per_device,
        mesh=mesh,
        in_specs=(
            P("exp", None),
            P("exp", None),
            P("exp", None),
            P("exp", None),
            P("exp", "tp", None),
            P("exp", "tp", None),
            P("exp", "tp", None),
        ),
        out_specs=(
            P("exp", None),
            P("exp", "tp", None),
            P("exp", "tp", None),
            P("exp", "tp", None),
        ),
        check_vma=False,
    )
```

time: 248 us -> 229 us (0.923)
  blocking collectives: 113 us -> 77.3 us
  starting transfers between devices: 1.45 us -> 16.1 us
  other arithmetic: 7.03 us -> 0 us
  waiting for transfers between devices: 56.2 us -> 60.6 us
    all_to_all x4 -> x1, blocking collectives: 113 us -> 50.5 us  [spread(): return lax.all_to_all(v, 'exp', split_axis=0, concat_axis=0, tiled=True)]
    all_gather x1 -> x0, waiting for transfers between devices: 28.1 us -> none  [per_device(): gathered = lax.all_gather(piece, 'tp', axis=0, tiled=False)]
    all_gather x0 -> x1, blocking collectives: none -> 26.8 us  [per_device(): gathered = lax.all_gather(piece, 'tp', axis=0, tiled=False)]
    reduce_scatter x2 -> x1, waiting for transfers between devices: 27.4 us -> 52.6 us  [per_device(): mine = lax.psum_scatter(both, 'tp', scatter_dimension=0, tiled=False)]
    all_to_all x0 -> x2, starting transfers between devices: none -> 15 us  [spread(): return lax.all_to_all(v, 'exp', split_axis=0, concat_axis=0, tiled=True)]
    all_to_all x0 -> x2, waiting for transfers between devices: none -> 5.46 us  [spread(): return lax.all_to_all(v, 'exp', split_axis=0, concat_axis=0, tiled=True)]
    concatenate x1 -> x0, other arithmetic: 3.13 us -> none  [per_device(): pair_w = jnp.concatenate([gate_proj[0], up_proj[0]], axis=0)]
    pallas_call x3 -> x4, Pallas kernels: 6.93 us -> 9.08 us  [the longest x1 4.8 us: merge(): pl.pallas_call(merge_kernel, grid=(steps,), in_specs=[spec] * 4, out_spec...]
  transfers between devices with their start and end apart: 8 -> 8, of which waited for: 4 -> 4; matrix products, arithmetic and copies ran while one was open for 3% -> 0% of each run, Pallas kernels for 15% -> 16%
where the time goes in v3:
time: 229 us; the launch traced here: 228 us
  blocking collectives  77.3 us (34%)
  waiting for transfers between devices  60.6 us (26%)
  Pallas kernels  43.4 us (19%)
  local copies, waits for them, and re-layouts  16.3 us (7%)
  starting transfers between devices  16.1 us (7%)
  between operations  14.2 us (6%)
    reduce_scatter x1, waiting for transfers between devices, per_device(): mine = lax.psum_scatter(both, 'tp', scatter_dimension=0, tiled=False)  52.6 us
    all_to_all x1, blocking collectives, spread(): return lax.all_to_all(v, 'exp', split_axis=0, concat_axis=0, tiled=True)  50.5 us
    all_gather x1, blocking collectives, per_device(): gathered = lax.all_gather(piece, 'tp', axis=0, tiled=False)  26.8 us
    pallas_call x4, Pallas kernels, expert_part(): pl.pallas_call(functools.partial(expert_kernel, turn), grid=(2, steps), i...  24.8 us
    all_to_all x2, starting transfers between devices, spread(): return lax.all_to_all(v, 'exp', split_axis=0, concat_axis=0, tiled=True)  15 us
    unnamed x41, local copies, waits for them, and re-layouts  13.6 us
    pallas_call x1, Pallas kernels, weight_grads(): pl.pallas_call(functools.partial(weight_kernel, len(sources)), grid=(widt...  9.55 us
    all_to_all x2, waiting for transfers between devices, spread(): return lax.all_to_all(v, 'exp', split_axis=0, concat_axis=0, tiled=True)  5.46 us
  transfers between devices with their start and end apart: 8, of which 4 were waited for; matrix products, arithmetic and copies ran while one was open for 0% of the time, Pallas kernels for 16%

profile of v3, /device:TPU:2, one launch (start us, length us, event | category | flops | bytes accessed | tf_op | source)
XLA Modules:
  0.0 227.9 jit_solution(12326308316290361247)
XLA Ops:
  7.2 0.0 copy-start.3
  7.2 1.2 copy-done.3
  8.4 1.2 copy-done.5
  9.5 0.7 copy-done.7
  10.2 0.7 copy-done.9
  10.9 1.3 shard_map.102
  12.2 1.2 copy.14
  13.4 7.6 %all-to-all-start = ((bf16[32,2,3584]{2,1,0:T(2,128)(2,1)}), bf16[32,2,3584]{2,1,0:T(2,128)(2,1)S(1)}, u32[]{:S(2)}, u32[]{:S(2)}) async-start(bf16[32,2,3584]{2,1,0:T(2,128)(2,1)} %copy.14), calls=%async_computation | async-start | bytes 917504 | tf_op jit(solution)/shard_map/all_to_all | solution.py:309
  21.0 0.0 all-gather.4.cloned.1.call-start
  21.1 2.5 %shard_map.103 = bf16[32,2,8,3584]{3,2,1,0:T(8,128)(2,1)S(1)} custom-call(s32[2,128]{1,0:T(2,128)S(1)} %bitcast.22, f32[2,128]{1,0:T(2,128)S(1)} %bitcast.25, bf16[128,3584]{1,0:T(8,128)(2,1)S(1)} %copy-done.4, bf16[128,3584]{1,0:T(8,128)(2,1)S(1)} %copy-done.6), custom_call_target="tpu_custom_call" | custom-call | flops 1879048192 | bytes 5505024 | tf_op jit(solution)/shard_map/pallas_call | solution.py:62
  23.7 1.9 copy-done
  25.6 5.2 %all-to-all-done = bf16[32,2,3584]{2,1,0:T(2,128)(2,1)S(1)} async-done(((bf16[32,2,3584]{2,1,0:T(2,128)(2,1)}), bf16[32,2,3584]{2,1,0:T(2,128)(2,1)S(1)}, u32[]{:S(2)}, u32[]{:S(2)}) %all-to-all-start) | async-done | bytes 458784 | tf_op jit(solution)/shard_map/all_to_all | solution.py:309
  30.8 0.8 copy.15
  31.6 0.0 all-gather.4.cloned.1.call-update
  31.7 0.0 reduce-scatter.2.cloned.1.call-start
  31.7 0.0 copy-start.11
  31.7 0.0 copy-start.12
  31.7 50.5 %all_to_all.15 = bf16[32,16,3584]{2,1,0:T(8,128)(2,1)} all-to-all(bf16[32,16,3584]{2,1,0:T(8,128)(2,1)} %bitcast.19), channel_id=1, replica_groups=mesh['exp'=32,'tp'=8] {'exp'}, dimensions={0} | all-to-all | bytes 7340032 | tf_op jit(solution)/shard_map/all_to_all | solution.py:309
  82.2 0.4 collective-permute-start
  82.6 0.1 collective-permute-start.2
  82.8 0.0 copy-done.12
  82.8 1.3 copy-done.13
  84.1 6.1 %shard_map.104 = (bf16[256,3584]{1,0:T(8,128)(2,1)}, bf16[576,256]{1,0:T(8,128)(2,1)S(1)}) custom-call(bf16[32,2,8,3584]{3,2,1,0:T(8,128)(2,1)} %bitcast.5.src_ref.refs_0_, bf16[192,3584]{1,0:T(8,128)(2,1)S(1)} %bitcast.26, bf16[192,3584]{1,0:T(8,128)(2,1)S(1)} %bitcast.30, bf16[192,3584]{1,0:T(8,128)(2,1)S(1)} %bitcast.34), custom_call_target="tpu_custom_call" | custom-call | flops 7046430720 | bytes 9633792 | tf_op jit(solution)/shard_map/pallas_call | solution.py:168
  90.2 2.5 %collective-permute-done.src_ref.refs_1_ = bf16[32,2,8,3584]{3,2,1,0:T(8,128)(2,1)} collective-permute-done((bf16[32,2,8,3584]{3,2,1,0:T(8,128)(2,1)}, bf16[32,2,8,3584]{3,2,1,0:T(8,128)(2,1)}, u32[]{:S(2)}, u32[]{:S(2)}) %collective-permute-start) | collective-permute-done | bytes 3670048 | tf_op jit(solution)/shard_map/ppermute | solution.py:306
  92.7 6.1 %shard_map.105 = (bf16[256,3584]{1,0:T(8,128)(2,1)}, bf16[576,256]{1,0:T(8,128)(2,1)S(1)}) custom-call(bf16[32,2,8,3584]{3,2,1,0:T(8,128)(2,1)} %collective-permute-done.src_ref.refs_1_, bf16[192,3584]{1,0:T(8,128)(2,1)S(1)} %bitcast.27, bf16[192,3584]{1,0:T(8,128)(2,1)S(1)} %bitcast.31, bf16[192,3584]{1,0:T(8,128)(2,1)S(1)} %bitcast.35), custom_call_target="tpu_custom_call" | custom-call | flops 7046430720 | bytes 9633792 | tf_op jit(solution)/shard_map/pallas_call | solution.py:168
  98.8 0.4 collective-permute-start.1
  99.2 0.0 collective-permute-done.2.src_ref.refs_3_
  99.2 1.9 copy-done.19
  101.1 6.2 %shard_map.106 = (bf16[256,3584]{1,0:T(8,128)(2,1)}, bf16[576,256]{1,0:T(8,128)(2,1)S(1)}) custom-call(bf16[8,2,32,3584]{3,2,1,0:T(8,128)(2,1)} %copy-done.19, bf16[192,3584]{1,0:T(8,128)(2,1)S(1)} %bitcast.28, bf16[192,3584]{1,0:T(8,128)(2,1)S(1)} %bitcast.32, bf16[192,3584]{1,0:T(8,128)(2,1)S(1)} %bitcast.36), custom_call_target="tpu_custom_call" | custom-call | flops 7046430720 | bytes 9633792 | tf_op jit(solution)/shard_map/pallas_call | solution.py:168
  107.3 0.1 collective-permute-start.3
  107.4 6.4 %shard_map.107 = (bf16[256,3584]{1,0:T(8,128)(2,1)}, bf16[576,256]{1,0:T(8,128)(2,1)S(1)}) custom-call(bf16[8,2,32,3584]{3,2,1,0:T(8,128)(2,1)} %bitcast.43, bf16[192,3584]{1,0:T(8,128)(2,1)S(1)} %bitcast.29, bf16[192,3584]{1,0:T(8,128)(2,1)S(1)} %bitcast.33, bf16[192,3584]{1,0:T(8,128)(2,1)S(1)} %bitcast.37), custom_call_target="tpu_custom_call" | custom-call | flops 7046430720 | bytes 9633792 | tf_op jit(solution)/shard_map/pallas_call | solution.py:168
  113.8 0.7 copy-done.16
  114.5 0.0 collective-permute-done.1.far_more_ref
  114.5 0.0 collective-permute-done.3.near_more_ref
  114.5 1.2 copy-done.18
  115.7 1.5 copy-done.2
  117.2 4.8 %shard_map.108 = bf16[8,256,896]{2,1,0:T(8,128)(2,1)} custom-call(bf16[256,3584]{1,0:T(8,128)(2,1)S(1)} %copy-done.1, bf16[256,3584]{1,0:T(8,128)(2,1)S(1)} %collective-permute-done.1.far_more_ref, bf16[256,3584]{1,0:T(8,128)(2,1)S(1)} %copy-done.2, bf16[256,3584]{1,0:T(8,128)(2,1)} %copy-done.18), custom_call_target="tpu_custom_call" | custom-call | tf_op jit(solution)/shard_map/pallas_call | solution.py:213
  122.0 0.0 reduce-scatter.2.cloned.1.call-update
  122.1 52.6 %reduce-scatter.2.cloned.1.call-done = bf16[1,256,896]{2,1,0:T(8,128)(2,1)} async-done(((bf16[8,256,896]{2,1,0:T(8,128)(2,1)}), bf16[1,256,896]{2,1,0:T(8,128)(2,1)}) %reduce-scatter.2.cloned.1.call-update) | async-done | bytes 458768 | tf_op jit(solution)/shard_map/reduce_scatter | solution.py:331
  174.6 7.4 %all-to-all-start.2 = ((bf16[32,8,896]{2,1,0:T(8,128)(2,1)}), bf16[32,8,896]{2,1,0:T(8,128)(2,1)S(1)}, u32[]{:S(2)}, u32[]{:S(2)}) async-start(bf16[32,8,896]{2,1,0:T(8,128)(2,1)} %bitcast.41), calls=%async_computation.3 | async-start | bytes 917504 | tf_op jit(solution)/shard_map/all_to_all | solution.py:309
  182.0 0.0 copy-done.15
  182.1 0.0 copy-done.17
  182.1 9.6 %shard_map.110 = (bf16[192,3584]{1,0:T(8,128)(2,1)}, bf16[192,3584]{1,0:T(8,128)(2,1)}, bf16[192,3584]{1,0:T(8,128)(2,1)}) custom-call(bf16[32,2,8,3584]{3,2,1,0:T(8,128)(2,1)} %bitcast.5.src_ref.refs_0_, bf16[32,2,8,3584]{3,2,1,0:T(8,128)(2,1)} %collective-permute-done.src_ref.refs_1_, bf16[8,2,32,3584]{3,2,1,0:T(8,128)(2,1)} %bitcast.44, ...), custom_call_target="tpu_custom_call" | custom-call | flops 16911433728 | bytes 18808832 | tf_op jit(solution)/shard_map/pallas_call | solution.py:246
  191.6 0.2 all-to-all-done.2.back_ref
  191.8 0.5 shard_map.109
  192.3 26.8 %all-gather.1 = bf16[1024,448]{1,0:T(8,128)(2,1)S(1)} all-gather(bf16[128,448]{1,0:T(8,128)(2,1)S(1)} %shard_map.109), channel_id=3, replica_groups=mesh['exp'=32,'tp'=8] {'tp'}, dimensions={0}, use_global_device_ids=true | all-gather | bytes 1032192 | tf_op jit(solution)/shard_map/all_gather | solution.py:334
  219.2 0.6 copy.16
  219.8 1.3 copy.17
  (25 shorter events, 0.0 us)
Async XLA Ops:
  7.2 1.2 copy-start.3
  8.3 1.2 copy-start.5
  9.5 0.7 copy-start.7
  10.2 0.7 copy-start.9
  10.9 10.2 %copy-start.4 = (bf16[128,3584]{1,0:T(8,128)(2,1)S(1)}, bf16[128,3584]{1,0:T(8,128)(2,1)}, u32[]{:S(2)}) copy-start(bf16[128,3584]{1,0:T(8,128)(2,1)} %act_ref.3) | copy-start | bytes 2752516
  10.9 10.2 %copy-start.6 = (bf16[128,3584]{1,0:T(8,128)(2,1)S(1)}, bf16[128,3584]{1,0:T(8,128)(2,1)}, u32[]{:S(2)}) copy-start(bf16[128,3584]{1,0:T(8,128)(2,1)} %grad_ref.3) | copy-start | bytes 2752516
  10.9 10.2 %copy-start.8 = (s32[128,2]{0,1:T(2,128)S(1)}, s32[128,2]{0,1:T(2,128)}, u32[]{:S(2)}) copy-start(s32[128,2]{0,1:T(2,128)} %param.9) | copy-start | bytes 3076
  10.9 10.2 %copy-start.10 = (f32[128,2]{0,1:T(2,128)S(1)}, f32[128,2]{0,1:T(2,128)}, u32[]{:S(2)}) copy-start(f32[128,2]{0,1:T(2,128)} %param.10) | copy-start | bytes 3076
  13.4 17.4 %all-to-all-start = ((bf16[32,2,3584]{2,1,0:T(2,128)(2,1)}), bf16[32,2,3584]{2,1,0:T(2,128)(2,1)S(1)}, u32[]{:S(2)}, u32[]{:S(2)}) async-start(bf16[32,2,3584]{2,1,0:T(2,128)(2,1)} %copy.14), calls=%async_computation | async-start | bytes 917504 | tf_op jit(solution)/shard_map/all_to_all | solution.py:309
  21.0 61.6 %all-gather.4.cloned.1.call-start = ((), (), s32[]{:S(2)}) async-start(), calls=%async_computation.5 | async-start | bytes 4128768 | tf_op jit(solution)/shard_map/all_gather | solution.py:316
  23.7 1.9 copy-start
  31.7 143.0 %reduce-scatter.2.cloned.1.call-start = ((), (), s32[]{:S(2)}) async-start(), calls=%async_computation.4 | async-start | bytes 4128768 | tf_op jit(solution)/shard_map/reduce_scatter | solution.py:331
  31.7 51.0 %copy-start.11 = (bf16[1,192,3584]{2,1,0:T(8,128)(2,1)S(1)}, bf16[1,192,3584]{2,1,0:T(8,128)(2,1)}, u32[]{:S(2)}) copy-start(bf16[1,192,3584]{2,1,0:T(8,128)(2,1)} %param.11) | copy-start | bytes 4128772
  31.7 51.0 %copy-start.12 = (bf16[1,192,3584]{2,1,0:T(8,128)(2,1)S(1)}, bf16[1,192,3584]{2,1,0:T(8,128)(2,1)}, u32[]{:S(2)}) copy-start(bf16[1,192,3584]{2,1,0:T(8,128)(2,1)} %param.12) | copy-start | bytes 4128772
  82.2 10.5 %collective-permute-start = (bf16[32,2,8,3584]{3,2,1,0:T(8,128)(2,1)}, bf16[32,2,8,3584]{3,2,1,0:T(8,128)(2,1)}, u32[]{:S(2)}, u32[]{:S(2)}) collective-permute-start(bf16[32,2,8,3584]{3,2,1,0:T(8,128)(2,1)} %bitcast.5.src_ref.refs_0_), channel_id=1, source_target_pairs={{0,8},{8,0},{16,24},{24,16},{32,40},{40,32},{48,56},{56,48},{64,72... | collective-permute-start | bytes 11010056 | tf_op jit(solution)/shard_map/ppermute | solution.py:306
  82.6 16.6 %collective-permute-start.2 = (bf16[8,2,32,3584]{3,2,1,0:T(8,128)(2,1)}, bf16[8,2,32,3584]{3,2,1,0:T(8,128)(2,1)S(1)}, u32[]{:S(2)}, u32[]{:S(2)}) collective-permute-start(bf16[8,2,32,3584]{3,2,1,0:T(8,128)(2,1)} %bitcast.42), channel_id=1, source_target_pairs={{0,8},{8,0},{16,24},{24,16},{32,40},{40,32},{48,56},{56,48},{64,72... | collective-permute-start | bytes 11010056 | tf_op jit(solution)/shard_map/ppermute | solution.py:306
  82.8 1.3 copy-start.13
  98.8 15.7 %collective-permute-start.1 = (bf16[256,3584]{1,0:T(8,128)(2,1)}, bf16[256,3584]{1,0:T(8,128)(2,1)S(1)}, u32[]{:S(2)}, u32[]{:S(2)}) collective-permute-start(bf16[256,3584]{1,0:T(8,128)(2,1)} %get-tuple-element.25), channel_id=1, source_target_pairs={{0,8},{8,0},{16,24},{24,16},{32,40},{40,32},{48,56},{56,48},{64,72... | collective-permute-start | bytes 5505032 | tf_op jit(solution)/shard_map/ppermute | solution.py:306
  99.2 1.9 copy-start.19
  107.3 6.5 %copy-start.14 = (bf16[576,256]{1,0:T(8,128)(2,1)}, bf16[576,256]{1,0:T(8,128)(2,1)S(1)}, u32[]{:S(2)}) copy-start(bf16[576,256]{1,0:T(8,128)(2,1)S(1)} %get-tuple-element.34.refs_7_) | copy-start | bytes 884740
  107.3 8.5 %copy-start.1 = (bf16[256,3584]{1,0:T(8,128)(2,1)S(1)}, bf16[256,3584]{1,0:T(8,128)(2,1)}, u32[]{:S(2)}) copy-start(bf16[256,3584]{1,0:T(8,128)(2,1)} %get-tuple-element.23.far_ref) | copy-start | bytes 5505028
  107.3 7.2 %collective-permute-start.3 = (bf16[256,3584]{1,0:T(8,128)(2,1)}, bf16[256,3584]{1,0:T(8,128)(2,1)S(1)}, u32[]{:S(2)}, u32[]{:S(2)}) collective-permute-start(bf16[256,3584]{1,0:T(8,128)(2,1)} %get-tuple-element.28), channel_id=1, source_target_pairs={{0,8},{8,0},{16,24},{24,16},{32,40},{40,32},{48,56},{56,48},{64,72... | collective-permute-start | bytes 5505032 | tf_op jit(solution)/shard_map/ppermute | solution.py:306
  113.8 0.7 copy-start.16
  114.5 1.2 copy-start.18
  115.7 1.5 copy-start.2
  122.0 60.0 %copy-start.15 = (bf16[576,256]{1,0:T(8,128)(2,1)S(1)}, bf16[576,256]{1,0:T(8,128)(2,1)}, u32[]{:S(2)}) copy-start(bf16[576,256]{1,0:T(8,128)(2,1)} %copy-done.14) | copy-start | bytes 884740
  122.0 60.0 %copy-start.17 = (bf16[576,256]{1,0:T(8,128)(2,1)S(1)}, bf16[576,256]{1,0:T(8,128)(2,1)}, u32[]{:S(2)}) copy-start(bf16[576,256]{1,0:T(8,128)(2,1)} %copy-done.16) | copy-start | bytes 884740
  174.6 17.2 %all-to-all-start.2 = ((bf16[32,8,896]{2,1,0:T(8,128)(2,1)}), bf16[32,8,896]{2,1,0:T(8,128)(2,1)S(1)}, u32[]{:S(2)}, u32[]{:S(2)}) async-start(bf16[32,8,896]{2,1,0:T(8,128)(2,1)} %bitcast.41), calls=%async_computation.3 | async-start | bytes 917504 | tf_op jit(solution)/shard_map/all_to_all | solution.py:309
Sparse Core Ops, SparseCore 0:
  31.8 50.1 all-gather.3
  122.2 52.3 reduce-scatter.1

commit v4 on v3

--- a/solution.py
+++ b/solution.py
@@ -10,7 +10,8 @@
 F32 = jnp.float32
 BF16 = jnp.bfloat16
 VMEM = pltpu.VMEM
-LIMIT = 48 * 1024 * 1024
+LIMIT = 28 * 1024 * 1024
+WHOLE = 60 * 1024 * 1024
 
 
 def table(ids, experts):
@@ -26,34 +27,50 @@
     return first, second, jnp.where(named > 0.0, rank, -1.0)
 
 
-def select(ids_ref, gate_ref, act_ref, grad_ref, slots):
+def choose(ids, gate, slots):
     experts, count, toks = slots.shape
-    first, second, rank = table(ids_ref[...], experts)
-    gate = jnp.where(first, gate_ref[0:1, :], 0.0) + jnp.where(second, gate_ref[1:2, :], 0.0)
+    first, second, rank = table(ids, experts)
+    gate = jnp.where(first, gate[0:1, :], 0.0) + jnp.where(second, gate[1:2, :], 0.0)
     hit = (rank[:, None, :] == slots.astype(F32)).reshape(experts * count, toks)
     weight = jnp.broadcast_to(gate[:, None, :], slots.shape).reshape(experts * count, toks)
     scale = jnp.sum(jnp.where(hit, weight, 0.0), axis=1, keepdims=True)
-    mask = jnp.where(hit, 1.0, 0.0).astype(BF16)
-    rows = jnp.dot(mask, act_ref[...], preferred_element_type=F32).astype(BF16)
-    picked = jnp.dot(mask, grad_ref[...], preferred_element_type=F32)
-    return rows, (picked * scale).astype(BF16)
+    return jnp.where(hit, 1.0, 0.0), scale
 
 
 def far_kernel(ids_ref, gate_ref, act_ref, grad_ref, out_ref):
     experts, count, toks = out_ref.shape[0] // 2, 2 * out_ref.shape[2], ids_ref.shape[1]
     slots = lax.broadcasted_iota(jnp.int32, (experts, count, toks), 1)
-    rows, weighted = select(ids_ref, gate_ref, act_ref, grad_ref, slots)
+    mask, scale = choose(ids_ref[...], gate_ref[...], slots)
+    mask = mask.astype(BF16)
+    rows = jnp.dot(mask, act_ref[...], preferred_element_type=F32).astype(BF16)
+    picked = jnp.dot(mask, grad_ref[...], preferred_element_type=F32)
     out_ref[:, 0] = rows.reshape(2 * experts, count // 2, -1)
-    out_ref[:, 1] = weighted.reshape(2 * experts, count // 2, -1)
-
-
-def near_kernel(half, tp_ref, ids_ref, gate_ref, act_ref, grad_ref, out_ref):
-    experts, toks = out_ref.shape[1] // 2, ids_ref.shape[1]
+    out_ref[:, 1] = (picked * scale).astype(BF16).reshape(2 * experts, count // 2, -1)
+
+
+def near_kernel(
+    half, tp_ref, ids_hbm, gate_hbm, act_hbm, grad_hbm, out_ref, ids_ref, gate_ref, act_ref, grad_ref, sems
+):
+    pairs = ((ids_hbm, ids_ref), (gate_hbm, gate_ref), (act_hbm, act_ref), (grad_hbm, grad_ref))
+    copies = [pltpu.make_async_copy(a, b, sems.at[i]) for i, (a, b) in enumerate(pairs)]
+    for copy in copies:
+        copy.start()
+    experts, toks = out_ref.shape[0], ids_ref.shape[1]
     inner = lax.broadcasted_iota(jnp.int32, (experts, 8, toks), 1)
-    slots = jnp.where(inner < 2, half + 2 * tp_ref[0] + inner, -2)
-    rows, weighted = select(ids_ref, gate_ref, act_ref, grad_ref, slots)
-    out_ref[0] = rows.reshape(experts, 8, -1)[:, :2].reshape(2 * experts, -1)
-    out_ref[1] = weighted.reshape(experts, 8, -1)[:, :2].reshape(2 * experts, -1)
+    slots = jnp.where(inner < 4, half + 2 * tp_ref[0] + inner // 2, -2)
+    copies[0].wait()
+    copies[1].wait()
+    mask, scale = choose(ids_ref[...], gate_ref[...], slots)
+    kind = (inner % 2).reshape(mask.shape)
+    of_rows = jnp.where(kind == 0, mask, 0.0).astype(BF16)
+    of_grads = jnp.where(kind == 1, mask, 0.0).astype(BF16)
+    copies[2].wait()
+    copies[3].wait()
+    rows = jnp.dot(of_rows, act_ref[...], preferred_element_type=F32)
+    picked = jnp.dot(of_grads, grad_ref[...], preferred_element_type=F32)
+    both = (rows + picked * scale).reshape(experts, 8, -1)
+    out_ref[:, 0] = both[:, 0:2].astype(BF16)
+    out_ref[:, 1] = both[:, 2:4].astype(BF16)
 
 
 def send_far(ids_t, gate_t, acts, grads, experts, half):
@@ -70,7 +87,7 @@
         ],
         out_specs=pl.BlockSpec((2 * experts, 2, half // 2, tile), lambda i: (0, 0, 0, i)),
         out_shape=jax.ShapeDtypeStruct((2 * experts, 2, half // 2, width), BF16),
-        compiler_params=pltpu.CompilerParams(vmem_limit_bytes=LIMIT),
+        compiler_params=pltpu.CompilerParams(vmem_limit_bytes=WHOLE),
         cost_estimate=pl.CostEstimate(
             flops=16 * experts * half * toks * width,
             bytes_accessed=4 * (toks + experts * half) * width,
@@ -81,20 +98,20 @@
 
 def send_near(tp_at, ids_t, gate_t, acts, grads, experts, half):
     toks, width = acts.shape
-    tile = width // 2
     return pl.pallas_call(
         functools.partial(near_kernel, half),
-        grid=(width // tile,),
-        in_specs=[
-            pl.BlockSpec(memory_space=pltpu.SMEM),
-            pl.BlockSpec((2, toks), lambda i: (0, 0)),
-            pl.BlockSpec((2, toks), lambda i: (0, 0)),
-            pl.BlockSpec((toks, tile), lambda i: (0, i)),
-            pl.BlockSpec((toks, tile), lambda i: (0, i)),
-        ],
-        out_specs=pl.BlockSpec((2, 2 * experts, tile), lambda i: (0, 0, i)),
-        out_shape=jax.ShapeDtypeStruct((2, 2 * experts, width), BF16),
-        compiler_params=pltpu.CompilerParams(vmem_limit_bytes=LIMIT),
+        in_specs=[pl.BlockSpec(memory_space=pltpu.SMEM)]
+        + [pl.BlockSpec(memory_space=pltpu.HBM)] * 4,
+        out_specs=pl.BlockSpec(memory_space=VMEM),
+        out_shape=jax.ShapeDtypeStruct((experts, 2, 2, width), BF16),
+        scratch_shapes=[
+            VMEM((2, toks), ids_t.dtype),
+            VMEM((2, toks), gate_t.dtype),
+            VMEM((toks, width), acts.dtype),
+            VMEM((toks, width), grads.dtype),
+            pltpu.SemaphoreType.DMA((4,)),
+        ],
+        compiler_params=pltpu.CompilerParams(vmem_limit_bytes=WHOLE),
     )(tp_at, ids_t, gate_t, acts, grads)
 
 
@@ -157,7 +174,7 @@
     outer, _, inner, width = src.shape
     rows = outer * inner
     units = down_w.shape[0]
-    steps = 2
+    steps = 1
     tile = width // steps
     last = steps - 1
 
@@ -215,7 +232,7 @@
         grid=(steps,),
         in_specs=[spec] * 4,
         out_specs=pl.BlockSpec((2, rows, 2 * width // pieces), lambda i: (i, 0, 0)),
-        out_shape=jax.ShapeDtypeStruct((pieces, rows, 2 * width // pieces), BF16),
+        out_shape=pltpu.HBM((pieces, rows, 2 * width // pieces), BF16),
         compiler_params=pltpu.CompilerParams(vmem_limit_bytes=LIMIT),
     )(far, far_more, near, near_more)
 
@@ -309,7 +326,7 @@
         return lax.all_to_all(v, "exp", split_axis=0, concat_axis=0, tiled=True)
 
     near = send_near(tp_at, ids_t, gate_t, activations, out_grad, experts, half)
-    near = spread(jnp.transpose(near, (1, 0, 2)))
+    near = spread(near.reshape(devices, 2, width))
     far = send_far(ids_t, gate_t, activations, out_grad, experts, half)
     near, far = lax.optimization_barrier((near, far))
     near = jnp.transpose(near, (1, 0, 2))
@@ -328,15 +345,17 @@
     near, near_other_part = lax.optimization_barrier((near, near_other_part))
     near_part, near_side = expert_part(near, *weights, True)
     both = merge(far_part, far_sent, near_part, near_sent, planes)
+    both, far = lax.optimization_barrier((both, far))
+    gate_g, up_g, down_g = weight_grads(
+        [far, far_other, near, near_other],
+        [far_side, far_other_side, near_side, near_other_side],
+    )
     mine = lax.psum_scatter(both, "tp", scatter_dimension=0, tiled=False)
+    mine, gate_g, up_g, down_g = lax.optimization_barrier((mine, gate_g, up_g, down_g))
     returned = spread(mine.reshape(devices, half // 2, -1))
     piece = combine(ids_t, returned, half)
     gathered = lax.all_gather(piece, "tp", axis=0, tiled=False)
     in_grad = jnp.transpose(gathered, (1, 0, 2)).reshape(toks, width)
-    gate_g, up_g, down_g = weight_grads(
-        [far, far_other, near, near_other],
-        [far_side, far_other_side, near_side, near_other_side],
-    )
     return (in_grad, gate_g[None], up_g[None], down_g[None])
 
 

time: 229 us -> 213 us (0.930)
  blocking collectives: 77.3 us -> 94.5 us
  waiting for transfers between devices: 60.6 us -> 47.3 us
  starting transfers between devices: 16.1 us -> 8.83 us
  Pallas kernels: 43.4 us -> 36.6 us
  local copies, waits for them, and re-layouts: 16.3 us -> 10.6 us
    all_to_all x1 -> x2, blocking collectives: 50.5 us -> 67.7 us  [spread(): return lax.all_to_all(v, 'exp', split_axis=0, concat_axis=0, tiled=True)]
    reduce_scatter x1, waiting for transfers between devices: 52.6 us -> 39.2 us  [per_device(): mine = lax.psum_scatter(both, 'tp', scatter_dimension=0, tiled=False)]
    pallas_call x4, Pallas kernels: 24.8 us -> 16.5 us  [expert_part(): pl.pallas_call(functools.partial(expert_kernel, turn), grid=(2, steps), i...]
    all_to_all x2 -> x1, starting transfers between devices: 15 us -> 7.63 us  [spread(): return lax.all_to_all(v, 'exp', split_axis=0, concat_axis=0, tiled=True)]
    unnamed x41 -> x27, local copies, waits for them, and re-layouts: 13.6 us -> 9.16 us
    pallas_call x1, Pallas kernels: 2.53 us -> 5.18 us  [send_far(): pl.pallas_call(far_kernel, grid=(width // tile,), in_specs=[pl.BlockSpec(...]
    all_to_all x2 -> x1, waiting for transfers between devices: 5.46 us -> 4.57 us  [spread(): return lax.all_to_all(v, 'exp', split_axis=0, concat_axis=0, tiled=True)]
  transfers between devices with their start and end apart: 8 -> 7, of which waited for: 4 -> 3; matrix products, arithmetic and copies ran while one was open for 0% -> 0% of each run, Pallas kernels for 16% -> 14%
where the time goes in v4:
time: 213 us; the launch traced here: 212 us
  blocking collectives  94.5 us (44%)
  waiting for transfers between devices  47.3 us (22%)
  Pallas kernels  36.6 us (17%)
  between operations  14.2 us (7%)
  local copies, waits for them, and re-layouts  10.6 us (5%)
  starting transfers between devices  8.83 us (4%)
    all_to_all x2, blocking collectives, spread(): return lax.all_to_all(v, 'exp', split_axis=0, concat_axis=0, tiled=True)  67.7 us
    reduce_scatter x1, waiting for transfers between devices, per_device(): mine = lax.psum_scatter(both, 'tp', scatter_dimension=0, tiled=False)  39.2 us
    all_gather x1, blocking collectives, per_device(): gathered = lax.all_gather(piece, 'tp', axis=0, tiled=False)  26.8 us
    pallas_call x4, Pallas kernels, expert_part(): pl.pallas_call(functools.partial(expert_kernel, turn), grid=(2, steps), i...  16.5 us
    unnamed x27, local copies, waits for them, and re-layouts  9.16 us
    pallas_call x1, Pallas kernels, weight_grads(): pl.pallas_call(functools.partial(weight_kernel, len(sources)), grid=(widt...  8.16 us
    all_to_all x1, starting transfers between devices, spread(): return lax.all_to_all(v, 'exp', split_axis=0, concat_axis=0, tiled=True)  7.63 us
    pallas_call x1, Pallas kernels, send_far(): pl.pallas_call(far_kernel, grid=(width // tile,), in_specs=[pl.BlockSpec(...  5.18 us
  transfers between devices with their start and end apart: 7, of which 3 were waited for; matrix products, arithmetic and copies ran while one was open for 0% of the time, Pallas kernels for 14%

profile of v4, /device:TPU:2, one launch (start us, length us, event | category | flops | bytes accessed | tf_op | source)
XLA Modules:
  0.0 212.1 jit_solution(13377211513461210715)
XLA Ops:
  7.2 3.0 %shard_map.102 = bf16[16,2,2,3584]{3,2,1,0:T(2,128)(2,1)} custom-call(s32[1]{0:T(128)} %bitcast.1.tp_ref, s32[2,128]{1,0:T(2,128)} %bitcast.20, f32[2,128]{1,0:T(2,128)} %bitcast.44, bf16[128,3584]{1,0:T(8,128)(2,1)} %act_ref.1, bf16[128,3584]{1,0:T(8,128)(2,1)} %grad_ref.1), custom_call_target="tpu_custom_call" | custom-call | tf_op jit(solution)/shard_map/pallas_call | solution.py:101
  10.2 7.6 %all-to-all-start = ((bf16[32,2,3584]{2,1,0:T(2,128)(2,1)}), bf16[32,2,3584]{2,1,0:T(2,128)(2,1)S(1)}, u32[]{:S(2)}, u32[]{:S(2)}) async-start(bf16[32,2,3584]{2,1,0:T(2,128)(2,1)} %bitcast.42), calls=%async_computation | async-start | bytes 917504 | tf_op jit(solution)/shard_map/all_to_all | solution.py:326
  17.8 0.0 all-gather.4.cloned.1.call-start
  17.9 5.2 %shard_map.103 = bf16[32,2,8,3584]{3,2,1,0:T(8,128)(2,1)} custom-call(s32[2,128]{1,0:T(2,128)} %bitcast.21, f32[2,128]{1,0:T(2,128)} %bitcast.45, bf16[128,3584]{1,0:T(8,128)(2,1)} %act_ref.1, bf16[128,3584]{1,0:T(8,128)(2,1)} %grad_ref.1), custom_call_target="tpu_custom_call" | custom-call | flops 1879048192 | bytes 5505024 | tf_op jit(solution)/shard_map/pallas_call | solution.py:79
  23.0 4.6 %all-to-all-done = bf16[32,2,3584]{2,1,0:T(2,128)(2,1)S(1)} async-done(((bf16[32,2,3584]{2,1,0:T(2,128)(2,1)}), bf16[32,2,3584]{2,1,0:T(2,128)(2,1)S(1)}, u32[]{:S(2)}, u32[]{:S(2)}) %all-to-all-start) | async-done | bytes 458784 | tf_op jit(solution)/shard_map/all_to_all | solution.py:326
  27.6 0.8 copy.16
  28.4 0.0 all-gather.4.cloned.1.call-update
  28.4 0.0 reduce-scatter.2.cloned.1.call-start
  28.5 0.0 copy-start.5
  28.5 0.0 copy-start.6
  28.5 50.5 %all_to_all.15 = bf16[32,16,3584]{2,1,0:T(8,128)(2,1)} all-to-all(bf16[32,16,3584]{2,1,0:T(8,128)(2,1)} %bitcast.39), channel_id=1, replica_groups=mesh['exp'=32,'tp'=8] {'exp'}, dimensions={0} | all-to-all | bytes 7340032 | tf_op jit(solution)/shard_map/all_to_all | solution.py:326
  79.0 0.4 collective-permute-start
  79.4 0.1 collective-permute-start.2
  79.5 0.0 copy-done.5
  79.5 0.0 copy-done.6
  79.5 1.3 copy-done.7
  80.9 5.1 %shard_map.104 = (bf16[256,3584]{1,0:T(8,128)(2,1)S(1)}, bf16[576,256]{1,0:T(8,128)(2,1)S(1)}) custom-call(bf16[32,2,8,3584]{3,2,1,0:T(8,128)(2,1)} %bitcast.5.src_ref.refs_0_, bf16[192,3584]{1,0:T(8,128)(2,1)S(1)} %bitcast.26, bf16[192,3584]{1,0:T(8,128)(2,1)S(1)} %bitcast.30, bf16[192,3584]{1,0:T(8,128)(2,1)S(1)} %bitcast.34), custom_call_target="tpu_custom_call" | custom-call | flops 7046430720 | bytes 9633792 | tf_op jit(solution)/shard_map/pallas_call | solution.py:185
  86.0 3.5 %collective-permute-done.src_ref.refs_1_ = bf16[32,2,8,3584]{3,2,1,0:T(8,128)(2,1)} collective-permute-done((bf16[32,2,8,3584]{3,2,1,0:T(8,128)(2,1)}, bf16[32,2,8,3584]{3,2,1,0:T(8,128)(2,1)}, u32[]{:S(2)}, u32[]{:S(2)}) %collective-permute-start) | collective-permute-done | bytes 3670048 | tf_op jit(solution)/shard_map/ppermute | solution.py:323
  89.5 5.1 %shard_map.105 = (bf16[256,3584]{1,0:T(8,128)(2,1)S(1)}, bf16[576,256]{1,0:T(8,128)(2,1)S(1)}) custom-call(bf16[32,2,8,3584]{3,2,1,0:T(8,128)(2,1)} %collective-permute-done.src_ref.refs_1_, bf16[192,3584]{1,0:T(8,128)(2,1)S(1)} %bitcast.27, bf16[192,3584]{1,0:T(8,128)(2,1)S(1)} %bitcast.31, bf16[192,3584]{1,0:T(8,128)(2,1)S(1)} %bitcast.35), custom_call_target="tpu_custom_call" | custom-call | flops 7046430720 | bytes 9633792 | tf_op jit(solution)/shard_map/pallas_call | solution.py:185
  94.6 0.0 copy-start.1
  94.6 0.0 copy-start.8
  94.6 0.5 collective-permute-start.1
  95.1 0.0 collective-permute-done.2.src_ref.refs_3_
  95.1 3.1 %shard_map.106 = (bf16[256,3584]{1,0:T(8,128)(2,1)S(1)}, bf16[576,256]{1,0:T(8,128)(2,1)S(1)}) custom-call(bf16[8,2,32,3584]{3,2,1,0:T(8,128)(2,1)S(1)} %collective-permute-done.2.src_ref.refs_3_, bf16[192,3584]{1,0:T(8,128)(2,1)S(1)} %bitcast.28, bf16[192,3584]{1,0:T(8,128)(2,1)S(1)} %bitcast.32, bf16[192,3584]{1,0:T(8,128)(2,1)S(1)} %bitcast.36), custom_call_target="tpu_custom_call" | custom-call | flops 7046430720 | bytes 9633792 | tf_op jit(solution)/shard_map/pallas_call | solution.py:185
  98.3 0.0 copy-done.3
  98.3 0.0 copy-start.9
  98.3 0.7 copy-done.9
  99.0 0.1 collective-permute-start.3
  99.1 0.0 copy-done.1
  99.1 3.1 %shard_map.107 = (bf16[256,3584]{1,0:T(8,128)(2,1)S(1)}, bf16[576,256]{1,0:T(8,128)(2,1)S(1)}) custom-call(bf16[8,2,32,3584]{3,2,1,0:T(8,128)(2,1)S(1)} %bitcast.24, bf16[192,3584]{1,0:T(8,128)(2,1)S(1)} %bitcast.29, bf16[192,3584]{1,0:T(8,128)(2,1)S(1)} %bitcast.33, bf16[192,3584]{1,0:T(8,128)(2,1)S(1)} %bitcast.37), custom_call_target="tpu_custom_call" | custom-call | flops 7046430720 | bytes 9633792 | tf_op jit(solution)/shard_map/pallas_call | solution.py:185
  102.3 0.0 copy-start.11
  102.3 0.7 copy-done.11
  103.0 0.0 collective-permute-done.1.far_more_ref
  103.0 0.0 collective-permute-done.3.near_more_ref
  103.0 3.3 %shard_map.108 = bf16[8,256,896]{2,1,0:T(8,128)(2,1)} custom-call(bf16[256,3584]{1,0:T(8,128)(2,1)S(1)} %get-tuple-element.29.far_ref, bf16[256,3584]{1,0:T(8,128)(2,1)S(1)} %collective-permute-done.1.far_more_ref, bf16[256,3584]{1,0:T(8,128)(2,1)S(1)} %get-tuple-element.36.near_ref, bf16[256,3584]{1,0:T(8,128)(2,1)S(1)} %collective-permute-done.3.near_more_ref), custom_call_target="tpu_custom_call" | custom-call | tf_op jit(solution)/shard_map/pallas_call | solution.py:230
  106.3 0.0 reduce-scatter.2.cloned.1.call-update
  106.3 0.9 copy-done.10
  107.3 0.1 copy-done.12
  107.3 2.0 copy-done.2
  109.4 2.0 copy-done.4
  111.4 8.2 %shard_map.109 = (bf16[192,3584]{1,0:T(8,128)(2,1)}, bf16[192,3584]{1,0:T(8,128)(2,1)}, bf16[192,3584]{1,0:T(8,128)(2,1)}) custom-call(bf16[32,2,8,3584]{3,2,1,0:T(8,128)(2,1)} %bitcast.5.src_ref.refs_0_, bf16[32,2,8,3584]{3,2,1,0:T(8,128)(2,1)} %collective-permute-done.src_ref.refs_1_, bf16[8,2,32,3584]{3,2,1,0:T(8,128)(2,1)S(1)} %bitcast.25, ...), custom_call_target="tpu_custom_call" | custom-call | flops 16911433728 | bytes 18808832 | tf_op jit(solution)/shard_map/pallas_call | solution.py:263
  119.6 39.2 %reduce-scatter.2.cloned.1.call-done = bf16[1,256,896]{2,1,0:T(8,128)(2,1)} async-done(((bf16[8,256,896]{2,1,0:T(8,128)(2,1)}), bf16[1,256,896]{2,1,0:T(8,128)(2,1)}) %reduce-scatter.2.cloned.1.call-update) | async-done | bytes 458768 | tf_op jit(solution)/shard_map/reduce_scatter | solution.py:353
  158.8 17.2 %all_to_all.16.back_ref = bf16[32,8,896]{2,1,0:T(8,128)(2,1)S(1)} all-to-all(bf16[32,8,896]{2,1,0:T(8,128)(2,1)} %bitcast.43), channel_id=1, replica_groups=mesh['exp'=32,'tp'=8] {'exp'}, dimensions={0} | all-to-all | bytes 917504 | tf_op jit(solution)/shard_map/all_to_all | solution.py:326
  176.0 0.0 copy-done
  176.0 0.5 shard_map.110
  176.5 26.8 %all-gather.1 = bf16[1024,448]{1,0:T(8,128)(2,1)S(1)} all-gather(bf16[128,448]{1,0:T(8,128)(2,1)S(1)} %shard_map.110), channel_id=3, replica_groups=mesh['exp'=32,'tp'=8] {'tp'}, dimensions={0}, use_global_device_ids=true | all-gather | bytes 1032192 | tf_op jit(solution)/shard_map/all_gather | solution.py:357
  203.3 0.6 copy.17
  204.0 1.3 copy.18
  (9 shorter events, 0.0 us)
Async XLA Ops:
  10.2 17.4 %all-to-all-start = ((bf16[32,2,3584]{2,1,0:T(2,128)(2,1)}), bf16[32,2,3584]{2,1,0:T(2,128)(2,1)S(1)}, u32[]{:S(2)}, u32[]{:S(2)}) async-start(bf16[32,2,3584]{2,1,0:T(2,128)(2,1)} %bitcast.42), calls=%async_computation | async-start | bytes 917504 | tf_op jit(solution)/shard_map/all_to_all | solution.py:326
  17.8 61.6 %all-gather.4.cloned.1.call-start = ((), (), s32[]{:S(2)}) async-start(), calls=%async_computation.5 | async-start | bytes 4128768 | tf_op jit(solution)/shard_map/all_gather | solution.py:333
  28.4 130.4 %reduce-scatter.2.cloned.1.call-start = ((), (), s32[]{:S(2)}) async-start(), calls=%async_computation.4 | async-start | bytes 4128768 | tf_op jit(solution)/shard_map/reduce_scatter | solution.py:353
  28.5 51.1 %copy-start.5 = (bf16[1,192,3584]{2,1,0:T(8,128)(2,1)S(1)}, bf16[1,192,3584]{2,1,0:T(8,128)(2,1)}, u32[]{:S(2)}) copy-start(bf16[1,192,3584]{2,1,0:T(8,128)(2,1)} %param.11) | copy-start | bytes 4128772
  28.5 51.0 %copy-start.6 = (bf16[1,192,3584]{2,1,0:T(8,128)(2,1)S(1)}, bf16[1,192,3584]{2,1,0:T(8,128)(2,1)}, u32[]{:S(2)}) copy-start(bf16[1,192,3584]{2,1,0:T(8,128)(2,1)} %param.12) | copy-start | bytes 4128772
  79.0 10.5 %collective-permute-start = (bf16[32,2,8,3584]{3,2,1,0:T(8,128)(2,1)}, bf16[32,2,8,3584]{3,2,1,0:T(8,128)(2,1)}, u32[]{:S(2)}, u32[]{:S(2)}) collective-permute-start(bf16[32,2,8,3584]{3,2,1,0:T(8,128)(2,1)} %bitcast.5.src_ref.refs_0_), channel_id=1, source_target_pairs={{0,8},{8,0},{16,24},{24,16},{32,40},{40,32},{48,56},{56,48},{64,72... | collective-permute-start | bytes 11010056 | tf_op jit(solution)/shard_map/ppermute | solution.py:323
  79.4 15.7 %collective-permute-start.2 = (bf16[8,2,32,3584]{3,2,1,0:T(8,128)(2,1)}, bf16[8,2,32,3584]{3,2,1,0:T(8,128)(2,1)S(1)}, u32[]{:S(2)}, u32[]{:S(2)}) collective-permute-start(bf16[8,2,32,3584]{3,2,1,0:T(8,128)(2,1)} %bitcast.23), channel_id=1, source_target_pairs={{0,8},{8,0},{16,24},{24,16},{32,40},{40,32},{48,56},{56,48},{64,72... | collective-permute-start | bytes 11010056 | tf_op jit(solution)/shard_map/ppermute | solution.py:323
  79.5 1.3 copy-start.7
  94.6 4.5 %copy-start.1 = (bf16[16,32,3584]{2,1,0:T(8,128)(2,1)S(1)}, bf16[16,32,3584]{2,1,0:T(8,128)(2,1)}, u32[]{:S(2)}) copy-start(bf16[16,32,3584]{2,1,0:T(8,128)(2,1)} %all-gather.4.cloned.1.call-done) | copy-start | bytes 11010052
  94.6 4.5 %copy-start.8 = (bf16[1,192,3584]{2,1,0:T(8,128)(2,1)S(1)}, bf16[1,192,3584]{2,1,0:T(8,128)(2,1)}, u32[]{:S(2)}) copy-start(bf16[1,192,3584]{2,1,0:T(8,128)(2,1)} %param.13) | copy-start | bytes 4128772
  94.6 8.4 %collective-permute-start.1 = (bf16[256,3584]{1,0:T(8,128)(2,1)S(1)}, bf16[256,3584]{1,0:T(8,128)(2,1)S(1)}, u32[]{:S(2)}, u32[]{:S(2)}) collective-permute-start(bf16[256,3584]{1,0:T(8,128)(2,1)S(1)} %get-tuple-element.31), channel_id=1, source_target_pairs={{0,8},{8,0},{16,24},{24,16},{32,40},{40,32},{48,56},{56,48},{64,72... | collective-permute-start | bytes 5505032 | tf_op jit(solution)/shard_map/ppermute | solution.py:323
  95.1 3.2 %copy-start.3 = (bf16[8,2,32,3584]{3,2,1,0:T(8,128)(2,1)}, bf16[8,2,32,3584]{3,2,1,0:T(8,128)(2,1)S(1)}, u32[]{:S(2)}) copy-start(bf16[8,2,32,3584]{3,2,1,0:T(8,128)(2,1)S(1)} %collective-permute-done.2.src_ref.refs_3_) | copy-start | bytes 11010052
  98.3 0.7 copy-start.9
  99.0 4.0 %collective-permute-start.3 = (bf16[256,3584]{1,0:T(8,128)(2,1)S(1)}, bf16[256,3584]{1,0:T(8,128)(2,1)S(1)}, u32[]{:S(2)}, u32[]{:S(2)}) collective-permute-start(bf16[256,3584]{1,0:T(8,128)(2,1)S(1)} %get-tuple-element.34), channel_id=1, source_target_pairs={{0,8},{8,0},{16,24},{24,16},{32,40},{40,32},{48,56},{56,48},{64,72... | collective-permute-start | bytes 5505032 | tf_op jit(solution)/shard_map/ppermute | solution.py:323
  102.3 0.7 copy-start.11
  106.3 1.0 copy-start.10
  106.3 1.0 copy-start.12
  107.3 2.0 copy-start.2
  109.4 2.0 copy-start.4
  111.4 64.6 %copy-start = (s32[128,2]{0,1:T(2,128)S(1)}, s32[128,2]{0,1:T(2,128)}, u32[]{:S(2)}) copy-start(s32[128,2]{0,1:T(2,128)} %param.9) | copy-start | bytes 3076
Sparse Core Ops, SparseCore 0:
  28.6 50.1 all-gather.3
  106.4 52.3 reduce-scatter.1

commit v5 on v4

--- a/solution.py
+++ b/solution.py
@@ -38,14 +38,15 @@
 
 
 def far_kernel(ids_ref, gate_ref, act_ref, grad_ref, out_ref):
-    experts, count, toks = out_ref.shape[0] // 2, 2 * out_ref.shape[2], ids_ref.shape[1]
+    experts, _, count, tile = out_ref.shape
+    toks = ids_ref.shape[1]
     slots = lax.broadcasted_iota(jnp.int32, (experts, count, toks), 1)
     mask, scale = choose(ids_ref[...], gate_ref[...], slots)
     mask = mask.astype(BF16)
     rows = jnp.dot(mask, act_ref[...], preferred_element_type=F32).astype(BF16)
     picked = jnp.dot(mask, grad_ref[...], preferred_element_type=F32)
-    out_ref[:, 0] = rows.reshape(2 * experts, count // 2, -1)
-    out_ref[:, 1] = (picked * scale).astype(BF16).reshape(2 * experts, count // 2, -1)
+    out_ref[:, 0] = rows.reshape(experts, count, tile)
+    out_ref[:, 1] = (picked * scale).astype(BF16).reshape(experts, count, tile)
 
 
 def near_kernel(
@@ -57,11 +58,11 @@
         copy.start()
     experts, toks = out_ref.shape[0], ids_ref.shape[1]
     inner = lax.broadcasted_iota(jnp.int32, (experts, 8, toks), 1)
-    slots = jnp.where(inner < 4, half + 2 * tp_ref[0] + inner // 2, -2)
+    slots = jnp.where(inner < 4, half + 2 * tp_ref[0] + inner % 2, -2)
     copies[0].wait()
     copies[1].wait()
     mask, scale = choose(ids_ref[...], gate_ref[...], slots)
-    kind = (inner % 2).reshape(mask.shape)
+    kind = (inner // 2).reshape(mask.shape)
     of_rows = jnp.where(kind == 0, mask, 0.0).astype(BF16)
     of_grads = jnp.where(kind == 1, mask, 0.0).astype(BF16)
     copies[2].wait()
@@ -69,8 +70,7 @@
     rows = jnp.dot(of_rows, act_ref[...], preferred_element_type=F32)
     picked = jnp.dot(of_grads, grad_ref[...], preferred_element_type=F32)
     both = (rows + picked * scale).reshape(experts, 8, -1)
-    out_ref[:, 0] = both[:, 0:2].astype(BF16)
-    out_ref[:, 1] = both[:, 2:4].astype(BF16)
+    out_ref[...] = both[:, :4].astype(BF16)
 
 
 def send_far(ids_t, gate_t, acts, grads, experts, half):
@@ -85,8 +85,8 @@
             pl.BlockSpec((toks, tile), lambda i: (0, i)),
             pl.BlockSpec((toks, tile), lambda i: (0, i)),
         ],
-        out_specs=pl.BlockSpec((2 * experts, 2, half // 2, tile), lambda i: (0, 0, 0, i)),
-        out_shape=jax.ShapeDtypeStruct((2 * experts, 2, half // 2, width), BF16),
+        out_specs=pl.BlockSpec((experts, 2, half, tile), lambda i: (0, 0, 0, i)),
+        out_shape=jax.ShapeDtypeStruct((experts, 2, half, width), BF16),
         compiler_params=pltpu.CompilerParams(vmem_limit_bytes=WHOLE),
         cost_estimate=pl.CostEstimate(
             flops=16 * experts * half * toks * width,
@@ -103,7 +103,7 @@
         in_specs=[pl.BlockSpec(memory_space=pltpu.SMEM)]
         + [pl.BlockSpec(memory_space=pltpu.HBM)] * 4,
         out_specs=pl.BlockSpec(memory_space=VMEM),
-        out_shape=jax.ShapeDtypeStruct((experts, 2, 2, width), BF16),
+        out_shape=jax.ShapeDtypeStruct((experts, 4, width), BF16),
         scratch_shapes=[
             VMEM((2, toks), ids_t.dtype),
             VMEM((2, toks), gate_t.dtype),
@@ -113,6 +113,26 @@
         ],
         compiler_params=pltpu.CompilerParams(vmem_limit_bytes=WHOLE),
     )(tp_at, ids_t, gate_t, acts, grads)
+
+
+def sort_kernel(in_ref, out_ref):
+    every = in_ref[...].astype(F32)
+    for kind in range(2):
+        some = every[:, 2 * kind : 2 * kind + 2].reshape(out_ref.shape[1], -1)
+        out_ref[kind] = some.astype(BF16)
+
+
+def sort_kinds(near):
+    chips, _, width = near.shape
+    tile = width // 2
+    return pl.pallas_call(
+        sort_kernel,
+        grid=(width // tile,),
+        in_specs=[pl.BlockSpec((chips, 4, tile), lambda i: (0, 0, i))],
+        out_specs=pl.BlockSpec((2, 2 * chips, tile), lambda i: (0, 0, i)),
+        out_shape=pltpu.HBM((2, 2 * chips, width), BF16),
+        compiler_params=pltpu.CompilerParams(vmem_limit_bytes=LIMIT),
+    )(near)
 
 
 def expert_kernel(
@@ -161,7 +181,9 @@
         if turn:
             to = lax.broadcasted_iota(jnp.int32, (rows, rows), 0)
             of = lax.broadcasted_iota(jnp.int32, (rows, rows), 1)
-            moved = jnp.where(of == (to % outer) * inner + to // outer, 1.0, 0.0).astype(BF16)
+            chip, place = to // (2 * outer), to % (2 * outer)
+            moved = of == (place // 2) * inner + 2 * chip + place % 2
+            moved = jnp.where(moved, 1.0, 0.0).astype(BF16)
             dgu_ref[...] = jnp.dot(moved, dgu_ref[...], preferred_element_type=F32).astype(BF16)
 
     @pl.when(phase == 1)
@@ -278,16 +300,15 @@
     )(*sources, *sides)
 
 
-def combine_kernel(half, ids_ref, back_ref, out_ref):
-    experts, per_core = back_ref.shape[0] // 2, back_ref.shape[1]
+def combine_kernel(ids_ref, back_ref, out_ref):
+    experts, half = back_ref.shape[0], back_ref.shape[1]
     toks = ids_ref.shape[1]
     wide = out_ref.shape[1]
     _, _, rank = table(ids_ref[...], experts)
-    row = lax.broadcasted_iota(jnp.int32, (experts, 2 * per_core, toks), 1)
-    late = half + 2 * (row % per_core) + row // per_core
-    rows = back_ref[...].reshape(2 * experts * per_core, 2 * wide)
-    total = gather_slots(rank, row.astype(F32), rows)[:, :wide]
-    total += gather_slots(rank, late.astype(F32), rows)[:, wide:]
+    slots = lax.broadcasted_iota(jnp.int32, (experts, half, toks), 1)
+    rows = back_ref[...].reshape(experts * half, 2 * wide)
+    total = gather_slots(rank, slots.astype(F32), rows)[:, :wide]
+    total += gather_slots(rank, (slots + half).astype(F32), rows)[:, wide:]
     out_ref[...] = total.astype(BF16)
 
 
@@ -296,10 +317,10 @@
     return lax.dot_general(hit, rows, (((0,), (0,)), ((), ())), preferred_element_type=F32)
 
 
-def combine(ids_t, returned, half):
+def combine(ids_t, returned):
     toks = ids_t.shape[1]
     return pl.pallas_call(
-        functools.partial(combine_kernel, half),
+        combine_kernel,
         in_specs=[pl.BlockSpec(memory_space=VMEM)] * 2,
         out_specs=pl.BlockSpec(memory_space=VMEM),
         out_shape=jax.ShapeDtypeStruct((toks, returned.shape[2] // 2), BF16),
@@ -322,28 +343,32 @@
     def trade(v):
         return lax.ppermute(v, "exp", swap)
 
+    sides = [list(range(core, devices, 2)) for core in range(2)]
+
     def spread(v):
-        return lax.all_to_all(v, "exp", split_axis=0, concat_axis=0, tiled=True)
+        return lax.all_to_all(
+            v, "exp", split_axis=0, concat_axis=0, tiled=True, axis_index_groups=sides
+        )
 
     near = send_near(tp_at, ids_t, gate_t, activations, out_grad, experts, half)
-    near = spread(near.reshape(devices, 2, width))
+    near = spread(near)
     far = send_far(ids_t, gate_t, activations, out_grad, experts, half)
     near, far = lax.optimization_barrier((near, far))
-    near = jnp.transpose(near, (1, 0, 2))
+    near = sort_kinds(near)
     near = lax.all_gather(near, "tp", axis=0, tiled=False)
-    far = spread(far.reshape(devices, half, width)).reshape(far.shape)
+    far = spread(far.reshape(experts, 2 * half, width)).reshape(far.shape)
     weights = (gate_proj[0], up_proj[0], down_proj[0])
     far_other = trade(far)
     near_other = trade(near)
     far_part, far_side = expert_part(far, *weights, False)
-    far_other, far_part = lax.optimization_barrier((far_other, far_part))
+    near, far_part = lax.optimization_barrier((near, far_part))
+    near_part, near_side = expert_part(near, *weights, True)
+    far_other, near_part = lax.optimization_barrier((far_other, near_part))
     far_other_part, far_other_side = expert_part(far_other, *weights, False)
     far_sent = trade(far_other_part)
     near_other, far_other_part = lax.optimization_barrier((near_other, far_other_part))
     near_other_part, near_other_side = expert_part(near_other, *weights, True)
     near_sent = trade(near_other_part)
-    near, near_other_part = lax.optimization_barrier((near, near_other_part))
-    near_part, near_side = expert_part(near, *weights, True)
     both = merge(far_part, far_sent, near_part, near_sent, planes)
     both, far = lax.optimization_barrier((both, far))
     gate_g, up_g, down_g = weight_grads(
@@ -352,8 +377,8 @@
     )
     mine = lax.psum_scatter(both, "tp", scatter_dimension=0, tiled=False)
     mine, gate_g, up_g, down_g = lax.optimization_barrier((mine, gate_g, up_g, down_g))
-    returned = spread(mine.reshape(devices, half // 2, -1))
-    piece = combine(ids_t, returned, half)
+    returned = spread(mine.reshape(experts, half, -1))
+    piece = combine(ids_t, returned)
     gathered = lax.all_gather(piece, "tp", axis=0, tiled=False)
     in_grad = jnp.transpose(gathered, (1, 0, 2)).reshape(toks, width)
     return (in_grad, gate_g[None], up_g[None], down_g[None])

time: 213 us -> 210 us (0.986)
  transfers between devices with their start and end apart: 7 -> 7, of which waited for: 3 -> 4; matrix products, arithmetic and copies ran while one was open for 0% -> 0% of each run, Pallas kernels for 14% -> 14%
where the time goes in v5:
time: 210 us
  blocking collectives  93.3 us (44%)
  waiting for transfers between devices  46.6 us (22%)
  Pallas kernels  37.8 us (18%)
  between operations  14.2 us (7%)
  local copies, waits for them, and re-layouts  9.77 us (5%)
  starting transfers between devices  8.1 us (4%)
    all_to_all x2, blocking collectives, spread(): lax.all_to_all(v, 'exp', split_axis=0, concat_axis=0, tiled=True, axis_in...  66.2 us
    reduce_scatter x1, waiting for transfers between devices, per_device(): mine = lax.psum_scatter(both, 'tp', scatter_dimension=0, tiled=False)  38.1 us
    all_gather x1, blocking collectives, per_device(): gathered = lax.all_gather(piece, 'tp', axis=0, tiled=False)  27.1 us
    pallas_call x4, Pallas kernels, expert_part(): pl.pallas_call(functools.partial(expert_kernel, turn), grid=(2, steps), i...  16.8 us
    unnamed x27, local copies, waits for them, and re-layouts  9.16 us
    pallas_call x1, Pallas kernels, weight_grads(): pl.pallas_call(functools.partial(weight_kernel, len(sources)), grid=(widt...  8.14 us
    all_to_all x1, starting transfers between devices, spread(): lax.all_to_all(v, 'exp', split_axis=0, concat_axis=0, tiled=True, axis_in...  7.49 us
    pallas_call x1, Pallas kernels, send_far(): pl.pallas_call(far_kernel, grid=(width // tile,), in_specs=[pl.BlockSpec(...  5.18 us
  transfers between devices with their start and end apart: 7, of which 4 were waited for; matrix products, arithmetic and copies ran while one was open for 0% of the time, Pallas kernels for 14%

profile of v5, /device:TPU:2, one launch (start us, length us, event | category | flops | bytes accessed | tf_op | source)
XLA Modules:
  0.0 209.7 jit_solution(3906971874321741111)
XLA Ops:
  7.2 2.9 %shard_map.102 = bf16[16,4,3584]{2,1,0:T(4,128)(2,1)} custom-call(s32[1]{0:T(128)} %bitcast.1.tp_ref, s32[2,128]{1,0:T(2,128)} %bitcast.18, f32[2,128]{1,0:T(2,128)} %bitcast.40, bf16[128,3584]{1,0:T(8,128)(2,1)} %act_ref.1, bf16[128,3584]{1,0:T(8,128)(2,1)} %grad_ref.1), custom_call_target="tpu_custom_call" | custom-call | tf_op jit(solution)/shard_map/pallas_call | solution.py:101
  10.1 7.5 %all-to-all-start = ((bf16[16,4,3584]{2,1,0:T(4,128)(2,1)}), bf16[16,4,3584]{2,1,0:T(4,128)(2,1)S(1)}, u32[]{:S(2)}, u32[]{:S(2)}) async-start(bf16[16,4,3584]{2,1,0:T(4,128)(2,1)} %shard_map.102), calls=%async_computation | async-start | bytes 917504 | tf_op jit(solution)/shard_map/all_to_all | solution.py:349
  17.6 0.0 all-gather.4.cloned.1.call-start
  17.6 5.2 %shard_map.103 = bf16[16,2,16,3584]{3,2,1,0:T(8,128)(2,1)} custom-call(s32[2,128]{1,0:T(2,128)} %bitcast.19, f32[2,128]{1,0:T(2,128)} %bitcast.41, bf16[128,3584]{1,0:T(8,128)(2,1)} %act_ref.1, bf16[128,3584]{1,0:T(8,128)(2,1)} %grad_ref.1), custom_call_target="tpu_custom_call" | custom-call | flops 1879048192 | bytes 5505024 | tf_op jit(solution)/shard_map/pallas_call | solution.py:79
  22.8 4.2 %all-to-all-done.in_ref = bf16[16,4,3584]{2,1,0:T(4,128)(2,1)S(1)} async-done(((bf16[16,4,3584]{2,1,0:T(4,128)(2,1)}), bf16[16,4,3584]{2,1,0:T(4,128)(2,1)S(1)}, u32[]{:S(2)}, u32[]{:S(2)}) %all-to-all-start) | async-done | bytes 458784 | tf_op jit(solution)/shard_map/all_to_all | solution.py:349
  27.0 0.9 shard_map.104
  28.0 0.0 all-gather.4.cloned.1.call-update
  28.0 0.0 reduce-scatter.2.cloned.1.call-start
  28.0 0.0 copy-start.5
  28.0 0.0 copy-start.6
  28.1 49.5 %all_to_all.15 = bf16[16,32,3584]{2,1,0:T(8,128)(2,1)} all-to-all(bf16[16,32,3584]{2,1,0:T(8,128)(2,1)} %bitcast.37), channel_id=1, replica_groups={{0,16,32,48,64,80,96,112,128,144,160,176,192,208,224,240},{8,24,40,56,7..., dimensions={0} | all-to-all | bytes 7340032 | tf_op jit(solution)/shard_map/all_to_all | solution.py:349
  77.5 0.0 collective-permute-start
  77.5 0.5 all-gather.4.cloned.1.call-done
  78.0 0.0 collective-permute-start.2
  78.0 0.0 copy-done.5
  78.0 0.0 copy-done.6
  78.0 1.3 copy-done.7
  79.4 5.3 %shard_map.105 = (bf16[256,3584]{1,0:T(8,128)(2,1)S(1)}, bf16[576,256]{1,0:T(8,128)(2,1)S(1)}) custom-call(bf16[16,2,16,3584]{3,2,1,0:T(8,128)(2,1)} %bitcast.5.src_ref.refs_0_, bf16[192,3584]{1,0:T(8,128)(2,1)S(1)} %bitcast.24, bf16[192,3584]{1,0:T(8,128)(2,1)S(1)} %bitcast.28, bf16[192,3584]{1,0:T(8,128)(2,1)S(1)} %bitcast.32), custom_call_target="tpu_custom_call" | custom-call | flops 7046430720 | bytes 9633792 | tf_op jit(solution)/shard_map/pallas_call | solution.py:207
  84.7 0.0 copy-done.1
  84.7 3.2 %shard_map.106 = (bf16[256,3584]{1,0:T(8,128)(2,1)S(1)}, bf16[576,256]{1,0:T(8,128)(2,1)S(1)}) custom-call(bf16[8,2,32,3584]{3,2,1,0:T(8,128)(2,1)S(1)} %bitcast.22, bf16[192,3584]{1,0:T(8,128)(2,1)S(1)} %bitcast.25, bf16[192,3584]{1,0:T(8,128)(2,1)S(1)} %bitcast.29, bf16[192,3584]{1,0:T(8,128)(2,1)S(1)} %bitcast.33), custom_call_target="tpu_custom_call" | custom-call | flops 7046430720 | bytes 9633792 | tf_op jit(solution)/shard_map/pallas_call | solution.py:207
  87.9 0.0 collective-permute-done.src_ref.refs_1_
  87.9 0.0 copy-start.8
  87.9 5.2 %shard_map.107 = (bf16[256,3584]{1,0:T(8,128)(2,1)S(1)}, bf16[576,256]{1,0:T(8,128)(2,1)S(1)}) custom-call(bf16[16,2,16,3584]{3,2,1,0:T(8,128)(2,1)} %collective-permute-done.src_ref.refs_1_, bf16[192,3584]{1,0:T(8,128)(2,1)S(1)} %bitcast.26, bf16[192,3584]{1,0:T(8,128)(2,1)S(1)} %bitcast.30, bf16[192,3584]{1,0:T(8,128)(2,1)S(1)} %bitcast.34), custom_call_target="tpu_custom_call" | custom-call | flops 7046430720 | bytes 9633792 | tf_op jit(solution)/shard_map/pallas_call | solution.py:207
  93.1 0.0 copy-start.9
  93.1 0.7 copy-done.9
  93.8 0.5 collective-permute-start.1
  94.3 0.0 collective-permute-done.2.src_ref.refs_3_
  94.3 0.0 copy-done.8
  94.3 3.2 %shard_map.108 = (bf16[256,3584]{1,0:T(8,128)(2,1)S(1)}, bf16[576,256]{1,0:T(8,128)(2,1)S(1)}) custom-call(bf16[8,2,32,3584]{3,2,1,0:T(8,128)(2,1)S(1)} %collective-permute-done.2.src_ref.refs_3_, bf16[192,3584]{1,0:T(8,128)(2,1)S(1)} %bitcast.27, bf16[192,3584]{1,0:T(8,128)(2,1)S(1)} %bitcast.31, bf16[192,3584]{1,0:T(8,128)(2,1)S(1)} %bitcast.35), custom_call_target="tpu_custom_call" | custom-call | flops 7046430720 | bytes 9633792 | tf_op jit(solution)/shard_map/pallas_call | solution.py:207
  97.5 0.0 copy-done.3
  97.5 0.0 copy-start.11
  97.5 0.7 copy-done.11
  98.2 0.0 collective-permute-start.3
  98.3 0.0 collective-permute-done.1.far_more_ref
  98.3 3.8 %collective-permute-done.3.near_more_ref = bf16[256,3584]{1,0:T(8,128)(2,1)S(1)} collective-permute-done((bf16[256,3584]{1,0:T(8,128)(2,1)S(1)}, bf16[256,3584]{1,0:T(8,128)(2,1)S(1)}, u32[]{:S(2)}, u32[]{:S(2)}) %collective-permute-start.3) | collective-permute-done | bytes 1835040 | tf_op jit(solution)/shard_map/ppermute | solution.py:344
  102.0 3.3 %shard_map.109 = bf16[8,256,896]{2,1,0:T(8,128)(2,1)} custom-call(bf16[256,3584]{1,0:T(8,128)(2,1)S(1)} %get-tuple-element.31.far_ref, bf16[256,3584]{1,0:T(8,128)(2,1)S(1)} %collective-permute-done.1.far_more_ref, bf16[256,3584]{1,0:T(8,128)(2,1)S(1)} %get-tuple-element.36.near_ref, bf16[256,3584]{1,0:T(8,128)(2,1)S(1)} %collective-permute-done.3.near_more_ref), custom_call_target="tpu_custom_call" | custom-call | tf_op jit(solution)/shard_map/pallas_call | solution.py:252
  105.3 0.0 reduce-scatter.2.cloned.1.call-update
  105.3 0.9 copy-done.10
  106.3 0.1 copy-done.12
  106.4 2.0 copy-done.2
  108.4 2.0 copy-done.4
  110.4 8.1 %shard_map.110 = (bf16[192,3584]{1,0:T(8,128)(2,1)}, bf16[192,3584]{1,0:T(8,128)(2,1)}, bf16[192,3584]{1,0:T(8,128)(2,1)}) custom-call(bf16[16,2,16,3584]{3,2,1,0:T(8,128)(2,1)} %bitcast.5.src_ref.refs_0_, bf16[16,2,16,3584]{3,2,1,0:T(8,128)(2,1)} %collective-permute-done.src_ref.refs_1_, bf16[8,2,32,3584]{3,2,1,0:T(8,128)(2,1)S(1)} %bitcast.23, ...), custom_call_target="tpu_custom_call" | custom-call | flops 16911433728 | bytes 18808832 | tf_op jit(solution)/shard_map/pallas_call | solution.py:285
  118.6 38.1 %reduce-scatter.2.cloned.1.call-done = bf16[1,256,896]{2,1,0:T(8,128)(2,1)} async-done(((bf16[8,256,896]{2,1,0:T(8,128)(2,1)}), bf16[1,256,896]{2,1,0:T(8,128)(2,1)}) %reduce-scatter.2.cloned.1.call-update) | async-done | bytes 458768 | tf_op jit(solution)/shard_map/reduce_scatter | solution.py:378
  156.6 16.8 %all_to_all.16.back_ref = bf16[16,16,896]{2,1,0:T(8,128)(2,1)S(1)} all-to-all(bf16[16,16,896]{2,1,0:T(8,128)(2,1)} %bitcast.39), channel_id=1, replica_groups={{0,16,32,48,64,80,96,112,128,144,160,176,192,208,224,240},{8,24,40,56,7..., dimensions={0} | all-to-all | bytes 917504 | tf_op jit(solution)/shard_map/all_to_all | solution.py:349
  173.4 0.5 shard_map.111
  173.9 27.1 %all-gather.1 = bf16[1024,448]{1,0:T(8,128)(2,1)S(1)} all-gather(bf16[128,448]{1,0:T(8,128)(2,1)S(1)} %shard_map.111), channel_id=3, replica_groups=mesh['exp'=32,'tp'=8] {'tp'}, dimensions={0}, use_global_device_ids=true | all-gather | bytes 1032192 | tf_op jit(solution)/shard_map/all_gather | solution.py:382
  201.0 0.6 copy.14
  201.6 1.3 copy.15
  (9 shorter events, 0.0 us)
Async XLA Ops:
  10.1 16.9 %all-to-all-start = ((bf16[16,4,3584]{2,1,0:T(4,128)(2,1)}), bf16[16,4,3584]{2,1,0:T(4,128)(2,1)S(1)}, u32[]{:S(2)}, u32[]{:S(2)}) async-start(bf16[16,4,3584]{2,1,0:T(4,128)(2,1)} %shard_map.102), calls=%async_computation | async-start | bytes 917504 | tf_op jit(solution)/shard_map/all_to_all | solution.py:349
  17.6 60.4 %all-gather.4.cloned.1.call-start = ((), (), s32[]{:S(2)}) async-start(), calls=%async_computation.5 | async-start | bytes 4128768 | tf_op jit(solution)/shard_map/all_gather | solution.py:358
  28.0 128.7 %reduce-scatter.2.cloned.1.call-start = ((), (), s32[]{:S(2)}) async-start(), calls=%async_computation.4 | async-start | bytes 4128768 | tf_op jit(solution)/shard_map/reduce_scatter | solution.py:378
  28.0 50.0 %copy-start.5 = (bf16[1,192,3584]{2,1,0:T(8,128)(2,1)S(1)}, bf16[1,192,3584]{2,1,0:T(8,128)(2,1)}, u32[]{:S(2)}) copy-start(bf16[1,192,3584]{2,1,0:T(8,128)(2,1)} %param.11) | copy-start | bytes 4128772
  28.0 50.0 %copy-start.6 = (bf16[1,192,3584]{2,1,0:T(8,128)(2,1)S(1)}, bf16[1,192,3584]{2,1,0:T(8,128)(2,1)}, u32[]{:S(2)}) copy-start(bf16[1,192,3584]{2,1,0:T(8,128)(2,1)} %param.12) | copy-start | bytes 4128772
  77.5 10.3 %collective-permute-start = (bf16[16,2,16,3584]{3,2,1,0:T(8,128)(2,1)}, bf16[16,2,16,3584]{3,2,1,0:T(8,128)(2,1)}, u32[]{:S(2)}, u32[]{:S(2)}) collective-permute-start(bf16[16,2,16,3584]{3,2,1,0:T(8,128)(2,1)} %bitcast.5.src_ref.refs_0_), channel_id=1, source_target_pairs={{0,8},{8,0},{16,24},{24,16},{32,40},{40,32},{48,56},{56,48},{64,72... | collective-permute-start | bytes 11010056 | tf_op jit(solution)/shard_map/ppermute | solution.py:344
  78.0 16.3 %collective-permute-start.2 = (bf16[8,2,32,3584]{3,2,1,0:T(8,128)(2,1)}, bf16[8,2,32,3584]{3,2,1,0:T(8,128)(2,1)S(1)}, u32[]{:S(2)}, u32[]{:S(2)}) collective-permute-start(bf16[8,2,32,3584]{3,2,1,0:T(8,128)(2,1)} %bitcast.21), channel_id=1, source_target_pairs={{0,8},{8,0},{16,24},{24,16},{32,40},{40,32},{48,56},{56,48},{64,72... | collective-permute-start | bytes 11010056 | tf_op jit(solution)/shard_map/ppermute | solution.py:344
  78.0 1.3 copy-start.7
  79.4 5.3 %copy-start.1 = (bf16[16,32,3584]{2,1,0:T(8,128)(2,1)S(1)}, bf16[16,32,3584]{2,1,0:T(8,128)(2,1)}, u32[]{:S(2)}) copy-start(bf16[16,32,3584]{2,1,0:T(8,128)(2,1)} %all-gather.4.cloned.1.call-done) | copy-start | bytes 11010052
  87.9 6.5 %copy-start.8 = (bf16[1,192,3584]{2,1,0:T(8,128)(2,1)S(1)}, bf16[1,192,3584]{2,1,0:T(8,128)(2,1)}, u32[]{:S(2)}) copy-start(bf16[1,192,3584]{2,1,0:T(8,128)(2,1)} %param.13) | copy-start | bytes 4128772
  93.1 0.7 copy-start.9
  93.8 4.4 %collective-permute-start.1 = (bf16[256,3584]{1,0:T(8,128)(2,1)S(1)}, bf16[256,3584]{1,0:T(8,128)(2,1)S(1)}, u32[]{:S(2)}, u32[]{:S(2)}) collective-permute-start(bf16[256,3584]{1,0:T(8,128)(2,1)S(1)} %get-tuple-element.35), channel_id=1, source_target_pairs={{0,8},{8,0},{16,24},{24,16},{32,40},{40,32},{48,56},{56,48},{64,72... | collective-permute-start | bytes 5505032 | tf_op jit(solution)/shard_map/ppermute | solution.py:344
  94.3 3.2 %copy-start.3 = (bf16[8,2,32,3584]{3,2,1,0:T(8,128)(2,1)}, bf16[8,2,32,3584]{3,2,1,0:T(8,128)(2,1)S(1)}, u32[]{:S(2)}) copy-start(bf16[8,2,32,3584]{3,2,1,0:T(8,128)(2,1)S(1)} %collective-permute-done.2.src_ref.refs_3_) | copy-start | bytes 11010052
  97.5 0.7 copy-start.11
  98.2 3.8 %collective-permute-start.3 = (bf16[256,3584]{1,0:T(8,128)(2,1)S(1)}, bf16[256,3584]{1,0:T(8,128)(2,1)S(1)}, u32[]{:S(2)}, u32[]{:S(2)}) collective-permute-start(bf16[256,3584]{1,0:T(8,128)(2,1)S(1)} %get-tuple-element.38), channel_id=1, source_target_pairs={{0,8},{8,0},{16,24},{24,16},{32,40},{40,32},{48,56},{56,48},{64,72... | collective-permute-start | bytes 5505032 | tf_op jit(solution)/shard_map/ppermute | solution.py:344
  105.3 1.0 copy-start.10
  105.3 1.0 copy-start.12
  106.4 2.0 copy-start.2
  108.4 2.0 copy-start.4
  110.4 63.0 %copy-start = (s32[128,2]{0,1:T(2,128)S(1)}, s32[128,2]{0,1:T(2,128)}, u32[]{:S(2)}) copy-start(s32[128,2]{0,1:T(2,128)} %param.9) | copy-start | bytes 3076
Sparse Core Ops, SparseCore 0:
  28.1 49.8 all-gather.3
  105.5 51.1 reduce-scatter.1

commit v6 on v5

--- a/solution.py
+++ b/solution.py
@@ -12,6 +12,7 @@
 VMEM = pltpu.VMEM
 LIMIT = 28 * 1024 * 1024
 WHOLE = 60 * 1024 * 1024
+PASS = 62 * 1024 * 1024
 
 
 def table(ids, experts):
@@ -136,168 +137,168 @@
 
 
 def expert_kernel(
-    turn, src_ref, gate_ref, up_ref, down_ref, part_ref, side_ref, pre_acc, back_acc, dgu_ref, kept
+    far_ref, near_ref, g0, u0, g1, u1, d0, d1, part_ref, side_ref, pre_acc, back_acc, both_ref, kept
 ):
-    outer, _, inner, width = src_ref.shape
-    rows = outer * inner
-    units = down_ref.shape[0]
+    units = g0.shape[0]
+    half = pre_acc.shape[0] // 2
     contract = (((1,), (1,)), ((), ()))
     phase, at = pl.program_id(0), pl.program_id(1)
 
     @pl.when(phase == 0)
     def _():
-        x = src_ref[:, 0].reshape(rows, width)
-        g = src_ref[:, 1].reshape(rows, width)
-        kept[at, :units] = gate_ref[...]
-        kept[at, units:] = up_ref[...]
-        pre = lax.dot_general(x, kept[at], contract, preferred_element_type=F32)
-        back = lax.dot_general(g, down_ref[...], contract, preferred_element_type=F32)
-
-        @pl.when(at == 0)
-        def _():
-            pre_acc[...] = pre
-            back_acc[...] = back
-
-        @pl.when(at > 0)
-        def _():
-            pre_acc[...] += pre
-            back_acc[...] += back
+        for i, ref in enumerate((g0, u0, g1, u1)):
+            kept[at, i * units : (i + 1) * units] = ref[...]
+        down = jnp.concatenate([d0[...], d1[...]], axis=0)
+        for i, ref in enumerate((far_ref, near_ref)):
+            rows = slice(i * half, (i + 1) * half)
+            x = ref[:, 0].reshape(half, -1)
+            g = ref[:, 1].reshape(half, -1)
+            pre = lax.dot_general(x, kept[at], contract, preferred_element_type=F32)
+            back = lax.dot_general(g, down, contract, preferred_element_type=F32)
+
+            @pl.when(at == 0)
+            def _():
+                pre_acc[rows] = pre
+                back_acc[rows] = back
+
+            @pl.when(at > 0)
+            def _():
+                pre_acc[rows] += pre
+                back_acc[rows] += back
 
     @pl.when((phase == 0) & (at == pl.num_programs(1) - 1))
     def _():
-        pre_gate = pre_acc[:, :units]
-        pre_up = pre_acc[:, units:]
-        back = back_acc[...]
-        sig = jax.nn.sigmoid(pre_gate)
-        silu = pre_gate * sig
-        hidden = (silu * pre_up).astype(BF16)
-        d_gate = (back * pre_up * sig * (1.0 + pre_gate * (1.0 - sig))).astype(BF16)
-        d_up = (back * silu).astype(BF16)
-        side_ref[:units, :] = d_gate.T
-        side_ref[units : 2 * units, :] = d_up.T
-        side_ref[2 * units :, :] = hidden.T
-        dgu_ref[:, :units] = d_gate
-        dgu_ref[:, units:] = d_up
-        if turn:
-            to = lax.broadcasted_iota(jnp.int32, (rows, rows), 0)
-            of = lax.broadcasted_iota(jnp.int32, (rows, rows), 1)
-            chip, place = to // (2 * outer), to % (2 * outer)
-            moved = of == (place // 2) * inner + 2 * chip + place % 2
-            moved = jnp.where(moved, 1.0, 0.0).astype(BF16)
-            dgu_ref[...] = jnp.dot(moved, dgu_ref[...], preferred_element_type=F32).astype(BF16)
+        for i in range(2):
+            pre_gate = pre_acc[:, 2 * i * units : (2 * i + 1) * units]
+            pre_up = pre_acc[:, (2 * i + 1) * units : (2 * i + 2) * units]
+            back = back_acc[:, i * units : (i + 1) * units]
+            sig = jax.nn.sigmoid(pre_gate)
+            silu = pre_gate * sig
+            hidden = (silu * pre_up).astype(BF16)
+            d_gate = (back * pre_up * sig * (1.0 + pre_gate * (1.0 - sig))).astype(BF16)
+            d_up = (back * silu).astype(BF16)
+            base = 3 * i * units
+            side_ref[base : base + units] = d_gate.T
+            side_ref[base + units : base + 2 * units] = d_up.T
+            side_ref[base + 2 * units : base + 3 * units] = hidden.T
+            both_ref[:, 2 * i * units : (2 * i + 1) * units] = d_gate
+            both_ref[:, (2 * i + 1) * units : (2 * i + 2) * units] = d_up
+        outer, inner = near_ref.shape[0], near_ref.shape[2]
+        to = lax.broadcasted_iota(jnp.int32, (half, half), 0)
+        of = lax.broadcasted_iota(jnp.int32, (half, half), 1)
+        chip, place = to // (2 * outer), to % (2 * outer)
+        moved = of == (place // 2) * inner + 2 * chip + place % 2
+        moved = jnp.where(moved, 1.0, 0.0).astype(BF16)
+        both_ref[half:] = jnp.dot(moved, both_ref[half:], preferred_element_type=F32).astype(BF16)
 
     @pl.when(phase == 1)
     def _():
-        part = jnp.dot(dgu_ref[...], kept[at], preferred_element_type=F32)
-        part_ref[...] = part.astype(BF16)
-
-
-def expert_part(src, gate_w, up_w, down_w, turn):
-    outer, _, inner, width = src.shape
-    rows = outer * inner
-    units = down_w.shape[0]
-    steps = 1
+        part = jnp.dot(both_ref[...], kept[at], preferred_element_type=F32).astype(BF16)
+        wide = part_ref.shape[2] // 2
+        for j in range(part_ref.shape[0]):
+            cut = part[:, j * wide : (j + 1) * wide]
+            part_ref[j] = jnp.concatenate([cut[:half], cut[half:]], axis=1)
+
+
+def expert_part(far, near, weights, pieces):
+    width = far.shape[3]
+    half = far.shape[0] * far.shape[2]
+    units = weights[0].shape[0]
+    steps = 2
     tile = width // steps
     last = steps - 1
 
     def first_phase(p, i):
         return jnp.where(p == 0, i, last)
 
-    weight_spec = pl.BlockSpec((units, tile), lambda p, i: (0, first_phase(p, i)))
-    return pl.pallas_call(
-        functools.partial(expert_kernel, turn),
+    return pl.pallas_call(
+        expert_kernel,
         grid=(2, steps),
         in_specs=[
-            pl.BlockSpec((outer, 2, inner, tile), lambda p, i: (0, 0, 0, first_phase(p, i))),
-            weight_spec,
-            weight_spec,
-            weight_spec,
-        ],
+            pl.BlockSpec(src.shape[:3] + (tile,), lambda p, i: (0, 0, 0, first_phase(p, i)))
+            for src in (far, near)
+        ]
+        + [pl.BlockSpec((units, tile), lambda p, i: (0, first_phase(p, i)))] * 6,
         out_specs=[
-            pl.BlockSpec((rows, tile), lambda p, i: (0, p * i)),
-            pl.BlockSpec((3 * units, rows), lambda p, i: (0, 0)),
+            pl.BlockSpec((pieces // steps, half, 2 * width // pieces), lambda p, i: (p * i, 0, 0)),
+            pl.BlockSpec((6 * units, 2 * half), lambda p, i: (0, 0)),
         ],
         out_shape=[
-            jax.ShapeDtypeStruct((rows, width), BF16),
-            jax.ShapeDtypeStruct((3 * units, rows), BF16),
+            pltpu.HBM((pieces, half, 2 * width // pieces), BF16),
+            jax.ShapeDtypeStruct((6 * units, 2 * half), BF16),
         ],
         scratch_shapes=[
-            VMEM((rows, 2 * units), F32),
-            VMEM((rows, units), F32),
-            VMEM((rows, 2 * units), BF16),
-            VMEM((steps, 2 * units, tile), BF16),
-        ],
+            VMEM((2 * half, 4 * units), F32),
+            VMEM((2 * half, 2 * units), F32),
+            VMEM((2 * half, 4 * units), BF16),
+            VMEM((steps, 4 * units, tile), BF16),
+        ],
+        compiler_params=pltpu.CompilerParams(vmem_limit_bytes=PASS),
+        cost_estimate=pl.CostEstimate(
+            flops=40 * half * width * units,
+            bytes_accessed=2 * (6 * half * width + 6 * units * width),
+            transcendentals=4 * half * units,
+        ),
+    )(far, near, *weights)
+
+
+def weight_kernel(base, far_ref, near_ref, side_ref, *refs):
+    tile = far_ref.shape[3]
+    units = side_ref.shape[0] // 6
+    base = base * units
+
+    def stacked(kind):
+        return jnp.concatenate(
+            [ref[:, kind].reshape(-1, tile) for ref in (far_ref, near_ref)], axis=0
+        )
+
+    pair = jnp.dot(side_ref[base : base + 2 * units], stacked(0), preferred_element_type=F32)
+    down = jnp.dot(
+        side_ref[base + 2 * units : base + 3 * units], stacked(1), preferred_element_type=F32
+    )
+    if len(refs) == 1:
+        refs[0][: 2 * units] = pair.astype(BF16)
+        refs[0][2 * units :] = down.astype(BF16)
+    else:
+        more_ref, gate_ref, up_ref, down_ref = refs
+        pair += more_ref[: 2 * units].astype(F32)
+        down += more_ref[2 * units :].astype(F32)
+        gate_ref[...] = pair[:units].astype(BF16)
+        up_ref[...] = pair[units:].astype(BF16)
+        down_ref[...] = down.astype(BF16)
+
+
+def weight_grads(far, near, side, more):
+    width = far.shape[3]
+    units = side.shape[0] // 6
+    tile = width // 4
+    specs = [
+        pl.BlockSpec(far.shape[:3] + (tile,), lambda i: (0, 0, 0, i)),
+        pl.BlockSpec(near.shape[:3] + (tile,), lambda i: (0, 0, 0, i)),
+        pl.BlockSpec(side.shape, lambda i: (0, 0)),
+    ]
+    three = pl.BlockSpec((3 * units, tile), lambda i: (0, i))
+    one = pl.BlockSpec((units, tile), lambda i: (0, i))
+    if more is None:
+        base, operands = 3, (far, near, side)
+        out_specs, out_shape = three, jax.ShapeDtypeStruct((3 * units, width), BF16)
+    else:
+        base, operands = 0, (far, near, side, more)
+        specs = specs + [three]
+        out_specs, out_shape = [one] * 3, [jax.ShapeDtypeStruct((units, width), BF16)] * 3
+    return pl.pallas_call(
+        functools.partial(weight_kernel, base),
+        grid=(width // tile,),
+        in_specs=specs,
+        out_specs=out_specs,
+        out_shape=out_shape,
         compiler_params=pltpu.CompilerParams(vmem_limit_bytes=LIMIT),
         cost_estimate=pl.CostEstimate(
-            flops=40 * rows * width * units,
-            bytes_accessed=2 * (3 * rows * width + 3 * units * width),
-            transcendentals=rows * units,
-        ),
-    )(src, gate_w, up_w, down_w)
-
-
-def merge_kernel(far_ref, far_more_ref, near_ref, near_more_ref, out_ref):
-    wide = out_ref.shape[2] // 2
-    far = (far_ref[...].astype(F32) + far_more_ref[...].astype(F32)).astype(BF16)
-    near = (near_ref[...].astype(F32) + near_more_ref[...].astype(F32)).astype(BF16)
-    for j in range(out_ref.shape[0]):
-        at = slice(j * wide, (j + 1) * wide)
-        out_ref[j] = jnp.concatenate([far[:, at], near[:, at]], axis=1)
-
-
-def merge(far, far_more, near, near_more, pieces):
-    rows, width = far.shape
-    steps = pieces // 2
-    spec = pl.BlockSpec((rows, width // steps), lambda i: (0, i))
-    return pl.pallas_call(
-        merge_kernel,
-        grid=(steps,),
-        in_specs=[spec] * 4,
-        out_specs=pl.BlockSpec((2, rows, 2 * width // pieces), lambda i: (i, 0, 0)),
-        out_shape=pltpu.HBM((pieces, rows, 2 * width // pieces), BF16),
-        compiler_params=pltpu.CompilerParams(vmem_limit_bytes=LIMIT),
-    )(far, far_more, near, near_more)
-
-
-def weight_kernel(count, *refs):
-    sources, sides = refs[:count], refs[count : 2 * count]
-    gate_ref, up_ref, down_ref = refs[2 * count :]
-    units = gate_ref.shape[0]
-    tile = sources[0].shape[3]
-
-    def stacked(kind):
-        return jnp.concatenate([s[:, kind].reshape(-1, tile) for s in sources], axis=0)
-
-    left = jnp.concatenate([s[: 2 * units] for s in sides], axis=1)
-    pair = jnp.dot(left, stacked(0), preferred_element_type=F32)
-    left = jnp.concatenate([s[2 * units :] for s in sides], axis=1)
-    down = jnp.dot(left, stacked(1), preferred_element_type=F32)
-    gate_ref[...] = pair[:units].astype(BF16)
-    up_ref[...] = pair[units:].astype(BF16)
-    down_ref[...] = down.astype(BF16)
-
-
-def weight_grads(sources, sides):
-    width = sources[0].shape[3]
-    units = sides[0].shape[0] // 3
-    rows = sum(side.shape[1] for side in sides)
-    tile = width // 4
-    return pl.pallas_call(
-        functools.partial(weight_kernel, len(sources)),
-        grid=(width // tile,),
-        in_specs=[
-            pl.BlockSpec(src.shape[:3] + (tile,), lambda i: (0, 0, 0, i)) for src in sources
-        ]
-        + [pl.BlockSpec(side.shape, lambda i: (0, 0)) for side in sides],
-        out_specs=[pl.BlockSpec((units, tile), lambda i: (0, i))] * 3,
-        out_shape=[jax.ShapeDtypeStruct((units, width), BF16)] * 3,
-        compiler_params=pltpu.CompilerParams(vmem_limit_bytes=LIMIT),
-        cost_estimate=pl.CostEstimate(
-            flops=24 * rows * width * units,
-            bytes_accessed=2 * (2 * rows * width + 3 * units * width),
+            flops=6 * side.shape[1] * width * units,
+            bytes_accessed=2 * (2 * side.shape[1] * width + 6 * units * width),
             transcendentals=0,
         ),
-    )(*sources, *sides)
+    )(*operands)
 
 
 def combine_kernel(ids_ref, back_ref, out_ref):
@@ -357,24 +358,13 @@
     near = sort_kinds(near)
     near = lax.all_gather(near, "tp", axis=0, tiled=False)
     far = spread(far.reshape(experts, 2 * half, width)).reshape(far.shape)
-    weights = (gate_proj[0], up_proj[0], down_proj[0])
-    far_other = trade(far)
-    near_other = trade(near)
-    far_part, far_side = expert_part(far, *weights, False)
-    near, far_part = lax.optimization_barrier((near, far_part))
-    near_part, near_side = expert_part(near, *weights, True)
-    far_other, near_part = lax.optimization_barrier((far_other, near_part))
-    far_other_part, far_other_side = expert_part(far_other, *weights, False)
-    far_sent = trade(far_other_part)
-    near_other, far_other_part = lax.optimization_barrier((near_other, far_other_part))
-    near_other_part, near_other_side = expert_part(near_other, *weights, True)
-    near_sent = trade(near_other_part)
-    both = merge(far_part, far_sent, near_part, near_sent, planes)
-    both, far = lax.optimization_barrier((both, far))
-    gate_g, up_g, down_g = weight_grads(
-        [far, far_other, near, near_other],
-        [far_side, far_other_side, near_side, near_other_side],
-    )
+    own = (gate_proj[0], up_proj[0], down_proj[0])
+    other = tuple(trade(v) for v in own)
+    weights = (own[0], own[1], other[0], other[1], own[2], other[2])
+    both, side = expert_part(far, near, weights, planes)
+    both, side = lax.optimization_barrier((both, side))
+    shared = trade(weight_grads(far, near, side, None))
+    gate_g, up_g, down_g = weight_grads(far, near, side, shared)
     mine = lax.psum_scatter(both, "tp", scatter_dimension=0, tiled=False)
     mine, gate_g, up_g, down_g = lax.optimization_barrier((mine, gate_g, up_g, down_g))
     returned = spread(mine.reshape(experts, half, -1))

time: 210 us -> 207 us (0.986)
  blocking collectives: 93.3 us -> 43.9 us
  waiting for transfers between devices: 46.6 us -> 90.5 us
  starting transfers between devices: 8.1 us -> 14.3 us
  local copies, waits for them, and re-layouts: 9.77 us -> 6.27 us
    all_to_all x2 -> x1, blocking collectives: 66.2 us -> 16.8 us  [spread(): lax.all_to_all(v, 'exp', split_axis=0, concat_axis=0, tiled=True, axis_in...]
    all_to_all x1 -> x2, waiting for transfers between devices: 4.2 us -> 43.6 us  [spread(): lax.all_to_all(v, 'exp', split_axis=0, concat_axis=0, tiled=True, axis_in...]
    ppermute x4, waiting for transfers between devices: 3.77 us -> 13.5 us  [trade(): return lax.ppermute(v, 'exp', swap)]
    all_to_all x1 -> x2, starting transfers between devices: 7.49 us -> 13.5 us  [spread(): lax.all_to_all(v, 'exp', split_axis=0, concat_axis=0, tiled=True, axis_in...]
    reduce_scatter x1, waiting for transfers between devices: 38.1 us -> 33.4 us  [per_device(): mine = lax.psum_scatter(both, 'tp', scatter_dimension=0, tiled=False)]
    unnamed x27 -> x15, local copies, waits for them, and re-layouts: 9.16 us -> 5.66 us
    pallas_call x6 -> x3, Pallas kernels: 28.3 us -> 27.9 us  [the longest x1 16.9 us: expert_part(): pl.pallas_call(expert_kernel, grid=(2, steps), in_specs=[pl.BlockSpec(src...]
  transfers between devices with their start and end apart: 7 -> 8, of which waited for: 4 -> 6; matrix products, arithmetic and copies ran while one was open for 0% -> 0% of each run, Pallas kernels for 14% -> 8%
where the time goes in v6:
time: 207 us
  waiting for transfers between devices  90.5 us (44%)
  blocking collectives  43.9 us (21%)
  Pallas kernels  37.5 us (18%)
  starting transfers between devices  14.3 us (7%)
  between operations  14.1 us (7%)
  local copies, waits for them, and re-layouts  6.27 us (3%)
    all_to_all x2, waiting for transfers between devices, spread(): lax.all_to_all(v, 'exp', split_axis=0, concat_axis=0, tiled=True, axis_in...  43.6 us
    reduce_scatter x1, waiting for transfers between devices, per_device(): mine = lax.psum_scatter(both, 'tp', scatter_dimension=0, tiled=False)  33.4 us
    all_gather x1, blocking collectives, per_device(): gathered = lax.all_gather(piece, 'tp', axis=0, tiled=False)  27.1 us
    pallas_call x1, Pallas kernels, expert_part(): pl.pallas_call(expert_kernel, grid=(2, steps), in_specs=[pl.BlockSpec(src...  16.9 us
    all_to_all x1, blocking collectives, spread(): lax.all_to_all(v, 'exp', split_axis=0, concat_axis=0, tiled=True, axis_in...  16.8 us
    ppermute x4, waiting for transfers between devices, trade(): return lax.ppermute(v, 'exp', swap)  13.5 us
    all_to_all x2, starting transfers between devices, spread(): lax.all_to_all(v, 'exp', split_axis=0, concat_axis=0, tiled=True, axis_in...  13.5 us
    pallas_call x2, Pallas kernels, weight_grads(): pl.pallas_call(functools.partial(weight_kernel, base), grid=(width // til...  11.1 us
  transfers between devices with their start and end apart: 8, of which 6 were waited for; matrix products, arithmetic and copies ran while one was open for 0% of the time, Pallas kernels for 8%

profile of v6, /device:TPU:2, one launch (start us, length us, event | category | flops | bytes accessed | tf_op | source)
XLA Modules:
  0.0 206.6 jit_solution(15319615653459415306)
XLA Ops:
  7.2 2.9 %shard_map.102 = bf16[16,4,3584]{2,1,0:T(4,128)(2,1)} custom-call(s32[1]{0:T(128)} %bitcast.1.tp_ref, s32[2,128]{1,0:T(2,128)} %bitcast.21, f32[2,128]{1,0:T(2,128)} %bitcast.28, bf16[128,3584]{1,0:T(8,128)(2,1)} %act_ref.1, bf16[128,3584]{1,0:T(8,128)(2,1)} %grad_ref.1), custom_call_target="tpu_custom_call" | custom-call | tf_op jit(solution)/shard_map/pallas_call | solution.py:102
  10.1 7.5 %all-to-all-start = ((bf16[16,4,3584]{2,1,0:T(4,128)(2,1)}), bf16[16,4,3584]{2,1,0:T(4,128)(2,1)S(1)}, u32[]{:S(2)}, u32[]{:S(2)}) async-start(bf16[16,4,3584]{2,1,0:T(4,128)(2,1)} %shard_map.102), calls=%async_computation | async-start | bytes 917504 | tf_op jit(solution)/shard_map/all_to_all | solution.py:350
  17.6 0.0 all-gather.4.cloned.1.call-start
  17.6 5.2 %shard_map.103 = bf16[16,2,16,3584]{3,2,1,0:T(8,128)(2,1)} custom-call(s32[2,128]{1,0:T(2,128)} %bitcast.22, f32[2,128]{1,0:T(2,128)} %bitcast.29, bf16[128,3584]{1,0:T(8,128)(2,1)} %act_ref.1, bf16[128,3584]{1,0:T(8,128)(2,1)} %grad_ref.1), custom_call_target="tpu_custom_call" | custom-call | flops 1879048192 | bytes 5505024 | tf_op jit(solution)/shard_map/pallas_call | solution.py:80
  22.8 4.2 %all-to-all-done.in_ref = bf16[16,4,3584]{2,1,0:T(4,128)(2,1)S(1)} async-done(((bf16[16,4,3584]{2,1,0:T(4,128)(2,1)}), bf16[16,4,3584]{2,1,0:T(4,128)(2,1)S(1)}, u32[]{:S(2)}, u32[]{:S(2)}) %all-to-all-start) | async-done | bytes 458784 | tf_op jit(solution)/shard_map/all_to_all | solution.py:350
  27.0 0.9 shard_map.104
  28.0 0.0 all-gather.4.cloned.1.call-update
  28.0 0.0 copy-start.3
  28.0 0.0 copy-start.4
  28.0 6.0 %all-to-all-start.1 = ((bf16[16,32,3584]{2,1,0:T(8,128)(2,1)}), bf16[16,32,3584]{2,1,0:T(8,128)(2,1)}, u32[]{:S(2)}, u32[]{:S(2)}) async-start(bf16[16,32,3584]{2,1,0:T(8,128)(2,1)} %bitcast.25), calls=%async_computation.1 | async-start | bytes 7340032 | tf_op jit(solution)/shard_map/all_to_all | solution.py:350
  34.0 0.0 reduce-scatter.2.cloned.1.call-start
  34.0 0.0 copy-done.3
  34.0 0.1 collective-permute-start
  34.1 0.0 copy-done.4
  34.1 0.5 collective-permute-start.1
  34.6 0.1 collective-permute-start.2
  34.7 2.5 %collective-permute-done.g1 = bf16[192,3584]{1,0:T(8,128)(2,1)S(1)} collective-permute-done((bf16[192,3584]{1,0:T(8,128)(2,1)S(1)}, bf16[192,3584]{1,0:T(8,128)(2,1)S(1)}, u32[]{:S(2)}, u32[]{:S(2)}) %collective-permute-start) | collective-permute-done | bytes 1376288 | tf_op jit(solution)/shard_map/ppermute | solution.py:345
  37.2 0.0 copy-start.5
  37.2 3.9 %collective-permute-done.1.u1 = bf16[192,3584]{1,0:T(8,128)(2,1)S(1)} collective-permute-done((bf16[192,3584]{1,0:T(8,128)(2,1)S(1)}, bf16[192,3584]{1,0:T(8,128)(2,1)S(1)}, u32[]{:S(2)}, u32[]{:S(2)}) %collective-permute-start.1) | collective-permute-done | bytes 1376288 | tf_op jit(solution)/shard_map/ppermute | solution.py:345
  41.2 0.0 copy-done.5
  41.2 0.0 copy-start.6
  41.2 1.1 copy-done.6
  42.3 0.0 collective-permute-done.2.d1
  42.3 39.4 %all-to-all-done.1 = bf16[16,32,3584]{2,1,0:T(8,128)(2,1)} async-done(((bf16[16,32,3584]{2,1,0:T(8,128)(2,1)}), bf16[16,32,3584]{2,1,0:T(8,128)(2,1)}, u32[]{:S(2)}, u32[]{:S(2)}) %all-to-all-start.1) | async-done | bytes 3670048 | tf_op jit(solution)/shard_map/all_to_all | solution.py:350
  81.6 0.0 all-gather.4.cloned.1.call-done
  81.6 16.9 %shard_map.105 = (bf16[8,256,896]{2,1,0:T(8,128)(2,1)}, bf16[1152,512]{1,0:T(8,128)(2,1)}) custom-call(bf16[16,2,16,3584]{3,2,1,0:T(8,128)(2,1)} %bitcast.4.far_ref, bf16[8,2,32,3584]{3,2,1,0:T(8,128)(2,1)} %bitcast.18, bf16[192,3584]{1,0:T(8,128)(2,1)} %bitcast.30, bf16[192,3584]{1,0:T(8,128)(2,1)} %bitcast.32, bf16[192,3584]{1,0:T(8,128)(2,1)} %copy-done.5, ...), custom_call_target="tpu_custom_call" | custom-call | flops 7046430720 | bytes 19267584 | tf_op jit(solution)/shard_map/pallas_call | solution.py:214
  98.5 0.0 copy-start.1
  98.5 0.0 reduce-scatter.2.cloned.1.call-update
  98.5 1.2 copy-done.1
  99.8 0.0 copy-start
  99.8 2.0 copy-done
  101.8 5.1 %shard_map.106 = bf16[576,3584]{1,0:T(8,128)(2,1)S(1)} custom-call(bf16[16,2,16,3584]{3,2,1,0:T(8,128)(2,1)} %bitcast.4.far_ref, bf16[8,2,32,3584]{3,2,1,0:T(8,128)(2,1)S(1)} %bitcast.19, bf16[1152,512]{1,0:T(8,128)(2,1)S(1)} %copy-done.1), custom_call_target="tpu_custom_call" | custom-call | flops 2113929216 | bytes 15597568 | tf_op jit(solution)/shard_map/pallas_call | solution.py:289
  106.9 0.0 copy-start.2
  106.9 0.1 collective-permute-start.3
  107.0 7.1 %collective-permute-done.3.refs_0_ = bf16[576,3584]{1,0:T(8,128)(2,1)S(1)} collective-permute-done((bf16[576,3584]{1,0:T(8,128)(2,1)S(1)}, bf16[576,3584]{1,0:T(8,128)(2,1)S(1)}, u32[]{:S(2)}, u32[]{:S(2)}) %collective-permute-start.3) | collective-permute-done | bytes 4128800 | tf_op jit(solution)/shard_map/ppermute | solution.py:345
  114.1 6.0 %shard_map.107 = (bf16[192,3584]{1,0:T(8,128)(2,1)}, bf16[192,3584]{1,0:T(8,128)(2,1)}, bf16[192,3584]{1,0:T(8,128)(2,1)}) custom-call(bf16[16,2,16,3584]{3,2,1,0:T(8,128)(2,1)} %bitcast.4.far_ref, bf16[8,2,32,3584]{3,2,1,0:T(8,128)(2,1)S(1)} %bitcast.20, bf16[1152,512]{1,0:T(8,128)(2,1)S(1)} %copy-done.1, bf16[576,3584]{1,0:T(8,128)(2,1)S(1)} %collective-permute-done.3.refs_0_), custom_call_target="tpu_custom_call" | custom-call | flops 2113929216 | bytes 15597568 | tf_op jit(solution)/shard_map/pallas_call | solution.py:289
  120.1 33.4 %reduce-scatter.2.cloned.1.call-done = bf16[1,256,896]{2,1,0:T(8,128)(2,1)} async-done(((bf16[8,256,896]{2,1,0:T(8,128)(2,1)}), bf16[1,256,896]{2,1,0:T(8,128)(2,1)}) %reduce-scatter.2.cloned.1.call-update) | async-done | bytes 458768 | tf_op jit(solution)/shard_map/reduce_scatter | solution.py:368
  153.5 16.8 %all_to_all.15.back_ref = bf16[16,16,896]{2,1,0:T(8,128)(2,1)S(1)} all-to-all(bf16[16,16,896]{2,1,0:T(8,128)(2,1)} %bitcast.27), channel_id=1, replica_groups={{0,16,32,48,64,80,96,112,128,144,160,176,192,208,224,240},{8,24,40,56,7..., dimensions={0} | all-to-all | bytes 917504 | tf_op jit(solution)/shard_map/all_to_all | solution.py:350
  170.2 0.0 copy-done.2
  170.2 0.5 shard_map.108
  170.8 27.1 %all-gather.1 = bf16[1024,448]{1,0:T(8,128)(2,1)S(1)} all-gather(bf16[128,448]{1,0:T(8,128)(2,1)S(1)} %shard_map.108), channel_id=3, replica_groups=mesh['exp'=32,'tp'=8] {'tp'}, dimensions={0}, use_global_device_ids=true | all-gather | bytes 1032192 | tf_op jit(solution)/shard_map/all_gather | solution.py:372
  197.9 0.6 copy.14
  198.5 1.3 copy.15
Async XLA Ops:
  10.1 16.9 %all-to-all-start = ((bf16[16,4,3584]{2,1,0:T(4,128)(2,1)}), bf16[16,4,3584]{2,1,0:T(4,128)(2,1)S(1)}, u32[]{:S(2)}, u32[]{:S(2)}) async-start(bf16[16,4,3584]{2,1,0:T(4,128)(2,1)} %shard_map.102), calls=%async_computation | async-start | bytes 917504 | tf_op jit(solution)/shard_map/all_to_all | solution.py:350
  17.6 64.1 %all-gather.4.cloned.1.call-start = ((), (), s32[]{:S(2)}) async-start(), calls=%async_computation.5 | async-start | bytes 4128768 | tf_op jit(solution)/shard_map/all_gather | solution.py:359
  28.0 6.0 %copy-start.3 = (bf16[1,192,3584]{2,1,0:T(8,128)(2,1)S(1)}, bf16[1,192,3584]{2,1,0:T(8,128)(2,1)}, u32[]{:S(2)}) copy-start(bf16[1,192,3584]{2,1,0:T(8,128)(2,1)} %param.11) | copy-start | bytes 4128772
  28.0 6.1 %copy-start.4 = (bf16[1,192,3584]{2,1,0:T(8,128)(2,1)S(1)}, bf16[1,192,3584]{2,1,0:T(8,128)(2,1)}, u32[]{:S(2)}) copy-start(bf16[1,192,3584]{2,1,0:T(8,128)(2,1)} %param.12) | copy-start | bytes 4128772
  28.0 53.6 %all-to-all-start.1 = ((bf16[16,32,3584]{2,1,0:T(8,128)(2,1)}), bf16[16,32,3584]{2,1,0:T(8,128)(2,1)}, u32[]{:S(2)}, u32[]{:S(2)}) async-start(bf16[16,32,3584]{2,1,0:T(8,128)(2,1)} %bitcast.25), calls=%async_computation.1 | async-start | bytes 7340032 | tf_op jit(solution)/shard_map/all_to_all | solution.py:350
  34.0 119.5 %reduce-scatter.2.cloned.1.call-start = ((), (), s32[]{:S(2)}) async-start(), calls=%async_computation.4 | async-start | bytes 4128768 | tf_op jit(solution)/shard_map/reduce_scatter | solution.py:368
  34.0 3.2 %collective-permute-start = (bf16[192,3584]{1,0:T(8,128)(2,1)S(1)}, bf16[192,3584]{1,0:T(8,128)(2,1)S(1)}, u32[]{:S(2)}, u32[]{:S(2)}) collective-permute-start(bf16[192,3584]{1,0:T(8,128)(2,1)S(1)} %bitcast.31), channel_id=1, source_target_pairs={{0,8},{8,0},{16,24},{24,16},{32,40},{40,32},{48,56},{56,48},{64,72... | collective-permute-start | bytes 4128776 | tf_op jit(solution)/shard_map/ppermute | solution.py:345
  34.1 7.0 %collective-permute-start.1 = (bf16[192,3584]{1,0:T(8,128)(2,1)S(1)}, bf16[192,3584]{1,0:T(8,128)(2,1)S(1)}, u32[]{:S(2)}, u32[]{:S(2)}) collective-permute-start(bf16[192,3584]{1,0:T(8,128)(2,1)S(1)} %bitcast.33), channel_id=1, source_target_pairs={{0,8},{8,0},{16,24},{24,16},{32,40},{40,32},{48,56},{56,48},{64,72... | collective-permute-start | bytes 4128776 | tf_op jit(solution)/shard_map/ppermute | solution.py:345
  34.6 7.6 %collective-permute-start.2 = (bf16[192,3584]{1,0:T(8,128)(2,1)}, bf16[192,3584]{1,0:T(8,128)(2,1)}, u32[]{:S(2)}, u32[]{:S(2)}) collective-permute-start(bf16[192,3584]{1,0:T(8,128)(2,1)} %bitcast.34), channel_id=1, source_target_pairs={{0,8},{8,0},{16,24},{24,16},{32,40},{40,32},{48,56},{56,48},{64,72... | collective-permute-start | bytes 4128776 | tf_op jit(solution)/shard_map/ppermute | solution.py:345
  37.2 3.9 %copy-start.5 = (bf16[192,3584]{1,0:T(8,128)(2,1)}, bf16[192,3584]{1,0:T(8,128)(2,1)S(1)}, u32[]{:S(2)}) copy-start(bf16[192,3584]{1,0:T(8,128)(2,1)S(1)} %collective-permute-done.g1) | copy-start | bytes 4128772
  41.2 1.1 copy-start.6
  98.5 1.3 copy-start.1
  99.8 2.0 copy-start
  106.9 63.3 %copy-start.2 = (s32[128,2]{0,1:T(2,128)S(1)}, s32[128,2]{0,1:T(2,128)}, u32[]{:S(2)}) copy-start(s32[128,2]{0,1:T(2,128)} %param.9) | copy-start | bytes 3076
  106.9 7.2 %collective-permute-start.3 = (bf16[576,3584]{1,0:T(8,128)(2,1)S(1)}, bf16[576,3584]{1,0:T(8,128)(2,1)S(1)}, u32[]{:S(2)}, u32[]{:S(2)}) collective-permute-start(bf16[576,3584]{1,0:T(8,128)(2,1)S(1)} %shard_map.106), channel_id=1, source_target_pairs={{0,8},{8,0},{16,24},{24,16},{32,40},{40,32},{48,56},{56,48},{64,72... | collective-permute-start | bytes 12386312 | tf_op jit(solution)/shard_map/ppermute | solution.py:345
Sparse Core Ops, SparseCore 0:
  28.1 49.8 all-gather.3
  98.7 54.7 reduce-scatter.1

commit v7 on v6

--- a/solution.py
+++ b/solution.py
@@ -352,14 +352,15 @@
         )
 
     near = send_near(tp_at, ids_t, gate_t, activations, out_grad, experts, half)
+    own = (gate_proj[0], up_proj[0], down_proj[0])
+    other = tuple(trade(v) for v in own)
+    other, ids_t = lax.optimization_barrier((other, ids_t))
     near = spread(near)
     far = send_far(ids_t, gate_t, activations, out_grad, experts, half)
     near, far = lax.optimization_barrier((near, far))
     near = sort_kinds(near)
     near = lax.all_gather(near, "tp", axis=0, tiled=False)
     far = spread(far.reshape(experts, 2 * half, width)).reshape(far.shape)
-    own = (gate_proj[0], up_proj[0], down_proj[0])
-    other = tuple(trade(v) for v in own)
     weights = (own[0], own[1], other[0], other[1], own[2], other[2])
     both, side = expert_part(far, near, weights, planes)
     both, side = lax.optimization_barrier((both, side))

time: 207 us -> 200 us (0.966)
  waiting for transfers between devices: 90.5 us -> 40.3 us
  blocking collectives: 43.9 us -> 93.4 us
  starting transfers between devices: 14.3 us -> 8.35 us
    all_to_all x1 -> x2, blocking collectives: 16.8 us -> 66.3 us  [spread(): lax.all_to_all(v, 'exp', split_axis=0, concat_axis=0, tiled=True, axis_in...]
    all_to_all x2 -> x1, waiting for transfers between devices: 43.6 us -> 4.39 us  [spread(): lax.all_to_all(v, 'exp', split_axis=0, concat_axis=0, tiled=True, axis_in...]
    ppermute x4, waiting for transfers between devices: 13.5 us -> 7.06 us  [trade(): return lax.ppermute(v, 'exp', swap)]
    all_to_all x2 -> x1, starting transfers between devices: 13.5 us -> 7.49 us  [spread(): lax.all_to_all(v, 'exp', split_axis=0, concat_axis=0, tiled=True, axis_in...]
    reduce_scatter x1, waiting for transfers between devices: 33.4 us -> 28.5 us  [per_device(): mine = lax.psum_scatter(both, 'tp', scatter_dimension=0, tiled=False)]
    pallas_call x2, Pallas kernels: 11.1 us -> 8.95 us  [weight_grads(): pl.pallas_call(functools.partial(weight_kernel, base), grid=(width // til...]
    unnamed x15 -> x11, local copies, waits for them, and re-layouts: 5.66 us -> 6.61 us
  transfers between devices with their start and end apart: 8 -> 7, of which waited for: 6 -> 4; matrix products, arithmetic and copies ran while one was open for 0% -> 0% of each run, Pallas kernels for 8% -> 9%
where the time goes in v7:
time: 200 us; the launch traced here: 199 us
  blocking collectives  93.4 us (47%)
  waiting for transfers between devices  40.3 us (20%)
  Pallas kernels  35.7 us (18%)
  between operations  14.1 us (7%)
  starting transfers between devices  8.35 us (4%)
  local copies, waits for them, and re-layouts  7.22 us (4%)
    all_to_all x2, blocking collectives, spread(): lax.all_to_all(v, 'exp', split_axis=0, concat_axis=0, tiled=True, axis_in...  66.3 us
    reduce_scatter x1, waiting for transfers between devices, per_device(): mine = lax.psum_scatter(both, 'tp', scatter_dimension=0, tiled=False)  28.5 us
    all_gather x1, blocking collectives, per_device(): gathered = lax.all_gather(piece, 'tp', axis=0, tiled=False)  27.1 us
    pallas_call x1, Pallas kernels, expert_part(): pl.pallas_call(expert_kernel, grid=(2, steps), in_specs=[pl.BlockSpec(src...  16.8 us
    pallas_call x2, Pallas kernels, weight_grads(): pl.pallas_call(functools.partial(weight_kernel, base), grid=(width // til...  8.95 us
    all_to_all x1, starting transfers between devices, spread(): lax.all_to_all(v, 'exp', split_axis=0, concat_axis=0, tiled=True, axis_in...  7.49 us
    ppermute x4, waiting for transfers between devices, trade(): return lax.ppermute(v, 'exp', swap)  7.06 us
    unnamed x11, local copies, waits for them, and re-layouts  6.61 us
  transfers between devices with their start and end apart: 7, of which 4 were waited for; matrix products, arithmetic and copies ran while one was open for 0% of the time, Pallas kernels for 9%

profile of v7, /device:TPU:2, one launch (start us, length us, event | category | flops | bytes accessed | tf_op | source)
XLA Modules:
  0.0 199.1 jit_solution(15856466744376383208)
XLA Ops:
  7.2 0.1 collective-permute-start
  7.3 0.5 collective-permute-start.1
  7.8 0.1 collective-permute-start.2
  7.9 2.9 %shard_map.102 = bf16[16,4,3584]{2,1,0:T(4,128)(2,1)} custom-call(s32[1]{0:T(128)} %bitcast.4.tp_ref, s32[2,128]{1,0:T(2,128)} %bitcast.24, f32[2,128]{1,0:T(2,128)} %bitcast.31, bf16[128,3584]{1,0:T(8,128)(2,1)} %act_ref.1, bf16[128,3584]{1,0:T(8,128)(2,1)} %grad_ref.1), custom_call_target="tpu_custom_call" | custom-call | tf_op jit(solution)/shard_map/pallas_call | solution.py:102
  10.8 7.5 %all-to-all-start = ((bf16[16,4,3584]{2,1,0:T(4,128)(2,1)}), bf16[16,4,3584]{2,1,0:T(4,128)(2,1)S(1)}, u32[]{:S(2)}, u32[]{:S(2)}) async-start(bf16[16,4,3584]{2,1,0:T(4,128)(2,1)} %shard_map.102), calls=%async_computation | async-start | bytes 917504 | tf_op jit(solution)/shard_map/all_to_all | solution.py:350
  18.3 0.0 all-gather.4.cloned.1.call-start
  18.3 0.0 collective-permute-done.g1
  18.3 0.0 copy-start.4
  18.4 0.0 collective-permute-done.1.u1
  18.4 0.0 collective-permute-done.2.d1
  18.4 5.6 %shard_map.103 = bf16[16,2,16,3584]{3,2,1,0:T(8,128)(2,1)} custom-call(s32[2,128]{1,0:T(2,128)} %bitcast.25, f32[2,128]{1,0:T(2,128)} %bitcast.32, bf16[128,3584]{1,0:T(8,128)(2,1)} %act_ref.1, bf16[128,3584]{1,0:T(8,128)(2,1)} %grad_ref.1), custom_call_target="tpu_custom_call" | custom-call | flops 1879048192 | bytes 5505024 | tf_op jit(solution)/shard_map/pallas_call | solution.py:80
  24.0 0.0 copy-done.4
  24.0 4.4 %all-to-all-done.in_ref = bf16[16,4,3584]{2,1,0:T(4,128)(2,1)S(1)} async-done(((bf16[16,4,3584]{2,1,0:T(4,128)(2,1)}), bf16[16,4,3584]{2,1,0:T(4,128)(2,1)S(1)}, u32[]{:S(2)}, u32[]{:S(2)}) %all-to-all-start) | async-done | bytes 458784 | tf_op jit(solution)/shard_map/all_to_all | solution.py:350
  28.4 0.9 shard_map.104
  29.3 0.0 all-gather.4.cloned.1.call-update
  29.3 0.0 reduce-scatter.2.cloned.1.call-start
  29.4 49.5 %all_to_all.15 = bf16[16,32,3584]{2,1,0:T(8,128)(2,1)} all-to-all(bf16[16,32,3584]{2,1,0:T(8,128)(2,1)} %bitcast.28), channel_id=1, replica_groups={{0,16,32,48,64,80,96,112,128,144,160,176,192,208,224,240},{8,24,40,56,7..., dimensions={0} | all-to-all | bytes 7340032 | tf_op jit(solution)/shard_map/all_to_all | solution.py:350
  78.9 0.3 all-gather.4.cloned.1.call-done
  79.2 16.8 %shard_map.105 = (bf16[8,256,896]{2,1,0:T(8,128)(2,1)}, bf16[1152,512]{1,0:T(8,128)(2,1)}) custom-call(bf16[16,2,16,3584]{3,2,1,0:T(8,128)(2,1)} %bitcast.18, bf16[8,2,32,3584]{3,2,1,0:T(8,128)(2,1)} %bitcast.21, bf16[192,3584]{1,0:T(8,128)(2,1)} %bitcast.34, bf16[192,3584]{1,0:T(8,128)(2,1)} %bitcast.36, bf16[192,3584]{1,0:T(8,128)(2,1)} %copy-done.4, ...), custom_call_target="tpu_custom_call" | custom-call | flops 7046430720 | bytes 19267584 | tf_op jit(solution)/shard_map/pallas_call | solution.py:214
  96.1 0.0 copy-start.2
  96.1 0.0 reduce-scatter.2.cloned.1.call-update
  96.1 1.2 copy-done.2
  97.3 0.0 copy-start
  97.3 2.0 %copy-done = bf16[16,32,3584]{2,1,0:T(8,128)(2,1)S(1)} copy-done((bf16[16,32,3584]{2,1,0:T(8,128)(2,1)S(1)}, bf16[16,32,3584]{2,1,0:T(8,128)(2,1)}, u32[]{:S(2)}) %copy-start) | copy-done | bytes 3670040
  99.4 0.0 copy-start.1
  99.4 2.0 %copy-done.1 = bf16[16,32,3584]{2,1,0:T(8,128)(2,1)S(1)} copy-done((bf16[16,32,3584]{2,1,0:T(8,128)(2,1)S(1)}, bf16[16,32,3584]{2,1,0:T(8,128)(2,1)}, u32[]{:S(2)}) %copy-start.1) | copy-done | bytes 3670040
  101.4 4.1 %shard_map.106 = bf16[576,3584]{1,0:T(8,128)(2,1)S(1)} custom-call(bf16[16,2,16,3584]{3,2,1,0:T(8,128)(2,1)S(1)} %bitcast.19, bf16[8,2,32,3584]{3,2,1,0:T(8,128)(2,1)S(1)} %bitcast.22, bf16[1152,512]{1,0:T(8,128)(2,1)S(1)} %copy-done.2), custom_call_target="tpu_custom_call" | custom-call | flops 2113929216 | bytes 15597568 | tf_op jit(solution)/shard_map/pallas_call | solution.py:289
  105.5 0.0 copy-start.3
  105.5 0.1 collective-permute-start.3
  105.6 7.1 %collective-permute-done.3.refs_0_ = bf16[576,3584]{1,0:T(8,128)(2,1)S(1)} collective-permute-done((bf16[576,3584]{1,0:T(8,128)(2,1)S(1)}, bf16[576,3584]{1,0:T(8,128)(2,1)S(1)}, u32[]{:S(2)}, u32[]{:S(2)}) %collective-permute-start.3) | collective-permute-done | bytes 4128800 | tf_op jit(solution)/shard_map/ppermute | solution.py:345
  112.6 4.9 %shard_map.107 = (bf16[192,3584]{1,0:T(8,128)(2,1)}, bf16[192,3584]{1,0:T(8,128)(2,1)}, bf16[192,3584]{1,0:T(8,128)(2,1)}) custom-call(bf16[16,2,16,3584]{3,2,1,0:T(8,128)(2,1)S(1)} %bitcast.20, bf16[8,2,32,3584]{3,2,1,0:T(8,128)(2,1)S(1)} %bitcast.23, bf16[1152,512]{1,0:T(8,128)(2,1)S(1)} %copy-done.2, bf16[576,3584]{1,0:T(8,128)(2,1)S(1)} %collective-permute-done.3.refs_0_), custom_call_target="tpu_custom_call" | custom-call | flops 2113929216 | bytes 15597568 | tf_op jit(solution)/shard_map/pallas_call | solution.py:289
  117.5 28.5 %reduce-scatter.2.cloned.1.call-done = bf16[1,256,896]{2,1,0:T(8,128)(2,1)} async-done(((bf16[8,256,896]{2,1,0:T(8,128)(2,1)}), bf16[1,256,896]{2,1,0:T(8,128)(2,1)}) %reduce-scatter.2.cloned.1.call-update) | async-done | bytes 458768 | tf_op jit(solution)/shard_map/reduce_scatter | solution.py:369
  146.0 16.8 %all_to_all.16.back_ref = bf16[16,16,896]{2,1,0:T(8,128)(2,1)S(1)} all-to-all(bf16[16,16,896]{2,1,0:T(8,128)(2,1)} %bitcast.30), channel_id=1, replica_groups={{0,16,32,48,64,80,96,112,128,144,160,176,192,208,224,240},{8,24,40,56,7..., dimensions={0} | all-to-all | bytes 917504 | tf_op jit(solution)/shard_map/all_to_all | solution.py:350
  162.7 0.0 copy-done.3
  162.7 0.5 shard_map.108
  163.2 27.1 %all-gather.1 = bf16[1024,448]{1,0:T(8,128)(2,1)S(1)} all-gather(bf16[128,448]{1,0:T(8,128)(2,1)S(1)} %shard_map.108), channel_id=3, replica_groups=mesh['exp'=32,'tp'=8] {'tp'}, dimensions={0}, use_global_device_ids=true | all-gather | bytes 1032192 | tf_op jit(solution)/shard_map/all_gather | solution.py:373
  190.4 0.6 copy.14
  191.0 1.3 copy.15
Async XLA Ops:
  7.2 11.2 %collective-permute-start = (bf16[192,3584]{1,0:T(8,128)(2,1)}, bf16[192,3584]{1,0:T(8,128)(2,1)S(1)}, u32[]{:S(2)}, u32[]{:S(2)}) collective-permute-start(bf16[192,3584]{1,0:T(8,128)(2,1)} %bitcast.33), channel_id=1, source_target_pairs={{0,8},{8,0},{16,24},{24,16},{32,40},{40,32},{48,56},{56,48},{64,72... | collective-permute-start | bytes 4128776 | tf_op jit(solution)/shard_map/ppermute | solution.py:345
  7.3 11.1 %collective-permute-start.1 = (bf16[192,3584]{1,0:T(8,128)(2,1)}, bf16[192,3584]{1,0:T(8,128)(2,1)}, u32[]{:S(2)}, u32[]{:S(2)}) collective-permute-start(bf16[192,3584]{1,0:T(8,128)(2,1)} %bitcast.35), channel_id=1, source_target_pairs={{0,8},{8,0},{16,24},{24,16},{32,40},{40,32},{48,56},{56,48},{64,72... | collective-permute-start | bytes 4128776 | tf_op jit(solution)/shard_map/ppermute | solution.py:345
  7.8 10.6 %collective-permute-start.2 = (bf16[192,3584]{1,0:T(8,128)(2,1)}, bf16[192,3584]{1,0:T(8,128)(2,1)}, u32[]{:S(2)}, u32[]{:S(2)}) collective-permute-start(bf16[192,3584]{1,0:T(8,128)(2,1)} %bitcast.37), channel_id=1, source_target_pairs={{0,8},{8,0},{16,24},{24,16},{32,40},{40,32},{48,56},{56,48},{64,72... | collective-permute-start | bytes 4128776 | tf_op jit(solution)/shard_map/ppermute | solution.py:345
  10.8 17.6 %all-to-all-start = ((bf16[16,4,3584]{2,1,0:T(4,128)(2,1)}), bf16[16,4,3584]{2,1,0:T(4,128)(2,1)S(1)}, u32[]{:S(2)}, u32[]{:S(2)}) async-start(bf16[16,4,3584]{2,1,0:T(4,128)(2,1)} %shard_map.102), calls=%async_computation | async-start | bytes 917504 | tf_op jit(solution)/shard_map/all_to_all | solution.py:350
  18.3 60.9 %all-gather.4.cloned.1.call-start = ((), (), s32[]{:S(2)}) async-start(), calls=%async_computation.5 | async-start | bytes 4128768 | tf_op jit(solution)/shard_map/all_gather | solution.py:362
  18.3 5.6 %copy-start.4 = (bf16[192,3584]{1,0:T(8,128)(2,1)}, bf16[192,3584]{1,0:T(8,128)(2,1)S(1)}, u32[]{:S(2)}) copy-start(bf16[192,3584]{1,0:T(8,128)(2,1)S(1)} %collective-permute-done.g1) | copy-start | bytes 4128772
  29.3 116.7 %reduce-scatter.2.cloned.1.call-start = ((), (), s32[]{:S(2)}) async-start(), calls=%async_computation.4 | async-start | bytes 4128768 | tf_op jit(solution)/shard_map/reduce_scatter | solution.py:369
  96.1 1.3 copy-start.2
  97.3 2.0 %copy-start = (bf16[16,32,3584]{2,1,0:T(8,128)(2,1)S(1)}, bf16[16,32,3584]{2,1,0:T(8,128)(2,1)}, u32[]{:S(2)}) copy-start(bf16[16,32,3584]{2,1,0:T(8,128)(2,1)} %all_to_all.15) | copy-start | bytes 11010052
  99.4 2.0 %copy-start.1 = (bf16[16,32,3584]{2,1,0:T(8,128)(2,1)S(1)}, bf16[16,32,3584]{2,1,0:T(8,128)(2,1)}, u32[]{:S(2)}) copy-start(bf16[16,32,3584]{2,1,0:T(8,128)(2,1)} %all-gather.4.cloned.1.call-done) | copy-start | bytes 11010052
  105.5 57.3 %copy-start.3 = (s32[128,2]{0,1:T(2,128)S(1)}, s32[128,2]{0,1:T(2,128)}, u32[]{:S(2)}) copy-start(s32[128,2]{0,1:T(2,128)} %param.9) | copy-start | bytes 3076
  105.5 7.2 %collective-permute-start.3 = (bf16[576,3584]{1,0:T(8,128)(2,1)S(1)}, bf16[576,3584]{1,0:T(8,128)(2,1)S(1)}, u32[]{:S(2)}, u32[]{:S(2)}) collective-permute-start(bf16[576,3584]{1,0:T(8,128)(2,1)S(1)} %shard_map.106), channel_id=1, source_target_pairs={{0,8},{8,0},{16,24},{24,16},{32,40},{40,32},{48,56},{56,48},{64,72... | collective-permute-start | bytes 12386312 | tf_op jit(solution)/shard_map/ppermute | solution.py:345
Sparse Core Ops, SparseCore 0:
  29.4 49.7 all-gather.3
  96.2 49.7 reduce-scatter.1

commit v8 on v7

--- a/solution.py
+++ b/solution.py
@@ -12,7 +12,7 @@
 VMEM = pltpu.VMEM
 LIMIT = 28 * 1024 * 1024
 WHOLE = 60 * 1024 * 1024
-PASS = 62 * 1024 * 1024
+PASS = 53 * 1024 * 1024
 
 
 def table(ids, experts):
@@ -149,22 +149,22 @@
         for i, ref in enumerate((g0, u0, g1, u1)):
             kept[at, i * units : (i + 1) * units] = ref[...]
         down = jnp.concatenate([d0[...], d1[...]], axis=0)
-        for i, ref in enumerate((far_ref, near_ref)):
-            rows = slice(i * half, (i + 1) * half)
-            x = ref[:, 0].reshape(half, -1)
-            g = ref[:, 1].reshape(half, -1)
-            pre = lax.dot_general(x, kept[at], contract, preferred_element_type=F32)
-            back = lax.dot_general(g, down, contract, preferred_element_type=F32)
-
-            @pl.when(at == 0)
-            def _():
-                pre_acc[rows] = pre
-                back_acc[rows] = back
-
-            @pl.when(at > 0)
-            def _():
-                pre_acc[rows] += pre
-                back_acc[rows] += back
+        x, g = [
+            jnp.concatenate([ref[:, k].reshape(half, -1) for ref in (far_ref, near_ref)], axis=0)
+            for k in range(2)
+        ]
+        pre = lax.dot_general(x, kept[at], contract, preferred_element_type=F32)
+        back = lax.dot_general(g, down, contract, preferred_element_type=F32)
+
+        @pl.when(at == 0)
+        def _():
+            pre_acc[...] = pre
+            back_acc[...] = back
+
+        @pl.when(at > 0)
+        def _():
+            pre_acc[...] += pre
+            back_acc[...] += back
 
     @pl.when((phase == 0) & (at == pl.num_programs(1) - 1))
     def _():
@@ -178,9 +178,9 @@
             d_gate = (back * pre_up * sig * (1.0 + pre_gate * (1.0 - sig))).astype(BF16)
             d_up = (back * silu).astype(BF16)
             base = 3 * i * units
-            side_ref[base : base + units] = d_gate.T
-            side_ref[base + units : base + 2 * units] = d_up.T
-            side_ref[base + 2 * units : base + 3 * units] = hidden.T
+            side_ref[:, base : base + units] = d_gate
+            side_ref[:, base + units : base + 2 * units] = d_up
+            side_ref[:, base + 2 * units : base + 3 * units] = hidden
             both_ref[:, 2 * i * units : (2 * i + 1) * units] = d_gate
             both_ref[:, (2 * i + 1) * units : (2 * i + 2) * units] = d_up
         outer, inner = near_ref.shape[0], near_ref.shape[2]
@@ -221,11 +221,11 @@
         + [pl.BlockSpec((units, tile), lambda p, i: (0, first_phase(p, i)))] * 6,
         out_specs=[
             pl.BlockSpec((pieces // steps, half, 2 * width // pieces), lambda p, i: (p * i, 0, 0)),
-            pl.BlockSpec((6 * units, 2 * half), lambda p, i: (0, 0)),
+            pl.BlockSpec((2 * half, 6 * units), lambda p, i: (0, 0)),
         ],
         out_shape=[
             pltpu.HBM((pieces, half, 2 * width // pieces), BF16),
-            jax.ShapeDtypeStruct((6 * units, 2 * half), BF16),
+            jax.ShapeDtypeStruct((2 * half, 6 * units), BF16),
         ],
         scratch_shapes=[
             VMEM((2 * half, 4 * units), F32),
@@ -244,7 +244,8 @@
 
 def weight_kernel(base, far_ref, near_ref, side_ref, *refs):
     tile = far_ref.shape[3]
-    units = side_ref.shape[0] // 6
+    units = side_ref.shape[1] // 6
+    contract = (((0,), (0,)), ((), ()))
     base = base * units
 
     def stacked(kind):
@@ -252,10 +253,10 @@
             [ref[:, kind].reshape(-1, tile) for ref in (far_ref, near_ref)], axis=0
         )
 
-    pair = jnp.dot(side_ref[base : base + 2 * units], stacked(0), preferred_element_type=F32)
-    down = jnp.dot(
-        side_ref[base + 2 * units : base + 3 * units], stacked(1), preferred_element_type=F32
-    )
+    left = side_ref[:, base : base + 2 * units]
+    pair = lax.dot_general(left, stacked(0), contract, preferred_element_type=F32)
+    left = side_ref[:, base + 2 * units : base + 3 * units]
+    down = lax.dot_general(left, stacked(1), contract, preferred_element_type=F32)
     if len(refs) == 1:
         refs[0][: 2 * units] = pair.astype(BF16)
         refs[0][2 * units :] = down.astype(BF16)
@@ -270,7 +271,7 @@
 
 def weight_grads(far, near, side, more):
     width = far.shape[3]
-    units = side.shape[0] // 6
+    units = side.shape[1] // 6
     tile = width // 4
     specs = [
         pl.BlockSpec(far.shape[:3] + (tile,), lambda i: (0, 0, 0, i)),
@@ -294,8 +295,8 @@
         out_shape=out_shape,
         compiler_params=pltpu.CompilerParams(vmem_limit_bytes=LIMIT),
         cost_estimate=pl.CostEstimate(
-            flops=6 * side.shape[1] * width * units,
-            bytes_accessed=2 * (2 * side.shape[1] * width + 6 * units * width),
+            flops=6 * side.shape[0] * width * units,
+            bytes_accessed=2 * (2 * side.shape[0] * width + 6 * units * width),
             transcendentals=0,
         ),
     )(*operands)

time: 200 us -> 198 us (0.990)
    unnamed x11 -> x13, local copies, waits for them, and re-layouts: 6.61 us -> 6.61 us
where the time goes in v8:
time: 198 us; the launch traced here: 197 us
  blocking collectives  93.4 us (47%)
  waiting for transfers between devices  39 us (20%)
  Pallas kernels  35.3 us (18%)
  between operations  14.2 us (7%)
  starting transfers between devices  8.35 us (4%)
  local copies, waits for them, and re-layouts  7.23 us (4%)
    all_to_all x2, blocking collectives, spread(): lax.all_to_all(v, 'exp', split_axis=0, concat_axis=0, tiled=True, axis_in...  66.3 us
    reduce_scatter x1, waiting for transfers between devices, per_device(): mine = lax.psum_scatter(both, 'tp', scatter_dimension=0, tiled=False)  27.3 us
    all_gather x1, blocking collectives, per_device(): gathered = lax.all_gather(piece, 'tp', axis=0, tiled=False)  27.1 us
    pallas_call x1, Pallas kernels, expert_part(): pl.pallas_call(expert_kernel, grid=(2, steps), in_specs=[pl.BlockSpec(src...  15.1 us
    pallas_call x2, Pallas kernels, weight_grads(): pl.pallas_call(functools.partial(weight_kernel, base), grid=(width // til...  10.1 us
    all_to_all x1, starting transfers between devices, spread(): lax.all_to_all(v, 'exp', split_axis=0, concat_axis=0, tiled=True, axis_in...  7.49 us
    ppermute x4, waiting for transfers between devices, trade(): return lax.ppermute(v, 'exp', swap)  7.06 us
    unnamed x13, local copies, waits for them, and re-layouts  6.61 us
  transfers between devices with their start and end apart: 7, of which 4 were waited for; matrix products, arithmetic and copies ran while one was open for 0% of the time, Pallas kernels for 9%

profile of v8, /device:TPU:2, one launch (start us, length us, event | category | flops | bytes accessed | tf_op | source)
XLA Modules:
  0.0 197.4 jit_solution(11935287240102662646)
XLA Ops:
  7.2 0.1 collective-permute-start
  7.3 0.5 collective-permute-start.1
  7.8 0.1 collective-permute-start.2
  7.9 2.9 %shard_map.102 = bf16[16,4,3584]{2,1,0:T(4,128)(2,1)} custom-call(s32[1]{0:T(128)} %bitcast.4.tp_ref, s32[2,128]{1,0:T(2,128)} %bitcast.24, f32[2,128]{1,0:T(2,128)} %bitcast.31, bf16[128,3584]{1,0:T(8,128)(2,1)} %act_ref.1, bf16[128,3584]{1,0:T(8,128)(2,1)} %grad_ref.1), custom_call_target="tpu_custom_call" | custom-call | tf_op jit(solution)/shard_map/pallas_call | solution.py:102
  10.8 7.5 %all-to-all-start = ((bf16[16,4,3584]{2,1,0:T(4,128)(2,1)}), bf16[16,4,3584]{2,1,0:T(4,128)(2,1)S(1)}, u32[]{:S(2)}, u32[]{:S(2)}) async-start(bf16[16,4,3584]{2,1,0:T(4,128)(2,1)} %shard_map.102), calls=%async_computation | async-start | bytes 917504 | tf_op jit(solution)/shard_map/all_to_all | solution.py:351
  18.3 0.0 all-gather.4.cloned.1.call-start
  18.3 0.0 collective-permute-done.g1
  18.3 0.0 copy-start.4
  18.4 0.0 collective-permute-done.1.u1
  18.4 0.0 copy-start.5
  18.4 0.0 collective-permute-done.2.d1
  18.4 5.7 %shard_map.103 = bf16[16,2,16,3584]{3,2,1,0:T(8,128)(2,1)} custom-call(s32[2,128]{1,0:T(2,128)} %bitcast.25, f32[2,128]{1,0:T(2,128)} %bitcast.32, bf16[128,3584]{1,0:T(8,128)(2,1)} %act_ref.1, bf16[128,3584]{1,0:T(8,128)(2,1)} %grad_ref.1), custom_call_target="tpu_custom_call" | custom-call | flops 1879048192 | bytes 5505024 | tf_op jit(solution)/shard_map/pallas_call | solution.py:80
  24.1 0.0 copy-done.4
  24.1 0.0 copy-done.5
  24.1 4.2 %all-to-all-done.in_ref = bf16[16,4,3584]{2,1,0:T(4,128)(2,1)S(1)} async-done(((bf16[16,4,3584]{2,1,0:T(4,128)(2,1)}), bf16[16,4,3584]{2,1,0:T(4,128)(2,1)S(1)}, u32[]{:S(2)}, u32[]{:S(2)}) %all-to-all-start) | async-done | bytes 458784 | tf_op jit(solution)/shard_map/all_to_all | solution.py:351
  28.4 0.9 shard_map.104
  29.3 0.0 all-gather.4.cloned.1.call-update
  29.3 0.0 reduce-scatter.2.cloned.1.call-start
  29.4 49.5 %all_to_all.15 = bf16[16,32,3584]{2,1,0:T(8,128)(2,1)} all-to-all(bf16[16,32,3584]{2,1,0:T(8,128)(2,1)} %bitcast.28), channel_id=1, replica_groups={{0,16,32,48,64,80,96,112,128,144,160,176,192,208,224,240},{8,24,40,56,7..., dimensions={0} | all-to-all | bytes 7340032 | tf_op jit(solution)/shard_map/all_to_all | solution.py:351
  78.9 0.3 all-gather.4.cloned.1.call-done
  79.2 15.1 %shard_map.105 = (bf16[8,256,896]{2,1,0:T(8,128)(2,1)}, bf16[512,1152]{1,0:T(8,128)(2,1)}) custom-call(bf16[16,2,16,3584]{3,2,1,0:T(8,128)(2,1)} %bitcast.18, bf16[8,2,32,3584]{3,2,1,0:T(8,128)(2,1)} %bitcast.21, bf16[192,3584]{1,0:T(8,128)(2,1)} %bitcast.34, bf16[192,3584]{1,0:T(8,128)(2,1)} %bitcast.36, bf16[192,3584]{1,0:T(8,128)(2,1)} %copy-done.4, ...), custom_call_target="tpu_custom_call" | custom-call | flops 7046430720 | bytes 19267584 | tf_op jit(solution)/shard_map/pallas_call | solution.py:214
  94.3 0.0 copy-start.2
  94.3 0.0 reduce-scatter.2.cloned.1.call-update
  94.3 1.2 copy-done.2
  95.6 0.0 copy-start
  95.6 2.0 %copy-done = bf16[16,32,3584]{2,1,0:T(8,128)(2,1)S(1)} copy-done((bf16[16,32,3584]{2,1,0:T(8,128)(2,1)S(1)}, bf16[16,32,3584]{2,1,0:T(8,128)(2,1)}, u32[]{:S(2)}) %copy-start) | copy-done | bytes 3670040
  97.6 0.0 copy-start.1
  97.6 2.0 %copy-done.1 = bf16[16,32,3584]{2,1,0:T(8,128)(2,1)S(1)} copy-done((bf16[16,32,3584]{2,1,0:T(8,128)(2,1)S(1)}, bf16[16,32,3584]{2,1,0:T(8,128)(2,1)}, u32[]{:S(2)}) %copy-start.1) | copy-done | bytes 3670040
  99.7 5.1 %shard_map.106 = bf16[576,3584]{1,0:T(8,128)(2,1)S(1)} custom-call(bf16[16,2,16,3584]{3,2,1,0:T(8,128)(2,1)S(1)} %bitcast.19, bf16[8,2,32,3584]{3,2,1,0:T(8,128)(2,1)S(1)} %bitcast.22, bf16[512,1152]{1,0:T(8,128)(2,1)S(1)} %copy-done.2), custom_call_target="tpu_custom_call" | custom-call | flops 2113929216 | bytes 15597568 | tf_op jit(solution)/shard_map/pallas_call | solution.py:290
  104.7 0.0 copy-start.3
  104.8 0.1 collective-permute-start.3
  104.9 7.1 %collective-permute-done.3.refs_0_ = bf16[576,3584]{1,0:T(8,128)(2,1)S(1)} collective-permute-done((bf16[576,3584]{1,0:T(8,128)(2,1)S(1)}, bf16[576,3584]{1,0:T(8,128)(2,1)S(1)}, u32[]{:S(2)}, u32[]{:S(2)}) %collective-permute-start.3) | collective-permute-done | bytes 4128800 | tf_op jit(solution)/shard_map/ppermute | solution.py:346
  111.9 5.0 %shard_map.107 = (bf16[192,3584]{1,0:T(8,128)(2,1)}, bf16[192,3584]{1,0:T(8,128)(2,1)}, bf16[192,3584]{1,0:T(8,128)(2,1)}) custom-call(bf16[16,2,16,3584]{3,2,1,0:T(8,128)(2,1)S(1)} %bitcast.20, bf16[8,2,32,3584]{3,2,1,0:T(8,128)(2,1)S(1)} %bitcast.23, bf16[512,1152]{1,0:T(8,128)(2,1)S(1)} %copy-done.2, bf16[576,3584]{1,0:T(8,128)(2,1)S(1)} %collective-permute-done.3.refs_0_), custom_call_target="tpu_custom_call" | custom-call | flops 2113929216 | bytes 15597568 | tf_op jit(solution)/shard_map/pallas_call | solution.py:290
  116.9 27.3 %reduce-scatter.2.cloned.1.call-done = bf16[1,256,896]{2,1,0:T(8,128)(2,1)} async-done(((bf16[8,256,896]{2,1,0:T(8,128)(2,1)}), bf16[1,256,896]{2,1,0:T(8,128)(2,1)}) %reduce-scatter.2.cloned.1.call-update) | async-done | bytes 458768 | tf_op jit(solution)/shard_map/reduce_scatter | solution.py:370
  144.2 16.7 %all_to_all.16.back_ref = bf16[16,16,896]{2,1,0:T(8,128)(2,1)S(1)} all-to-all(bf16[16,16,896]{2,1,0:T(8,128)(2,1)} %bitcast.30), channel_id=1, replica_groups={{0,16,32,48,64,80,96,112,128,144,160,176,192,208,224,240},{8,24,40,56,7..., dimensions={0} | all-to-all | bytes 917504 | tf_op jit(solution)/shard_map/all_to_all | solution.py:351
  161.0 0.0 copy-done.3
  161.0 0.5 shard_map.108
  161.5 27.1 %all-gather.1 = bf16[1024,448]{1,0:T(8,128)(2,1)S(1)} all-gather(bf16[128,448]{1,0:T(8,128)(2,1)S(1)} %shard_map.108), channel_id=3, replica_groups=mesh['exp'=32,'tp'=8] {'tp'}, dimensions={0}, use_global_device_ids=true | all-gather | bytes 1032192 | tf_op jit(solution)/shard_map/all_gather | solution.py:374
  188.6 0.6 copy.14
  189.3 1.3 copy.15
Async XLA Ops:
  7.2 11.2 %collective-permute-start = (bf16[192,3584]{1,0:T(8,128)(2,1)}, bf16[192,3584]{1,0:T(8,128)(2,1)S(1)}, u32[]{:S(2)}, u32[]{:S(2)}) collective-permute-start(bf16[192,3584]{1,0:T(8,128)(2,1)} %bitcast.33), channel_id=1, source_target_pairs={{0,8},{8,0},{16,24},{24,16},{32,40},{40,32},{48,56},{56,48},{64,72... | collective-permute-start | bytes 4128776 | tf_op jit(solution)/shard_map/ppermute | solution.py:346
  7.3 11.1 %collective-permute-start.1 = (bf16[192,3584]{1,0:T(8,128)(2,1)}, bf16[192,3584]{1,0:T(8,128)(2,1)S(1)}, u32[]{:S(2)}, u32[]{:S(2)}) collective-permute-start(bf16[192,3584]{1,0:T(8,128)(2,1)} %bitcast.35), channel_id=1, source_target_pairs={{0,8},{8,0},{16,24},{24,16},{32,40},{40,32},{48,56},{56,48},{64,72... | collective-permute-start | bytes 4128776 | tf_op jit(solution)/shard_map/ppermute | solution.py:346
  7.8 10.6 %collective-permute-start.2 = (bf16[192,3584]{1,0:T(8,128)(2,1)}, bf16[192,3584]{1,0:T(8,128)(2,1)}, u32[]{:S(2)}, u32[]{:S(2)}) collective-permute-start(bf16[192,3584]{1,0:T(8,128)(2,1)} %bitcast.37), channel_id=1, source_target_pairs={{0,8},{8,0},{16,24},{24,16},{32,40},{40,32},{48,56},{56,48},{64,72... | collective-permute-start | bytes 4128776 | tf_op jit(solution)/shard_map/ppermute | solution.py:346
  10.8 17.6 %all-to-all-start = ((bf16[16,4,3584]{2,1,0:T(4,128)(2,1)}), bf16[16,4,3584]{2,1,0:T(4,128)(2,1)S(1)}, u32[]{:S(2)}, u32[]{:S(2)}) async-start(bf16[16,4,3584]{2,1,0:T(4,128)(2,1)} %shard_map.102), calls=%async_computation | async-start | bytes 917504 | tf_op jit(solution)/shard_map/all_to_all | solution.py:351
  18.3 60.9 %all-gather.4.cloned.1.call-start = ((), (), s32[]{:S(2)}) async-start(), calls=%async_computation.5 | async-start | bytes 4128768 | tf_op jit(solution)/shard_map/all_gather | solution.py:363
  18.3 5.8 %copy-start.4 = (bf16[192,3584]{1,0:T(8,128)(2,1)}, bf16[192,3584]{1,0:T(8,128)(2,1)S(1)}, u32[]{:S(2)}) copy-start(bf16[192,3584]{1,0:T(8,128)(2,1)S(1)} %collective-permute-done.g1) | copy-start | bytes 4128772
  18.4 5.7 %copy-start.5 = (bf16[192,3584]{1,0:T(8,128)(2,1)}, bf16[192,3584]{1,0:T(8,128)(2,1)S(1)}, u32[]{:S(2)}) copy-start(bf16[192,3584]{1,0:T(8,128)(2,1)S(1)} %collective-permute-done.1.u1) | copy-start | bytes 4128772
  29.3 114.9 %reduce-scatter.2.cloned.1.call-start = ((), (), s32[]{:S(2)}) async-start(), calls=%async_computation.4 | async-start | bytes 4128768 | tf_op jit(solution)/shard_map/reduce_scatter | solution.py:370
  94.3 1.3 copy-start.2
  95.6 2.0 %copy-start = (bf16[16,32,3584]{2,1,0:T(8,128)(2,1)S(1)}, bf16[16,32,3584]{2,1,0:T(8,128)(2,1)}, u32[]{:S(2)}) copy-start(bf16[16,32,3584]{2,1,0:T(8,128)(2,1)} %all_to_all.15) | copy-start | bytes 11010052
  97.6 2.0 %copy-start.1 = (bf16[16,32,3584]{2,1,0:T(8,128)(2,1)S(1)}, bf16[16,32,3584]{2,1,0:T(8,128)(2,1)}, u32[]{:S(2)}) copy-start(bf16[16,32,3584]{2,1,0:T(8,128)(2,1)} %all-gather.4.cloned.1.call-done) | copy-start | bytes 11010052
  104.7 56.3 %copy-start.3 = (s32[128,2]{0,1:T(2,128)S(1)}, s32[128,2]{0,1:T(2,128)}, u32[]{:S(2)}) copy-start(s32[128,2]{0,1:T(2,128)} %param.9) | copy-start | bytes 3076
  104.8 7.2 %collective-permute-start.3 = (bf16[576,3584]{1,0:T(8,128)(2,1)S(1)}, bf16[576,3584]{1,0:T(8,128)(2,1)S(1)}, u32[]{:S(2)}, u32[]{:S(2)}) collective-permute-start(bf16[576,3584]{1,0:T(8,128)(2,1)S(1)} %shard_map.106), channel_id=1, source_target_pairs={{0,8},{8,0},{16,24},{24,16},{32,40},{40,32},{48,56},{56,48},{64,72... | collective-permute-start | bytes 12386312 | tf_op jit(solution)/shard_map/ppermute | solution.py:346
Sparse Core Ops, SparseCore 0:
  29.4 49.7 all-gather.3
  94.5 49.7 reduce-scatter.1

commit v9 on v8

--- a/solution.py
+++ b/solution.py
@@ -330,6 +330,45 @@
     )(ids_t, returned)
 
 
+def order_kernel(tp_ref, *refs):
+    pieces, out_ref, kept = refs[:-2], refs[-2], refs[-1]
+    count, toks, wide = kept.shape
+    reach = count // 2 - 1
+    me = tp_ref[0]
+    kept[me] = pieces[0][...]
+    for step in range(1, reach + 1):
+        kept[lax.rem(me + count - step, count)] = pieces[2 * step - 1][...]
+        kept[lax.rem(me + step, count)] = pieces[2 * step][...]
+    far = lax.rem(me + count // 2, count)
+    kept[far, : toks // 2] = pieces[-2][...]
+    kept[far, toks // 2 :] = pieces[-1][...]
+    for k in range(0, count, 2):
+        out_ref[:, k * wide : (k + 2) * wide] = jnp.concatenate([kept[k], kept[k + 1]], axis=1)
+
+
+def gather_columns(tp_at, piece, count):
+    toks, wide = piece.shape
+    up = [(i, (i + 1) % count) for i in range(count)]
+    down = [(i, (i - 1) % count) for i in range(count)]
+    from_below, from_above = piece, piece
+    pieces = [piece]
+    for _ in range(count // 2 - 1):
+        from_below = lax.ppermute(from_below, "tp", up)
+        from_above = lax.ppermute(from_above, "tp", down)
+        pieces += [from_below, from_above]
+    pieces.append(lax.ppermute(from_below[: toks // 2], "tp", up))
+    pieces.append(lax.ppermute(from_above[toks // 2 :], "tp", down))
+    return pl.pallas_call(
+        order_kernel,
+        in_specs=[pl.BlockSpec(memory_space=pltpu.SMEM)]
+        + [pl.BlockSpec(memory_space=VMEM)] * len(pieces),
+        out_specs=pl.BlockSpec(memory_space=VMEM),
+        out_shape=jax.ShapeDtypeStruct((toks, count * wide), BF16),
+        scratch_shapes=[VMEM((count, toks, wide), BF16)],
+        compiler_params=pltpu.CompilerParams(vmem_limit_bytes=LIMIT),
+    )(tp_at, *pieces)
+
+
 def per_device(activations, out_grad, expert_ids, gate_values, gate_proj, up_proj, down_proj):
     devices = lax.axis_size("exp")
     planes = lax.axis_size("tp")
@@ -371,8 +410,7 @@
     mine, gate_g, up_g, down_g = lax.optimization_barrier((mine, gate_g, up_g, down_g))
     returned = spread(mine.reshape(experts, half, -1))
     piece = combine(ids_t, returned)
-    gathered = lax.all_gather(piece, "tp", axis=0, tiled=False)
-    in_grad = jnp.transpose(gathered, (1, 0, 2)).reshape(toks, width)
+    in_grad = gather_columns(tp_at, piece, planes)
     return (in_grad, gate_g[None], up_g[None], down_g[None])
 
 

time: 198 us -> 197 us (level)
  blocking collectives: 93.4 us -> 66.2 us
  waiting for transfers between devices: 39 us -> 53.5 us
  starting transfers between devices: 8.35 us -> 20.2 us
    all_gather x1 -> x0, blocking collectives: 27.1 us -> none  [per_device(): gathered = lax.all_gather(piece, 'tp', axis=0, tiled=False)]
    ppermute x0 -> x8, waiting for transfers between devices: none -> 14.6 us  [the longest x3 9.07 us: gather_columns(): from_above = lax.ppermute(from_above, 'tp', down)]
    ppermute x0 -> x8, starting transfers between devices: none -> 11.8 us  [the longest x3 7.41 us: gather_columns(): from_above = lax.ppermute(from_above, 'tp', down)]
    unnamed x13 -> x12, local copies, waits for them, and re-layouts: 6.61 us -> 5.34 us
  transfers between devices with their start and end apart: 7 -> 15, of which waited for: 4 -> 9; matrix products, arithmetic and copies ran while one was open for 0% -> 0% of each run, Pallas kernels for 9% -> 10%
where the time goes in v9:
time: 197 us; the launch traced here: 196 us
  blocking collectives  66.2 us (34%)
  waiting for transfers between devices  53.5 us (27%)
  Pallas kernels  36.5 us (19%)
  starting transfers between devices  20.2 us (10%)
  between operations  14.2 us (7%)
  local copies, waits for them, and re-layouts  5.35 us (3%)
    all_to_all x2, blocking collectives, spread(): lax.all_to_all(v, 'exp', split_axis=0, concat_axis=0, tiled=True, axis_in...  66.2 us
    reduce_scatter x1, waiting for transfers between devices, per_device(): mine = lax.psum_scatter(both, 'tp', scatter_dimension=0, tiled=False)  27.3 us
    pallas_call x1, Pallas kernels, expert_part(): pl.pallas_call(expert_kernel, grid=(2, steps), in_specs=[pl.BlockSpec(src...  15.1 us
    pallas_call x2, Pallas kernels, weight_grads(): pl.pallas_call(functools.partial(weight_kernel, base), grid=(width // til...  10.1 us
    ppermute x3, waiting for transfers between devices, gather_columns(): from_above = lax.ppermute(from_above, 'tp', down)  9.07 us
    all_to_all x1, starting transfers between devices, spread(): lax.all_to_all(v, 'exp', split_axis=0, concat_axis=0, tiled=True, axis_in...  7.49 us
    ppermute x3, starting transfers between devices, gather_columns(): from_above = lax.ppermute(from_above, 'tp', down)  7.41 us
    ppermute x4, waiting for transfers between devices, trade(): return lax.ppermute(v, 'exp', swap)  7.06 us
  transfers between devices with their start and end apart: 15, of which 9 were waited for; matrix products, arithmetic and copies ran while one was open for 0% of the time, Pallas kernels for 10%

profile of v9, /device:TPU:2, one launch (start us, length us, event | category | flops | bytes accessed | tf_op | source)
XLA Modules:
  0.0 196.0 jit_solution(10678868150515030216)
XLA Ops:
  7.2 0.1 collective-permute-start
  7.3 0.5 collective-permute-start.1
  7.8 0.1 collective-permute-start.2
  7.9 2.9 %shard_map.102 = bf16[16,4,3584]{2,1,0:T(4,128)(2,1)} custom-call(s32[1]{0:T(128)} %bitcast.tp_ref, s32[2,128]{1,0:T(2,128)} %bitcast.20, f32[2,128]{1,0:T(2,128)} %bitcast.25, bf16[128,3584]{1,0:T(8,128)(2,1)} %act_ref.1, bf16[128,3584]{1,0:T(8,128)(2,1)} %grad_ref.1), custom_call_target="tpu_custom_call" | custom-call | tf_op jit(solution)/shard_map/pallas_call | solution.py:102
  10.8 7.5 %all-to-all-start = ((bf16[16,4,3584]{2,1,0:T(4,128)(2,1)}), bf16[16,4,3584]{2,1,0:T(4,128)(2,1)S(1)}, u32[]{:S(2)}, u32[]{:S(2)}) async-start(bf16[16,4,3584]{2,1,0:T(4,128)(2,1)} %shard_map.102), calls=%async_computation | async-start | bytes 917504 | tf_op jit(solution)/shard_map/all_to_all | solution.py:390
  18.3 0.0 all-gather.3.cloned.1.call-start
  18.3 0.0 collective-permute-done.g1
  18.3 0.0 copy-start.4
  18.4 0.0 copy-start.5
  18.4 0.0 collective-permute-done.2.d1
  18.4 5.8 %shard_map.103 = bf16[16,2,16,3584]{3,2,1,0:T(8,128)(2,1)} custom-call(s32[2,128]{1,0:T(2,128)} %bitcast.21, f32[2,128]{1,0:T(2,128)} %bitcast.26, bf16[128,3584]{1,0:T(8,128)(2,1)} %act_ref.1, bf16[128,3584]{1,0:T(8,128)(2,1)} %grad_ref.1), custom_call_target="tpu_custom_call" | custom-call | flops 1879048192 | bytes 5505024 | tf_op jit(solution)/shard_map/pallas_call | solution.py:80
  24.2 4.2 %all-to-all-done.in_ref = bf16[16,4,3584]{2,1,0:T(4,128)(2,1)S(1)} async-done(((bf16[16,4,3584]{2,1,0:T(4,128)(2,1)}), bf16[16,4,3584]{2,1,0:T(4,128)(2,1)S(1)}, u32[]{:S(2)}, u32[]{:S(2)}) %all-to-all-start) | async-done | bytes 458784 | tf_op jit(solution)/shard_map/all_to_all | solution.py:390
  28.4 0.9 shard_map.104
  29.3 0.0 all-gather.3.cloned.1.call-update
  29.3 0.0 reduce-scatter.2.cloned.1.call-start
  29.4 49.5 %all_to_all.15 = bf16[16,32,3584]{2,1,0:T(8,128)(2,1)} all-to-all(bf16[16,32,3584]{2,1,0:T(8,128)(2,1)} %bitcast.23), channel_id=1, replica_groups={{0,16,32,48,64,80,96,112,128,144,160,176,192,208,224,240},{8,24,40,56,7..., dimensions={0} | all-to-all | bytes 7340032 | tf_op jit(solution)/shard_map/all_to_all | solution.py:390
  78.9 0.3 all-gather.3.cloned.1.call-done
  79.2 15.1 %shard_map.105 = (bf16[8,256,896]{2,1,0:T(8,128)(2,1)}, bf16[512,1152]{1,0:T(8,128)(2,1)}) custom-call(bf16[16,2,16,3584]{3,2,1,0:T(8,128)(2,1)} %bitcast.14, bf16[8,2,32,3584]{3,2,1,0:T(8,128)(2,1)} %bitcast.17, bf16[192,3584]{1,0:T(8,128)(2,1)} %bitcast.28, bf16[192,3584]{1,0:T(8,128)(2,1)} %bitcast.30, bf16[192,3584]{1,0:T(8,128)(2,1)} %copy-done.4, ...), custom_call_target="tpu_custom_call" | custom-call | flops 7046430720 | bytes 19267584 | tf_op jit(solution)/shard_map/pallas_call | solution.py:214
  94.3 0.0 copy-start.2
  94.3 0.0 reduce-scatter.2.cloned.1.call-update
  94.4 1.2 copy-done.2
  95.6 2.0 %copy-done = bf16[16,32,3584]{2,1,0:T(8,128)(2,1)S(1)} copy-done((bf16[16,32,3584]{2,1,0:T(8,128)(2,1)S(1)}, bf16[16,32,3584]{2,1,0:T(8,128)(2,1)}, u32[]{:S(2)}) %copy-start) | copy-done | bytes 3670040
  97.6 2.0 %copy-done.1 = bf16[16,32,3584]{2,1,0:T(8,128)(2,1)S(1)} copy-done((bf16[16,32,3584]{2,1,0:T(8,128)(2,1)S(1)}, bf16[16,32,3584]{2,1,0:T(8,128)(2,1)}, u32[]{:S(2)}) %copy-start.1) | copy-done | bytes 3670040
  99.7 5.1 %shard_map.106 = bf16[576,3584]{1,0:T(8,128)(2,1)S(1)} custom-call(bf16[16,2,16,3584]{3,2,1,0:T(8,128)(2,1)S(1)} %bitcast.15, bf16[8,2,32,3584]{3,2,1,0:T(8,128)(2,1)S(1)} %bitcast.18, bf16[512,1152]{1,0:T(8,128)(2,1)S(1)} %copy-done.2), custom_call_target="tpu_custom_call" | custom-call | flops 2113929216 | bytes 15597568 | tf_op jit(solution)/shard_map/pallas_call | solution.py:290
  104.8 0.0 copy-start.3
  104.8 0.1 collective-permute-start.3
  104.9 7.1 %collective-permute-done.3.refs_0_ = bf16[576,3584]{1,0:T(8,128)(2,1)S(1)} collective-permute-done((bf16[576,3584]{1,0:T(8,128)(2,1)S(1)}, bf16[576,3584]{1,0:T(8,128)(2,1)S(1)}, u32[]{:S(2)}, u32[]{:S(2)}) %collective-permute-start.3) | collective-permute-done | bytes 4128800 | tf_op jit(solution)/shard_map/ppermute | solution.py:385
  111.9 5.0 %shard_map.107 = (bf16[192,3584]{1,0:T(8,128)(2,1)}, bf16[192,3584]{1,0:T(8,128)(2,1)}, bf16[192,3584]{1,0:T(8,128)(2,1)}) custom-call(bf16[16,2,16,3584]{3,2,1,0:T(8,128)(2,1)S(1)} %bitcast.16, bf16[8,2,32,3584]{3,2,1,0:T(8,128)(2,1)S(1)} %bitcast.19, bf16[512,1152]{1,0:T(8,128)(2,1)S(1)} %copy-done.2, bf16[576,3584]{1,0:T(8,128)(2,1)S(1)} %collective-permute-done.3.refs_0_), custom_call_target="tpu_custom_call" | custom-call | flops 2113929216 | bytes 15597568 | tf_op jit(solution)/shard_map/pallas_call | solution.py:290
  116.9 27.3 %reduce-scatter.2.cloned.1.call-done = bf16[1,256,896]{2,1,0:T(8,128)(2,1)} async-done(((bf16[8,256,896]{2,1,0:T(8,128)(2,1)}), bf16[1,256,896]{2,1,0:T(8,128)(2,1)}) %reduce-scatter.2.cloned.1.call-update) | async-done | bytes 458768 | tf_op jit(solution)/shard_map/reduce_scatter | solution.py:409
  144.2 16.7 %all_to_all.16.back_ref = bf16[16,16,896]{2,1,0:T(8,128)(2,1)S(1)} all-to-all(bf16[16,16,896]{2,1,0:T(8,128)(2,1)} %bitcast.24), channel_id=1, replica_groups={{0,16,32,48,64,80,96,112,128,144,160,176,192,208,224,240},{8,24,40,56,7..., dimensions={0} | all-to-all | bytes 917504 | tf_op jit(solution)/shard_map/all_to_all | solution.py:390
  161.0 0.5 shard_map.108.refs_0_
  161.5 1.6 collective-permute-start.5
  163.1 0.7 collective-permute-start.4
  163.8 2.9 %collective-permute-done.5.refs_2_ = bf16[128,448]{1,0:T(8,128)(2,1)S(1)} collective-permute-done((bf16[128,448]{1,0:T(8,128)(2,1)S(1)}, bf16[128,448]{1,0:T(8,128)(2,1)S(1)}, u32[]{:S(2)}, u32[]{:S(2)}) %collective-permute-start.5) | collective-permute-done | bytes 114720 | tf_op jit(solution)/shard_map/ppermute | solution.py:357
  166.7 2.6 %collective-permute-start.7 = (bf16[128,448]{1,0:T(8,128)(2,1)S(1)}, bf16[128,448]{1,0:T(8,128)(2,1)S(1)}, u32[]{:S(2)}, u32[]{:S(2)}) collective-permute-start(bf16[128,448]{1,0:T(8,128)(2,1)S(1)} %collective-permute-done.5.refs_2_), channel_id=1, source_target_pairs={{0,7},{1,0},{2,1},{3,2},{4,3},{5,4},{6,5},{7,6},{8,15},{9,8},{10,9... | collective-permute-start | bytes 344072 | tf_op jit(solution)/shard_map/ppermute | solution.py:357
  169.3 0.0 collective-permute-done.4.refs_1_
  169.3 0.0 collective-permute-start.6
  169.3 3.0 %collective-permute-done.7.refs_4_ = bf16[128,448]{1,0:T(8,128)(2,1)S(1)} collective-permute-done((bf16[128,448]{1,0:T(8,128)(2,1)S(1)}, bf16[128,448]{1,0:T(8,128)(2,1)S(1)}, u32[]{:S(2)}, u32[]{:S(2)}) %collective-permute-start.7) | collective-permute-done | bytes 114720 | tf_op jit(solution)/shard_map/ppermute | solution.py:357
  172.3 3.2 %collective-permute-start.9 = (bf16[128,448]{1,0:T(8,128)(2,1)S(1)}, bf16[128,448]{1,0:T(8,128)(2,1)S(1)}, u32[]{:S(2)}, u32[]{:S(2)}) collective-permute-start(bf16[128,448]{1,0:T(8,128)(2,1)S(1)} %collective-permute-done.7.refs_4_), channel_id=1, source_target_pairs={{0,7},{1,0},{2,1},{3,2},{4,3},{5,4},{6,5},{7,6},{8,15},{9,8},{10,9... | collective-permute-start | bytes 344072 | tf_op jit(solution)/shard_map/ppermute | solution.py:357
  175.5 0.0 collective-permute-done.6.refs_3_
  175.5 0.0 collective-permute-start.8
  175.5 3.1 %collective-permute-done.9.refs_6_ = bf16[128,448]{1,0:T(8,128)(2,1)S(1)} collective-permute-done((bf16[128,448]{1,0:T(8,128)(2,1)S(1)}, bf16[128,448]{1,0:T(8,128)(2,1)S(1)}, u32[]{:S(2)}, u32[]{:S(2)}) %collective-permute-start.9) | collective-permute-done | bytes 114720 | tf_op jit(solution)/shard_map/ppermute | solution.py:357
  178.7 3.7 %collective-permute-start.11 = (bf16[64,448]{1,0:T(8,128)(2,1)S(1)}, bf16[64,448]{1,0:T(8,128)(2,1)S(1)}, u32[]{:S(2)}, u32[]{:S(2)}) collective-permute-start(bf16[64,448]{1,0:T(8,128)(2,1)S(1)} %slice.9), channel_id=1, source_target_pairs={{0,7},{1,0},{2,1},{3,2},{4,3},{5,4},{6,5},{7,6},{8,15},{9,8},{10,9... | collective-permute-start | bytes 172040 | tf_op jit(solution)/shard_map/ppermute | solution.py:360
  182.4 0.0 collective-permute-done.8.refs_5_
  182.4 0.1 collective-permute-start.10
  182.5 1.8 collective-permute-done.11.refs_8_
  184.3 3.7 %collective-permute-done.10.refs_7_ = bf16[64,448]{1,0:T(8,128)(2,1)S(1)} collective-permute-done((bf16[64,448]{1,0:T(8,128)(2,1)S(1)}, bf16[64,448]{1,0:T(8,128)(2,1)S(1)}, u32[]{:S(2)}, u32[]{:S(2)}) %collective-permute-start.10) | collective-permute-done | bytes 57376 | tf_op jit(solution)/shard_map/ppermute | solution.py:359
  187.9 1.2 shard_map.109
  (8 shorter events, 0.0 us)
Async XLA Ops:
  7.2 11.2 %collective-permute-start = (bf16[192,3584]{1,0:T(8,128)(2,1)}, bf16[192,3584]{1,0:T(8,128)(2,1)S(1)}, u32[]{:S(2)}, u32[]{:S(2)}) collective-permute-start(bf16[192,3584]{1,0:T(8,128)(2,1)} %bitcast.27), channel_id=1, source_target_pairs={{0,8},{8,0},{16,24},{24,16},{32,40},{40,32},{48,56},{56,48},{64,72... | collective-permute-start | bytes 4128776 | tf_op jit(solution)/shard_map/ppermute | solution.py:385
  7.3 11.1 %collective-permute-start.1 = (bf16[192,3584]{1,0:T(8,128)(2,1)}, bf16[192,3584]{1,0:T(8,128)(2,1)S(1)}, u32[]{:S(2)}, u32[]{:S(2)}) collective-permute-start(bf16[192,3584]{1,0:T(8,128)(2,1)} %bitcast.29), channel_id=1, source_target_pairs={{0,8},{8,0},{16,24},{24,16},{32,40},{40,32},{48,56},{56,48},{64,72... | collective-permute-start | bytes 4128776 | tf_op jit(solution)/shard_map/ppermute | solution.py:385
  7.8 10.6 %collective-permute-start.2 = (bf16[192,3584]{1,0:T(8,128)(2,1)}, bf16[192,3584]{1,0:T(8,128)(2,1)}, u32[]{:S(2)}, u32[]{:S(2)}) collective-permute-start(bf16[192,3584]{1,0:T(8,128)(2,1)} %bitcast.31), channel_id=1, source_target_pairs={{0,8},{8,0},{16,24},{24,16},{32,40},{40,32},{48,56},{56,48},{64,72... | collective-permute-start | bytes 4128776 | tf_op jit(solution)/shard_map/ppermute | solution.py:385
  10.8 17.6 %all-to-all-start = ((bf16[16,4,3584]{2,1,0:T(4,128)(2,1)}), bf16[16,4,3584]{2,1,0:T(4,128)(2,1)S(1)}, u32[]{:S(2)}, u32[]{:S(2)}) async-start(bf16[16,4,3584]{2,1,0:T(4,128)(2,1)} %shard_map.102), calls=%async_computation | async-start | bytes 917504 | tf_op jit(solution)/shard_map/all_to_all | solution.py:390
  18.3 60.9 %all-gather.3.cloned.1.call-start = ((), (), s32[]{:S(2)}) async-start(), calls=%async_computation.5 | async-start | bytes 4128768 | tf_op jit(solution)/shard_map/all_gather | solution.py:402
  18.3 5.8 %copy-start.4 = (bf16[192,3584]{1,0:T(8,128)(2,1)}, bf16[192,3584]{1,0:T(8,128)(2,1)S(1)}, u32[]{:S(2)}) copy-start(bf16[192,3584]{1,0:T(8,128)(2,1)S(1)} %collective-permute-done.g1) | copy-start | bytes 4128772
  18.4 5.8 %copy-start.5 = (bf16[192,3584]{1,0:T(8,128)(2,1)}, bf16[192,3584]{1,0:T(8,128)(2,1)S(1)}, u32[]{:S(2)}) copy-start(bf16[192,3584]{1,0:T(8,128)(2,1)S(1)} %collective-permute-done.1.u1) | copy-start | bytes 4128772
  29.3 114.9 %reduce-scatter.2.cloned.1.call-start = ((), (), s32[]{:S(2)}) async-start(), calls=%async_computation.4 | async-start | bytes 4128768 | tf_op jit(solution)/shard_map/reduce_scatter | solution.py:409
  94.3 1.3 copy-start.2
  95.6 2.0 %copy-start = (bf16[16,32,3584]{2,1,0:T(8,128)(2,1)S(1)}, bf16[16,32,3584]{2,1,0:T(8,128)(2,1)}, u32[]{:S(2)}) copy-start(bf16[16,32,3584]{2,1,0:T(8,128)(2,1)} %all_to_all.15) | copy-start | bytes 11010052
  97.6 2.0 %copy-start.1 = (bf16[16,32,3584]{2,1,0:T(8,128)(2,1)S(1)}, bf16[16,32,3584]{2,1,0:T(8,128)(2,1)}, u32[]{:S(2)}) copy-start(bf16[16,32,3584]{2,1,0:T(8,128)(2,1)} %all-gather.3.cloned.1.call-done) | copy-start | bytes 11010052
  104.8 56.2 %copy-start.3 = (s32[128,2]{0,1:T(2,128)S(1)}, s32[128,2]{0,1:T(2,128)}, u32[]{:S(2)}) copy-start(s32[128,2]{0,1:T(2,128)} %param.9) | copy-start | bytes 3076
  104.8 7.2 %collective-permute-start.3 = (bf16[576,3584]{1,0:T(8,128)(2,1)S(1)}, bf16[576,3584]{1,0:T(8,128)(2,1)S(1)}, u32[]{:S(2)}, u32[]{:S(2)}) collective-permute-start(bf16[576,3584]{1,0:T(8,128)(2,1)S(1)} %shard_map.106), channel_id=1, source_target_pairs={{0,8},{8,0},{16,24},{24,16},{32,40},{40,32},{48,56},{56,48},{64,72... | collective-permute-start | bytes 12386312 | tf_op jit(solution)/shard_map/ppermute | solution.py:385
  161.5 5.2 %collective-permute-start.5 = (bf16[128,448]{1,0:T(8,128)(2,1)S(1)}, bf16[128,448]{1,0:T(8,128)(2,1)S(1)}, u32[]{:S(2)}, u32[]{:S(2)}) collective-permute-start(bf16[128,448]{1,0:T(8,128)(2,1)S(1)} %shard_map.108.refs_0_), channel_id=1, source_target_pairs={{0,7},{1,0},{2,1},{3,2},{4,3},{5,4},{6,5},{7,6},{8,15},{9,8},{10,9... | collective-permute-start | bytes 344072 | tf_op jit(solution)/shard_map/ppermute | solution.py:357
  163.1 6.2 %collective-permute-start.4 = (bf16[128,448]{1,0:T(8,128)(2,1)S(1)}, bf16[128,448]{1,0:T(8,128)(2,1)S(1)}, u32[]{:S(2)}, u32[]{:S(2)}) collective-permute-start(bf16[128,448]{1,0:T(8,128)(2,1)S(1)} %shard_map.108.refs_0_), channel_id=1, source_target_pairs={{0,1},{1,2},{2,3},{3,4},{4,5},{5,6},{6,7},{7,0},{8,9},{9,10},{10,1... | collective-permute-start | bytes 344072 | tf_op jit(solution)/shard_map/ppermute | solution.py:356
  166.7 5.6 %collective-permute-start.7 = (bf16[128,448]{1,0:T(8,128)(2,1)S(1)}, bf16[128,448]{1,0:T(8,128)(2,1)S(1)}, u32[]{:S(2)}, u32[]{:S(2)}) collective-permute-start(bf16[128,448]{1,0:T(8,128)(2,1)S(1)} %collective-permute-done.5.refs_2_), channel_id=1, source_target_pairs={{0,7},{1,0},{2,1},{3,2},{4,3},{5,4},{6,5},{7,6},{8,15},{9,8},{10,9... | collective-permute-start | bytes 344072 | tf_op jit(solution)/shard_map/ppermute | solution.py:357
  169.3 6.2 %collective-permute-start.6 = (bf16[128,448]{1,0:T(8,128)(2,1)S(1)}, bf16[128,448]{1,0:T(8,128)(2,1)S(1)}, u32[]{:S(2)}, u32[]{:S(2)}) collective-permute-start(bf16[128,448]{1,0:T(8,128)(2,1)S(1)} %collective-permute-done.4.refs_1_), channel_id=1, source_target_pairs={{0,1},{1,2},{2,3},{3,4},{4,5},{5,6},{6,7},{7,0},{8,9},{9,10},{10,1... | collective-permute-start | bytes 344072 | tf_op jit(solution)/shard_map/ppermute | solution.py:356
  172.3 6.4 %collective-permute-start.9 = (bf16[128,448]{1,0:T(8,128)(2,1)S(1)}, bf16[128,448]{1,0:T(8,128)(2,1)S(1)}, u32[]{:S(2)}, u32[]{:S(2)}) collective-permute-start(bf16[128,448]{1,0:T(8,128)(2,1)S(1)} %collective-permute-done.7.refs_4_), channel_id=1, source_target_pairs={{0,7},{1,0},{2,1},{3,2},{4,3},{5,4},{6,5},{7,6},{8,15},{9,8},{10,9... | collective-permute-start | bytes 344072 | tf_op jit(solution)/shard_map/ppermute | solution.py:357
  175.5 6.9 %collective-permute-start.8 = (bf16[128,448]{1,0:T(8,128)(2,1)S(1)}, bf16[128,448]{1,0:T(8,128)(2,1)S(1)}, u32[]{:S(2)}, u32[]{:S(2)}) collective-permute-start(bf16[128,448]{1,0:T(8,128)(2,1)S(1)} %collective-permute-done.6.refs_3_), channel_id=1, source_target_pairs={{0,1},{1,2},{2,3},{3,4},{4,5},{5,6},{6,7},{7,0},{8,9},{9,10},{10,1... | collective-permute-start | bytes 344072 | tf_op jit(solution)/shard_map/ppermute | solution.py:356
  178.7 5.6 %collective-permute-start.11 = (bf16[64,448]{1,0:T(8,128)(2,1)S(1)}, bf16[64,448]{1,0:T(8,128)(2,1)S(1)}, u32[]{:S(2)}, u32[]{:S(2)}) collective-permute-start(bf16[64,448]{1,0:T(8,128)(2,1)S(1)} %slice.9), channel_id=1, source_target_pairs={{0,7},{1,0},{2,1},{3,2},{4,3},{5,4},{6,5},{7,6},{8,15},{9,8},{10,9... | collective-permute-start | bytes 172040 | tf_op jit(solution)/shard_map/ppermute | solution.py:360
  182.4 5.5 %collective-permute-start.10 = (bf16[64,448]{1,0:T(8,128)(2,1)S(1)}, bf16[64,448]{1,0:T(8,128)(2,1)S(1)}, u32[]{:S(2)}, u32[]{:S(2)}) collective-permute-start(bf16[64,448]{1,0:T(8,128)(2,1)S(1)} %slice.8), channel_id=1, source_target_pairs={{0,1},{1,2},{2,3},{3,4},{4,5},{5,6},{6,7},{7,0},{8,9},{9,10},{10,1... | collective-permute-start | bytes 172040 | tf_op jit(solution)/shard_map/ppermute | solution.py:359
Sparse Core Ops, SparseCore 0:
  29.4 49.7 all-gather.2
  94.5 49.7 reduce-scatter.1

commit v10 on v9

--- a/solution.py
+++ b/solution.py
@@ -339,9 +339,7 @@
     for step in range(1, reach + 1):
         kept[lax.rem(me + count - step, count)] = pieces[2 * step - 1][...]
         kept[lax.rem(me + step, count)] = pieces[2 * step][...]
-    far = lax.rem(me + count // 2, count)
-    kept[far, : toks // 2] = pieces[-2][...]
-    kept[far, toks // 2 :] = pieces[-1][...]
+    kept[lax.rem(me + count // 2, count)] = pieces[-1][...]
     for k in range(0, count, 2):
         out_ref[:, k * wide : (k + 2) * wide] = jnp.concatenate([kept[k], kept[k + 1]], axis=1)
 
@@ -356,8 +354,7 @@
         from_below = lax.ppermute(from_below, "tp", up)
         from_above = lax.ppermute(from_above, "tp", down)
         pieces += [from_below, from_above]
-    pieces.append(lax.ppermute(from_below[: toks // 2], "tp", up))
-    pieces.append(lax.ppermute(from_above[toks // 2 :], "tp", down))
+    pieces.append(lax.ppermute(from_below, "tp", up))
     return pl.pallas_call(
         order_kernel,
         in_specs=[pl.BlockSpec(memory_space=pltpu.SMEM)]

time: 197 us -> 196 us (level)
    ppermute x3, waiting for transfers between devices: 0.07 us -> 9.81 us  [gather_columns(): from_below = lax.ppermute(from_below, 'tp', up)]
    ppermute x3, waiting for transfers between devices: 9.07 us -> 0.01 us  [gather_columns(): from_above = lax.ppermute(from_above, 'tp', down)]
    ppermute x2 -> x1, starting transfers between devices: 3.75 us -> 0.01 us  [gather_columns(): pieces.append(lax.ppermute(from_below, 'tp', up))]
    ppermute x3, starting transfers between devices: 7.41 us -> 9.71 us  [gather_columns(): from_above = lax.ppermute(from_above, 'tp', down)]
    ppermute x2 -> x1, waiting for transfers between devices: 5.46 us -> 6.17 us  [gather_columns(): pieces.append(lax.ppermute(from_below, 'tp', up))]
  transfers between devices with their start and end apart: 15 -> 14, of which waited for: 9 -> 8; matrix products, arithmetic and copies ran while one was open for 0% -> 0% of each run, Pallas kernels for 10% -> 10%
where the time goes in v10:
time: 196 us
  blocking collectives  66.2 us (34%)
  waiting for transfers between devices  54.9 us (28%)
  Pallas kernels  36.5 us (19%)
  starting transfers between devices  18.3 us (9%)
  between operations  14.2 us (7%)
  local copies, waits for them, and re-layouts  5.34 us (3%)
    all_to_all x2, blocking collectives, spread(): lax.all_to_all(v, 'exp', split_axis=0, concat_axis=0, tiled=True, axis_in...  66.2 us
    reduce_scatter x1, waiting for transfers between devices, per_device(): mine = lax.psum_scatter(both, 'tp', scatter_dimension=0, tiled=False)  27.3 us
    pallas_call x1, Pallas kernels, expert_part(): pl.pallas_call(expert_kernel, grid=(2, steps), in_specs=[pl.BlockSpec(src...  15.1 us
    pallas_call x2, Pallas kernels, weight_grads(): pl.pallas_call(functools.partial(weight_kernel, base), grid=(width // til...  10.1 us
    ppermute x3, waiting for transfers between devices, gather_columns(): from_below = lax.ppermute(from_below, 'tp', up)  9.81 us
    ppermute x3, starting transfers between devices, gather_columns(): from_above = lax.ppermute(from_above, 'tp', down)  9.71 us
    all_to_all x1, starting transfers between devices, spread(): lax.all_to_all(v, 'exp', split_axis=0, concat_axis=0, tiled=True, axis_in...  7.49 us
    ppermute x4, waiting for transfers between devices, trade(): return lax.ppermute(v, 'exp', swap)  7.06 us
  transfers between devices with their start and end apart: 14, of which 8 were waited for; matrix products, arithmetic and copies ran while one was open for 0% of the time, Pallas kernels for 10%

profile of v10, /device:TPU:2, one launch (start us, length us, event | category | flops | bytes accessed | tf_op | source)
XLA Modules:
  0.0 195.5 jit_solution(2377932205766978294)
XLA Ops:
  7.2 0.1 collective-permute-start
  7.3 0.5 collective-permute-start.1
  7.8 0.1 collective-permute-start.2
  7.9 2.9 %shard_map.102 = bf16[16,4,3584]{2,1,0:T(4,128)(2,1)} custom-call(s32[1]{0:T(128)} %bitcast.tp_ref, s32[2,128]{1,0:T(2,128)} %bitcast.20, f32[2,128]{1,0:T(2,128)} %bitcast.25, bf16[128,3584]{1,0:T(8,128)(2,1)} %act_ref.1, bf16[128,3584]{1,0:T(8,128)(2,1)} %grad_ref.1), custom_call_target="tpu_custom_call" | custom-call | tf_op jit(solution)/shard_map/pallas_call | solution.py:102
  10.8 7.5 %all-to-all-start = ((bf16[16,4,3584]{2,1,0:T(4,128)(2,1)}), bf16[16,4,3584]{2,1,0:T(4,128)(2,1)S(1)}, u32[]{:S(2)}, u32[]{:S(2)}) async-start(bf16[16,4,3584]{2,1,0:T(4,128)(2,1)} %shard_map.102), calls=%async_computation | async-start | bytes 917504 | tf_op jit(solution)/shard_map/all_to_all | solution.py:387
  18.3 0.0 all-gather.3.cloned.1.call-start
  18.3 0.0 collective-permute-done.g1
  18.3 0.0 copy-start.4
  18.4 0.0 collective-permute-done.1.u1
  18.4 0.0 copy-start.5
  18.4 0.0 collective-permute-done.2.d1
  18.4 5.7 %shard_map.103 = bf16[16,2,16,3584]{3,2,1,0:T(8,128)(2,1)} custom-call(s32[2,128]{1,0:T(2,128)} %bitcast.21, f32[2,128]{1,0:T(2,128)} %bitcast.26, bf16[128,3584]{1,0:T(8,128)(2,1)} %act_ref.1, bf16[128,3584]{1,0:T(8,128)(2,1)} %grad_ref.1), custom_call_target="tpu_custom_call" | custom-call | flops 1879048192 | bytes 5505024 | tf_op jit(solution)/shard_map/pallas_call | solution.py:80
  24.1 0.0 copy-done.4
  24.1 4.2 %all-to-all-done.in_ref = bf16[16,4,3584]{2,1,0:T(4,128)(2,1)S(1)} async-done(((bf16[16,4,3584]{2,1,0:T(4,128)(2,1)}), bf16[16,4,3584]{2,1,0:T(4,128)(2,1)S(1)}, u32[]{:S(2)}, u32[]{:S(2)}) %all-to-all-start) | async-done | bytes 458784 | tf_op jit(solution)/shard_map/all_to_all | solution.py:387
  28.4 0.9 shard_map.104
  29.3 0.0 all-gather.3.cloned.1.call-update
  29.3 0.0 reduce-scatter.2.cloned.1.call-start
  29.4 49.5 %all_to_all.15 = bf16[16,32,3584]{2,1,0:T(8,128)(2,1)} all-to-all(bf16[16,32,3584]{2,1,0:T(8,128)(2,1)} %bitcast.23), channel_id=1, replica_groups={{0,16,32,48,64,80,96,112,128,144,160,176,192,208,224,240},{8,24,40,56,7..., dimensions={0} | all-to-all | bytes 7340032 | tf_op jit(solution)/shard_map/all_to_all | solution.py:387
  78.9 0.3 all-gather.3.cloned.1.call-done
  79.2 15.1 %shard_map.105 = (bf16[8,256,896]{2,1,0:T(8,128)(2,1)}, bf16[512,1152]{1,0:T(8,128)(2,1)}) custom-call(bf16[16,2,16,3584]{3,2,1,0:T(8,128)(2,1)} %bitcast.14, bf16[8,2,32,3584]{3,2,1,0:T(8,128)(2,1)} %bitcast.17, bf16[192,3584]{1,0:T(8,128)(2,1)} %bitcast.28, bf16[192,3584]{1,0:T(8,128)(2,1)} %bitcast.30, bf16[192,3584]{1,0:T(8,128)(2,1)} %copy-done.4, ...), custom_call_target="tpu_custom_call" | custom-call | flops 7046430720 | bytes 19267584 | tf_op jit(solution)/shard_map/pallas_call | solution.py:214
  94.3 0.0 copy-start.2
  94.3 0.0 reduce-scatter.2.cloned.1.call-update
  94.4 1.2 copy-done.2
  95.6 2.0 %copy-done = bf16[16,32,3584]{2,1,0:T(8,128)(2,1)S(1)} copy-done((bf16[16,32,3584]{2,1,0:T(8,128)(2,1)S(1)}, bf16[16,32,3584]{2,1,0:T(8,128)(2,1)}, u32[]{:S(2)}) %copy-start) | copy-done | bytes 3670040
  97.6 2.0 %copy-done.1 = bf16[16,32,3584]{2,1,0:T(8,128)(2,1)S(1)} copy-done((bf16[16,32,3584]{2,1,0:T(8,128)(2,1)S(1)}, bf16[16,32,3584]{2,1,0:T(8,128)(2,1)}, u32[]{:S(2)}) %copy-start.1) | copy-done | bytes 3670040
  99.7 5.1 %shard_map.106 = bf16[576,3584]{1,0:T(8,128)(2,1)S(1)} custom-call(bf16[16,2,16,3584]{3,2,1,0:T(8,128)(2,1)S(1)} %bitcast.15, bf16[8,2,32,3584]{3,2,1,0:T(8,128)(2,1)S(1)} %bitcast.18, bf16[512,1152]{1,0:T(8,128)(2,1)S(1)} %copy-done.2), custom_call_target="tpu_custom_call" | custom-call | flops 2113929216 | bytes 15597568 | tf_op jit(solution)/shard_map/pallas_call | solution.py:290
  104.8 0.0 copy-start.3
  104.8 0.1 collective-permute-start.3
  104.9 7.1 %collective-permute-done.3.refs_0_ = bf16[576,3584]{1,0:T(8,128)(2,1)S(1)} collective-permute-done((bf16[576,3584]{1,0:T(8,128)(2,1)S(1)}, bf16[576,3584]{1,0:T(8,128)(2,1)S(1)}, u32[]{:S(2)}, u32[]{:S(2)}) %collective-permute-start.3) | collective-permute-done | bytes 4128800 | tf_op jit(solution)/shard_map/ppermute | solution.py:382
  111.9 5.0 %shard_map.107 = (bf16[192,3584]{1,0:T(8,128)(2,1)}, bf16[192,3584]{1,0:T(8,128)(2,1)}, bf16[192,3584]{1,0:T(8,128)(2,1)}) custom-call(bf16[16,2,16,3584]{3,2,1,0:T(8,128)(2,1)S(1)} %bitcast.16, bf16[8,2,32,3584]{3,2,1,0:T(8,128)(2,1)S(1)} %bitcast.19, bf16[512,1152]{1,0:T(8,128)(2,1)S(1)} %copy-done.2, bf16[576,3584]{1,0:T(8,128)(2,1)S(1)} %collective-permute-done.3.refs_0_), custom_call_target="tpu_custom_call" | custom-call | flops 2113929216 | bytes 15597568 | tf_op jit(solution)/shard_map/pallas_call | solution.py:290
  116.9 27.3 %reduce-scatter.2.cloned.1.call-done = bf16[1,256,896]{2,1,0:T(8,128)(2,1)} async-done(((bf16[8,256,896]{2,1,0:T(8,128)(2,1)}), bf16[1,256,896]{2,1,0:T(8,128)(2,1)}) %reduce-scatter.2.cloned.1.call-update) | async-done | bytes 458768 | tf_op jit(solution)/shard_map/reduce_scatter | solution.py:406
  144.2 16.7 %all_to_all.16.back_ref = bf16[16,16,896]{2,1,0:T(8,128)(2,1)S(1)} all-to-all(bf16[16,16,896]{2,1,0:T(8,128)(2,1)} %bitcast.24), channel_id=1, replica_groups={{0,16,32,48,64,80,96,112,128,144,160,176,192,208,224,240},{8,24,40,56,7..., dimensions={0} | all-to-all | bytes 917504 | tf_op jit(solution)/shard_map/all_to_all | solution.py:387
  161.0 0.5 shard_map.108.refs_0_
  161.5 0.3 collective-permute-start.4
  161.7 3.2 %collective-permute-start.5 = (bf16[128,448]{1,0:T(8,128)(2,1)S(1)}, bf16[128,448]{1,0:T(8,128)(2,1)S(1)}, u32[]{:S(2)}, u32[]{:S(2)}) collective-permute-start(bf16[128,448]{1,0:T(8,128)(2,1)S(1)} %shard_map.108.refs_0_), channel_id=1, source_target_pairs={{0,7},{1,0},{2,1},{3,2},{4,3},{5,4},{6,5},{7,6},{8,15},{9,8},{10,9... | collective-permute-start | bytes 344072 | tf_op jit(solution)/shard_map/ppermute | solution.py:355
  165.0 2.9 %collective-permute-done.4.refs_1_ = bf16[128,448]{1,0:T(8,128)(2,1)S(1)} collective-permute-done((bf16[128,448]{1,0:T(8,128)(2,1)S(1)}, bf16[128,448]{1,0:T(8,128)(2,1)S(1)}, u32[]{:S(2)}, u32[]{:S(2)}) %collective-permute-start.4) | collective-permute-done | bytes 114720 | tf_op jit(solution)/shard_map/ppermute | solution.py:354
  167.9 0.0 collective-permute-start.6
  167.9 0.0 collective-permute-done.5.refs_2_
  167.9 3.2 %collective-permute-start.7 = (bf16[128,448]{1,0:T(8,128)(2,1)S(1)}, bf16[128,448]{1,0:T(8,128)(2,1)S(1)}, u32[]{:S(2)}, u32[]{:S(2)}) collective-permute-start(bf16[128,448]{1,0:T(8,128)(2,1)S(1)} %collective-permute-done.5.refs_2_), channel_id=1, source_target_pairs={{0,7},{1,0},{2,1},{3,2},{4,3},{5,4},{6,5},{7,6},{8,15},{9,8},{10,9... | collective-permute-start | bytes 344072 | tf_op jit(solution)/shard_map/ppermute | solution.py:355
  171.2 2.9 %collective-permute-done.6.refs_3_ = bf16[128,448]{1,0:T(8,128)(2,1)S(1)} collective-permute-done((bf16[128,448]{1,0:T(8,128)(2,1)S(1)}, bf16[128,448]{1,0:T(8,128)(2,1)S(1)}, u32[]{:S(2)}, u32[]{:S(2)}) %collective-permute-start.6) | collective-permute-done | bytes 114720 | tf_op jit(solution)/shard_map/ppermute | solution.py:354
  174.1 0.0 collective-permute-start.8
  174.1 0.0 collective-permute-done.7.refs_4_
  174.1 3.3 %collective-permute-start.9 = (bf16[128,448]{1,0:T(8,128)(2,1)S(1)}, bf16[128,448]{1,0:T(8,128)(2,1)S(1)}, u32[]{:S(2)}, u32[]{:S(2)}) collective-permute-start(bf16[128,448]{1,0:T(8,128)(2,1)S(1)} %collective-permute-done.7.refs_4_), channel_id=1, source_target_pairs={{0,7},{1,0},{2,1},{3,2},{4,3},{5,4},{6,5},{7,6},{8,15},{9,8},{10,9... | collective-permute-start | bytes 344072 | tf_op jit(solution)/shard_map/ppermute | solution.py:355
  177.4 3.9 %collective-permute-done.8.refs_5_ = bf16[128,448]{1,0:T(8,128)(2,1)S(1)} collective-permute-done((bf16[128,448]{1,0:T(8,128)(2,1)S(1)}, bf16[128,448]{1,0:T(8,128)(2,1)S(1)}, u32[]{:S(2)}, u32[]{:S(2)}) %collective-permute-start.8) | collective-permute-done | bytes 114720 | tf_op jit(solution)/shard_map/ppermute | solution.py:354
  181.3 0.0 collective-permute-start.10
  181.3 0.0 collective-permute-done.9.refs_6_
  181.3 6.2 %collective-permute-done.10.refs_7_ = bf16[128,448]{1,0:T(8,128)(2,1)S(1)} collective-permute-done((bf16[128,448]{1,0:T(8,128)(2,1)S(1)}, bf16[128,448]{1,0:T(8,128)(2,1)S(1)}, u32[]{:S(2)}, u32[]{:S(2)}) %collective-permute-start.10) | collective-permute-done | bytes 114720 | tf_op jit(solution)/shard_map/ppermute | solution.py:357
  187.5 1.2 shard_map.109
  (4 shorter events, 0.0 us)
Async XLA Ops:
  7.2 11.2 %collective-permute-start = (bf16[192,3584]{1,0:T(8,128)(2,1)}, bf16[192,3584]{1,0:T(8,128)(2,1)S(1)}, u32[]{:S(2)}, u32[]{:S(2)}) collective-permute-start(bf16[192,3584]{1,0:T(8,128)(2,1)} %bitcast.27), channel_id=1, source_target_pairs={{0,8},{8,0},{16,24},{24,16},{32,40},{40,32},{48,56},{56,48},{64,72... | collective-permute-start | bytes 4128776 | tf_op jit(solution)/shard_map/ppermute | solution.py:382
  7.3 11.1 %collective-permute-start.1 = (bf16[192,3584]{1,0:T(8,128)(2,1)}, bf16[192,3584]{1,0:T(8,128)(2,1)S(1)}, u32[]{:S(2)}, u32[]{:S(2)}) collective-permute-start(bf16[192,3584]{1,0:T(8,128)(2,1)} %bitcast.29), channel_id=1, source_target_pairs={{0,8},{8,0},{16,24},{24,16},{32,40},{40,32},{48,56},{56,48},{64,72... | collective-permute-start | bytes 4128776 | tf_op jit(solution)/shard_map/ppermute | solution.py:382
  7.8 10.6 %collective-permute-start.2 = (bf16[192,3584]{1,0:T(8,128)(2,1)}, bf16[192,3584]{1,0:T(8,128)(2,1)}, u32[]{:S(2)}, u32[]{:S(2)}) collective-permute-start(bf16[192,3584]{1,0:T(8,128)(2,1)} %bitcast.31), channel_id=1, source_target_pairs={{0,8},{8,0},{16,24},{24,16},{32,40},{40,32},{48,56},{56,48},{64,72... | collective-permute-start | bytes 4128776 | tf_op jit(solution)/shard_map/ppermute | solution.py:382
  10.8 17.6 %all-to-all-start = ((bf16[16,4,3584]{2,1,0:T(4,128)(2,1)}), bf16[16,4,3584]{2,1,0:T(4,128)(2,1)S(1)}, u32[]{:S(2)}, u32[]{:S(2)}) async-start(bf16[16,4,3584]{2,1,0:T(4,128)(2,1)} %shard_map.102), calls=%async_computation | async-start | bytes 917504 | tf_op jit(solution)/shard_map/all_to_all | solution.py:387
  18.3 60.9 %all-gather.3.cloned.1.call-start = ((), (), s32[]{:S(2)}) async-start(), calls=%async_computation.5 | async-start | bytes 4128768 | tf_op jit(solution)/shard_map/all_gather | solution.py:399
  18.3 5.8 %copy-start.4 = (bf16[192,3584]{1,0:T(8,128)(2,1)}, bf16[192,3584]{1,0:T(8,128)(2,1)S(1)}, u32[]{:S(2)}) copy-start(bf16[192,3584]{1,0:T(8,128)(2,1)S(1)} %collective-permute-done.g1) | copy-start | bytes 4128772
  18.4 5.8 %copy-start.5 = (bf16[192,3584]{1,0:T(8,128)(2,1)}, bf16[192,3584]{1,0:T(8,128)(2,1)S(1)}, u32[]{:S(2)}) copy-start(bf16[192,3584]{1,0:T(8,128)(2,1)S(1)} %collective-permute-done.1.u1) | copy-start | bytes 4128772
  29.3 114.9 %reduce-scatter.2.cloned.1.call-start = ((), (), s32[]{:S(2)}) async-start(), calls=%async_computation.4 | async-start | bytes 4128768 | tf_op jit(solution)/shard_map/reduce_scatter | solution.py:406
  94.3 1.3 copy-start.2
  95.6 2.0 %copy-start = (bf16[16,32,3584]{2,1,0:T(8,128)(2,1)S(1)}, bf16[16,32,3584]{2,1,0:T(8,128)(2,1)}, u32[]{:S(2)}) copy-start(bf16[16,32,3584]{2,1,0:T(8,128)(2,1)} %all_to_all.15) | copy-start | bytes 11010052
  97.6 2.0 %copy-start.1 = (bf16[16,32,3584]{2,1,0:T(8,128)(2,1)S(1)}, bf16[16,32,3584]{2,1,0:T(8,128)(2,1)}, u32[]{:S(2)}) copy-start(bf16[16,32,3584]{2,1,0:T(8,128)(2,1)} %all-gather.3.cloned.1.call-done) | copy-start | bytes 11010052
  104.8 56.2 %copy-start.3 = (s32[128,2]{0,1:T(2,128)S(1)}, s32[128,2]{0,1:T(2,128)}, u32[]{:S(2)}) copy-start(s32[128,2]{0,1:T(2,128)} %param.9) | copy-start | bytes 3076
  104.8 7.2 %collective-permute-start.3 = (bf16[576,3584]{1,0:T(8,128)(2,1)S(1)}, bf16[576,3584]{1,0:T(8,128)(2,1)S(1)}, u32[]{:S(2)}, u32[]{:S(2)}) collective-permute-start(bf16[576,3584]{1,0:T(8,128)(2,1)S(1)} %shard_map.106), channel_id=1, source_target_pairs={{0,8},{8,0},{16,24},{24,16},{32,40},{40,32},{48,56},{56,48},{64,72... | collective-permute-start | bytes 12386312 | tf_op jit(solution)/shard_map/ppermute | solution.py:382
  161.5 6.4 %collective-permute-start.4 = (bf16[128,448]{1,0:T(8,128)(2,1)S(1)}, bf16[128,448]{1,0:T(8,128)(2,1)S(1)}, u32[]{:S(2)}, u32[]{:S(2)}) collective-permute-start(bf16[128,448]{1,0:T(8,128)(2,1)S(1)} %shard_map.108.refs_0_), channel_id=1, source_target_pairs={{0,1},{1,2},{2,3},{3,4},{4,5},{5,6},{6,7},{7,0},{8,9},{9,10},{10,1... | collective-permute-start | bytes 344072 | tf_op jit(solution)/shard_map/ppermute | solution.py:354
  161.7 6.2 %collective-permute-start.5 = (bf16[128,448]{1,0:T(8,128)(2,1)S(1)}, bf16[128,448]{1,0:T(8,128)(2,1)S(1)}, u32[]{:S(2)}, u32[]{:S(2)}) collective-permute-start(bf16[128,448]{1,0:T(8,128)(2,1)S(1)} %shard_map.108.refs_0_), channel_id=1, source_target_pairs={{0,7},{1,0},{2,1},{3,2},{4,3},{5,4},{6,5},{7,6},{8,15},{9,8},{10,9... | collective-permute-start | bytes 344072 | tf_op jit(solution)/shard_map/ppermute | solution.py:355
  167.9 6.2 %collective-permute-start.6 = (bf16[128,448]{1,0:T(8,128)(2,1)S(1)}, bf16[128,448]{1,0:T(8,128)(2,1)S(1)}, u32[]{:S(2)}, u32[]{:S(2)}) collective-permute-start(bf16[128,448]{1,0:T(8,128)(2,1)S(1)} %collective-permute-done.4.refs_1_), channel_id=1, source_target_pairs={{0,1},{1,2},{2,3},{3,4},{4,5},{5,6},{6,7},{7,0},{8,9},{9,10},{10,1... | collective-permute-start | bytes 344072 | tf_op jit(solution)/shard_map/ppermute | solution.py:354
  167.9 6.2 %collective-permute-start.7 = (bf16[128,448]{1,0:T(8,128)(2,1)S(1)}, bf16[128,448]{1,0:T(8,128)(2,1)S(1)}, u32[]{:S(2)}, u32[]{:S(2)}) collective-permute-start(bf16[128,448]{1,0:T(8,128)(2,1)S(1)} %collective-permute-done.5.refs_2_), channel_id=1, source_target_pairs={{0,7},{1,0},{2,1},{3,2},{4,3},{5,4},{6,5},{7,6},{8,15},{9,8},{10,9... | collective-permute-start | bytes 344072 | tf_op jit(solution)/shard_map/ppermute | solution.py:355
  174.1 7.2 %collective-permute-start.8 = (bf16[128,448]{1,0:T(8,128)(2,1)S(1)}, bf16[128,448]{1,0:T(8,128)(2,1)S(1)}, u32[]{:S(2)}, u32[]{:S(2)}) collective-permute-start(bf16[128,448]{1,0:T(8,128)(2,1)S(1)} %collective-permute-done.6.refs_3_), channel_id=1, source_target_pairs={{0,1},{1,2},{2,3},{3,4},{4,5},{5,6},{6,7},{7,0},{8,9},{9,10},{10,1... | collective-permute-start | bytes 344072 | tf_op jit(solution)/shard_map/ppermute | solution.py:354
  174.1 7.2 %collective-permute-start.9 = (bf16[128,448]{1,0:T(8,128)(2,1)S(1)}, bf16[128,448]{1,0:T(8,128)(2,1)S(1)}, u32[]{:S(2)}, u32[]{:S(2)}) collective-permute-start(bf16[128,448]{1,0:T(8,128)(2,1)S(1)} %collective-permute-done.7.refs_4_), channel_id=1, source_target_pairs={{0,7},{1,0},{2,1},{3,2},{4,3},{5,4},{6,5},{7,6},{8,15},{9,8},{10,9... | collective-permute-start | bytes 344072 | tf_op jit(solution)/shard_map/ppermute | solution.py:355
  181.3 6.2 %collective-permute-start.10 = (bf16[128,448]{1,0:T(8,128)(2,1)S(1)}, bf16[128,448]{1,0:T(8,128)(2,1)S(1)}, u32[]{:S(2)}, u32[]{:S(2)}) collective-permute-start(bf16[128,448]{1,0:T(8,128)(2,1)S(1)} %collective-permute-done.8.refs_5_), channel_id=1, source_target_pairs={{0,1},{1,2},{2,3},{3,4},{4,5},{5,6},{6,7},{7,0},{8,9},{9,10},{10,1... | collective-permute-start | bytes 344072 | tf_op jit(solution)/shard_map/ppermute | solution.py:357
Sparse Core Ops, SparseCore 0:
  29.4 49.7 all-gather.2
  94.5 49.7 reduce-scatter.1

commit v11 on v10

--- a/solution.py
+++ b/solution.py
@@ -354,7 +354,8 @@
         from_below = lax.ppermute(from_below, "tp", up)
         from_above = lax.ppermute(from_above, "tp", down)
         pieces += [from_below, from_above]
-    pieces.append(lax.ppermute(from_below, "tp", up))
+    across = [(i, (i + count // 2) % count) for i in range(count)]
+    pieces.append(lax.ppermute(piece, "tp", across))
     return pl.pallas_call(
         order_kernel,
         in_specs=[pl.BlockSpec(memory_space=pltpu.SMEM)]

time: 196 us -> 194 us (0.990)
  waiting for transfers between devices: 54.9 us -> 50.8 us
  starting transfers between devices: 18.3 us -> 20.8 us
    ppermute x1, waiting for transfers between devices: 6.17 us -> 0.69 us  [gather_columns(): pieces.append(lax.ppermute(piece, 'tp', across))]
    ppermute x1, starting transfers between devices: 0.01 us -> 4.28 us  [gather_columns(): pieces.append(lax.ppermute(piece, 'tp', across))]
    ppermute x3, waiting for transfers between devices: 0.01 us -> 2.98 us  [gather_columns(): from_above = lax.ppermute(from_above, 'tp', down)]
    ppermute x3, starting transfers between devices: 9.71 us -> 7.54 us  [gather_columns(): from_above = lax.ppermute(from_above, 'tp', down)]
where the time goes in v11:
time: 194 us
  blocking collectives  66.2 us (34%)
  waiting for transfers between devices  50.8 us (26%)
  Pallas kernels  36.5 us (19%)
  starting transfers between devices  20.8 us (11%)
  between operations  14.2 us (7%)
  local copies, waits for them, and re-layouts  5.34 us (3%)
    all_to_all x2, blocking collectives, spread(): lax.all_to_all(v, 'exp', split_axis=0, concat_axis=0, tiled=True, axis_in...  66.2 us
    reduce_scatter x1, waiting for transfers between devices, per_device(): mine = lax.psum_scatter(both, 'tp', scatter_dimension=0, tiled=False)  27.3 us
    pallas_call x1, Pallas kernels, expert_part(): pl.pallas_call(expert_kernel, grid=(2, steps), in_specs=[pl.BlockSpec(src...  15.1 us
    pallas_call x2, Pallas kernels, weight_grads(): pl.pallas_call(functools.partial(weight_kernel, base), grid=(width // til...  10.1 us
    ppermute x3, waiting for transfers between devices, gather_columns(): from_below = lax.ppermute(from_below, 'tp', up)  8.15 us
    ppermute x3, starting transfers between devices, gather_columns(): from_above = lax.ppermute(from_above, 'tp', down)  7.54 us
    all_to_all x1, starting transfers between devices, spread(): lax.all_to_all(v, 'exp', split_axis=0, concat_axis=0, tiled=True, axis_in...  7.49 us
    ppermute x4, waiting for transfers between devices, trade(): return lax.ppermute(v, 'exp', swap)  7.06 us
  transfers between devices with their start and end apart: 14, of which 8 were waited for; matrix products, arithmetic and copies ran while one was open for 0% of the time, Pallas kernels for 10%

profile of v11, /device:TPU:2, one launch (start us, length us, event | category | flops | bytes accessed | tf_op | source)
XLA Modules:
  0.0 193.8 jit_solution(7599929184146568726)
XLA Ops:
  7.2 0.1 collective-permute-start
  7.3 0.5 collective-permute-start.1
  7.8 0.1 collective-permute-start.2
  7.9 2.9 %shard_map.102 = bf16[16,4,3584]{2,1,0:T(4,128)(2,1)} custom-call(s32[1]{0:T(128)} %bitcast.tp_ref, s32[2,128]{1,0:T(2,128)} %bitcast.20, f32[2,128]{1,0:T(2,128)} %bitcast.25, bf16[128,3584]{1,0:T(8,128)(2,1)} %act_ref.1, bf16[128,3584]{1,0:T(8,128)(2,1)} %grad_ref.1), custom_call_target="tpu_custom_call" | custom-call | tf_op jit(solution)/shard_map/pallas_call | solution.py:102
  10.8 7.5 %all-to-all-start = ((bf16[16,4,3584]{2,1,0:T(4,128)(2,1)}), bf16[16,4,3584]{2,1,0:T(4,128)(2,1)S(1)}, u32[]{:S(2)}, u32[]{:S(2)}) async-start(bf16[16,4,3584]{2,1,0:T(4,128)(2,1)} %shard_map.102), calls=%async_computation | async-start | bytes 917504 | tf_op jit(solution)/shard_map/all_to_all | solution.py:388
  18.3 0.0 all-gather.3.cloned.1.call-start
  18.3 0.0 collective-permute-done.g1
  18.3 0.0 copy-start.4
  18.4 0.0 collective-permute-done.1.u1
  18.4 0.0 copy-start.5
  18.4 0.0 collective-permute-done.2.d1
  18.4 5.7 %shard_map.103 = bf16[16,2,16,3584]{3,2,1,0:T(8,128)(2,1)} custom-call(s32[2,128]{1,0:T(2,128)} %bitcast.21, f32[2,128]{1,0:T(2,128)} %bitcast.26, bf16[128,3584]{1,0:T(8,128)(2,1)} %act_ref.1, bf16[128,3584]{1,0:T(8,128)(2,1)} %grad_ref.1), custom_call_target="tpu_custom_call" | custom-call | flops 1879048192 | bytes 5505024 | tf_op jit(solution)/shard_map/pallas_call | solution.py:80
  24.1 0.0 copy-done.5
  24.1 4.2 %all-to-all-done.in_ref = bf16[16,4,3584]{2,1,0:T(4,128)(2,1)S(1)} async-done(((bf16[16,4,3584]{2,1,0:T(4,128)(2,1)}), bf16[16,4,3584]{2,1,0:T(4,128)(2,1)S(1)}, u32[]{:S(2)}, u32[]{:S(2)}) %all-to-all-start) | async-done | bytes 458784 | tf_op jit(solution)/shard_map/all_to_all | solution.py:388
  28.4 0.9 shard_map.104
  29.3 0.0 all-gather.3.cloned.1.call-update
  29.3 0.0 reduce-scatter.2.cloned.1.call-start
  29.4 49.5 %all_to_all.15 = bf16[16,32,3584]{2,1,0:T(8,128)(2,1)} all-to-all(bf16[16,32,3584]{2,1,0:T(8,128)(2,1)} %bitcast.23), channel_id=1, replica_groups={{0,16,32,48,64,80,96,112,128,144,160,176,192,208,224,240},{8,24,40,56,7..., dimensions={0} | all-to-all | bytes 7340032 | tf_op jit(solution)/shard_map/all_to_all | solution.py:388
  78.9 0.3 all-gather.3.cloned.1.call-done
  79.2 15.1 %shard_map.105 = (bf16[8,256,896]{2,1,0:T(8,128)(2,1)}, bf16[512,1152]{1,0:T(8,128)(2,1)}) custom-call(bf16[16,2,16,3584]{3,2,1,0:T(8,128)(2,1)} %bitcast.14, bf16[8,2,32,3584]{3,2,1,0:T(8,128)(2,1)} %bitcast.17, bf16[192,3584]{1,0:T(8,128)(2,1)} %bitcast.28, bf16[192,3584]{1,0:T(8,128)(2,1)} %bitcast.30, bf16[192,3584]{1,0:T(8,128)(2,1)} %copy-done.4, ...), custom_call_target="tpu_custom_call" | custom-call | flops 7046430720 | bytes 19267584 | tf_op jit(solution)/shard_map/pallas_call | solution.py:214
  94.3 0.0 copy-start.2
  94.3 0.0 reduce-scatter.2.cloned.1.call-update
  94.4 1.2 copy-done.2
  95.6 2.0 %copy-done = bf16[16,32,3584]{2,1,0:T(8,128)(2,1)S(1)} copy-done((bf16[16,32,3584]{2,1,0:T(8,128)(2,1)S(1)}, bf16[16,32,3584]{2,1,0:T(8,128)(2,1)}, u32[]{:S(2)}) %copy-start) | copy-done | bytes 3670040
  97.6 2.0 %copy-done.1 = bf16[16,32,3584]{2,1,0:T(8,128)(2,1)S(1)} copy-done((bf16[16,32,3584]{2,1,0:T(8,128)(2,1)S(1)}, bf16[16,32,3584]{2,1,0:T(8,128)(2,1)}, u32[]{:S(2)}) %copy-start.1) | copy-done | bytes 3670040
  99.7 5.1 %shard_map.106 = bf16[576,3584]{1,0:T(8,128)(2,1)S(1)} custom-call(bf16[16,2,16,3584]{3,2,1,0:T(8,128)(2,1)S(1)} %bitcast.15, bf16[8,2,32,3584]{3,2,1,0:T(8,128)(2,1)S(1)} %bitcast.18, bf16[512,1152]{1,0:T(8,128)(2,1)S(1)} %copy-done.2), custom_call_target="tpu_custom_call" | custom-call | flops 2113929216 | bytes 15597568 | tf_op jit(solution)/shard_map/pallas_call | solution.py:290
  104.8 0.0 copy-start.3
  104.8 0.1 collective-permute-start.3
  104.9 7.1 %collective-permute-done.3.refs_0_ = bf16[576,3584]{1,0:T(8,128)(2,1)S(1)} collective-permute-done((bf16[576,3584]{1,0:T(8,128)(2,1)S(1)}, bf16[576,3584]{1,0:T(8,128)(2,1)S(1)}, u32[]{:S(2)}, u32[]{:S(2)}) %collective-permute-start.3) | collective-permute-done | bytes 4128800 | tf_op jit(solution)/shard_map/ppermute | solution.py:383
  111.9 5.0 %shard_map.107 = (bf16[192,3584]{1,0:T(8,128)(2,1)}, bf16[192,3584]{1,0:T(8,128)(2,1)}, bf16[192,3584]{1,0:T(8,128)(2,1)}) custom-call(bf16[16,2,16,3584]{3,2,1,0:T(8,128)(2,1)S(1)} %bitcast.16, bf16[8,2,32,3584]{3,2,1,0:T(8,128)(2,1)S(1)} %bitcast.19, bf16[512,1152]{1,0:T(8,128)(2,1)S(1)} %copy-done.2, bf16[576,3584]{1,0:T(8,128)(2,1)S(1)} %collective-permute-done.3.refs_0_), custom_call_target="tpu_custom_call" | custom-call | flops 2113929216 | bytes 15597568 | tf_op jit(solution)/shard_map/pallas_call | solution.py:290
  116.9 27.3 %reduce-scatter.2.cloned.1.call-done = bf16[1,256,896]{2,1,0:T(8,128)(2,1)} async-done(((bf16[8,256,896]{2,1,0:T(8,128)(2,1)}), bf16[1,256,896]{2,1,0:T(8,128)(2,1)}) %reduce-scatter.2.cloned.1.call-update) | async-done | bytes 458768 | tf_op jit(solution)/shard_map/reduce_scatter | solution.py:407
  144.2 16.7 %all_to_all.16.back_ref = bf16[16,16,896]{2,1,0:T(8,128)(2,1)S(1)} all-to-all(bf16[16,16,896]{2,1,0:T(8,128)(2,1)} %bitcast.24), channel_id=1, replica_groups={{0,16,32,48,64,80,96,112,128,144,160,176,192,208,224,240},{8,24,40,56,7..., dimensions={0} | all-to-all | bytes 917504 | tf_op jit(solution)/shard_map/all_to_all | solution.py:388
  161.0 0.5 shard_map.108.refs_0_
  161.5 1.6 collective-permute-start.5
  163.1 0.7 collective-permute-start.4
  163.8 2.9 %collective-permute-done.5.refs_2_ = bf16[128,448]{1,0:T(8,128)(2,1)S(1)} collective-permute-done((bf16[128,448]{1,0:T(8,128)(2,1)S(1)}, bf16[128,448]{1,0:T(8,128)(2,1)S(1)}, u32[]{:S(2)}, u32[]{:S(2)}) %collective-permute-start.5) | collective-permute-done | bytes 114720 | tf_op jit(solution)/shard_map/ppermute | solution.py:355
  166.7 2.6 %collective-permute-start.7 = (bf16[128,448]{1,0:T(8,128)(2,1)S(1)}, bf16[128,448]{1,0:T(8,128)(2,1)S(1)}, u32[]{:S(2)}, u32[]{:S(2)}) collective-permute-start(bf16[128,448]{1,0:T(8,128)(2,1)S(1)} %collective-permute-done.5.refs_2_), channel_id=1, source_target_pairs={{0,7},{1,0},{2,1},{3,2},{4,3},{5,4},{6,5},{7,6},{8,15},{9,8},{10,9... | collective-permute-start | bytes 344072 | tf_op jit(solution)/shard_map/ppermute | solution.py:355
  169.3 0.0 collective-permute-done.4.refs_1_
  169.3 0.0 collective-permute-start.6
  169.3 4.3 %collective-permute-start.10 = (bf16[128,448]{1,0:T(8,128)(2,1)S(1)}, bf16[128,448]{1,0:T(8,128)(2,1)S(1)}, u32[]{:S(2)}, u32[]{:S(2)}) collective-permute-start(bf16[128,448]{1,0:T(8,128)(2,1)S(1)} %shard_map.108.refs_0_), channel_id=1, source_target_pairs={{0,4},{1,5},{2,6},{3,7},{4,0},{5,1},{6,2},{7,3},{8,12},{9,13},{10,... | collective-permute-start | bytes 344072 | tf_op jit(solution)/shard_map/ppermute | solution.py:358
  173.6 0.0 collective-permute-done.7.refs_4_
  173.6 3.3 %collective-permute-start.9 = (bf16[128,448]{1,0:T(8,128)(2,1)S(1)}, bf16[128,448]{1,0:T(8,128)(2,1)S(1)}, u32[]{:S(2)}, u32[]{:S(2)}) collective-permute-start(bf16[128,448]{1,0:T(8,128)(2,1)S(1)} %collective-permute-done.7.refs_4_), channel_id=1, source_target_pairs={{0,7},{1,0},{2,1},{3,2},{4,3},{5,4},{6,5},{7,6},{8,15},{9,8},{10,9... | collective-permute-start | bytes 344072 | tf_op jit(solution)/shard_map/ppermute | solution.py:355
  176.9 2.7 %collective-permute-done.6.refs_3_ = bf16[128,448]{1,0:T(8,128)(2,1)S(1)} collective-permute-done((bf16[128,448]{1,0:T(8,128)(2,1)S(1)}, bf16[128,448]{1,0:T(8,128)(2,1)S(1)}, u32[]{:S(2)}, u32[]{:S(2)}) %collective-permute-start.6) | collective-permute-done | bytes 114720 | tf_op jit(solution)/shard_map/ppermute | solution.py:354
  179.6 0.0 collective-permute-start.8
  179.6 0.7 collective-permute-done.10.refs_7_
  180.3 0.0 collective-permute-done.9.refs_6_
  180.3 5.4 %collective-permute-done.8.refs_5_ = bf16[128,448]{1,0:T(8,128)(2,1)S(1)} collective-permute-done((bf16[128,448]{1,0:T(8,128)(2,1)S(1)}, bf16[128,448]{1,0:T(8,128)(2,1)S(1)}, u32[]{:S(2)}, u32[]{:S(2)}) %collective-permute-start.8) | collective-permute-done | bytes 114720 | tf_op jit(solution)/shard_map/ppermute | solution.py:354
  185.8 1.2 shard_map.109
  (4 shorter events, 0.0 us)
Async XLA Ops:
  7.2 11.2 %collective-permute-start = (bf16[192,3584]{1,0:T(8,128)(2,1)}, bf16[192,3584]{1,0:T(8,128)(2,1)S(1)}, u32[]{:S(2)}, u32[]{:S(2)}) collective-permute-start(bf16[192,3584]{1,0:T(8,128)(2,1)} %bitcast.27), channel_id=1, source_target_pairs={{0,8},{8,0},{16,24},{24,16},{32,40},{40,32},{48,56},{56,48},{64,72... | collective-permute-start | bytes 4128776 | tf_op jit(solution)/shard_map/ppermute | solution.py:383
  7.3 11.1 %collective-permute-start.1 = (bf16[192,3584]{1,0:T(8,128)(2,1)}, bf16[192,3584]{1,0:T(8,128)(2,1)S(1)}, u32[]{:S(2)}, u32[]{:S(2)}) collective-permute-start(bf16[192,3584]{1,0:T(8,128)(2,1)} %bitcast.29), channel_id=1, source_target_pairs={{0,8},{8,0},{16,24},{24,16},{32,40},{40,32},{48,56},{56,48},{64,72... | collective-permute-start | bytes 4128776 | tf_op jit(solution)/shard_map/ppermute | solution.py:383
  7.8 10.6 %collective-permute-start.2 = (bf16[192,3584]{1,0:T(8,128)(2,1)}, bf16[192,3584]{1,0:T(8,128)(2,1)}, u32[]{:S(2)}, u32[]{:S(2)}) collective-permute-start(bf16[192,3584]{1,0:T(8,128)(2,1)} %bitcast.31), channel_id=1, source_target_pairs={{0,8},{8,0},{16,24},{24,16},{32,40},{40,32},{48,56},{56,48},{64,72... | collective-permute-start | bytes 4128776 | tf_op jit(solution)/shard_map/ppermute | solution.py:383
  10.8 17.6 %all-to-all-start = ((bf16[16,4,3584]{2,1,0:T(4,128)(2,1)}), bf16[16,4,3584]{2,1,0:T(4,128)(2,1)S(1)}, u32[]{:S(2)}, u32[]{:S(2)}) async-start(bf16[16,4,3584]{2,1,0:T(4,128)(2,1)} %shard_map.102), calls=%async_computation | async-start | bytes 917504 | tf_op jit(solution)/shard_map/all_to_all | solution.py:388
  18.3 60.9 %all-gather.3.cloned.1.call-start = ((), (), s32[]{:S(2)}) async-start(), calls=%async_computation.5 | async-start | bytes 4128768 | tf_op jit(solution)/shard_map/all_gather | solution.py:400
  18.3 5.8 %copy-start.4 = (bf16[192,3584]{1,0:T(8,128)(2,1)}, bf16[192,3584]{1,0:T(8,128)(2,1)S(1)}, u32[]{:S(2)}) copy-start(bf16[192,3584]{1,0:T(8,128)(2,1)S(1)} %collective-permute-done.g1) | copy-start | bytes 4128772
  18.4 5.8 %copy-start.5 = (bf16[192,3584]{1,0:T(8,128)(2,1)}, bf16[192,3584]{1,0:T(8,128)(2,1)S(1)}, u32[]{:S(2)}) copy-start(bf16[192,3584]{1,0:T(8,128)(2,1)S(1)} %collective-permute-done.1.u1) | copy-start | bytes 4128772
  29.3 114.9 %reduce-scatter.2.cloned.1.call-start = ((), (), s32[]{:S(2)}) async-start(), calls=%async_computation.4 | async-start | bytes 4128768 | tf_op jit(solution)/shard_map/reduce_scatter | solution.py:407
  94.3 1.3 copy-start.2
  95.6 2.0 %copy-start = (bf16[16,32,3584]{2,1,0:T(8,128)(2,1)S(1)}, bf16[16,32,3584]{2,1,0:T(8,128)(2,1)}, u32[]{:S(2)}) copy-start(bf16[16,32,3584]{2,1,0:T(8,128)(2,1)} %all_to_all.15) | copy-start | bytes 11010052
  97.6 2.0 %copy-start.1 = (bf16[16,32,3584]{2,1,0:T(8,128)(2,1)S(1)}, bf16[16,32,3584]{2,1,0:T(8,128)(2,1)}, u32[]{:S(2)}) copy-start(bf16[16,32,3584]{2,1,0:T(8,128)(2,1)} %all-gather.3.cloned.1.call-done) | copy-start | bytes 11010052
  104.8 56.2 %copy-start.3 = (s32[128,2]{0,1:T(2,128)S(1)}, s32[128,2]{0,1:T(2,128)}, u32[]{:S(2)}) copy-start(s32[128,2]{0,1:T(2,128)} %param.9) | copy-start | bytes 3076
  104.8 7.2 %collective-permute-start.3 = (bf16[576,3584]{1,0:T(8,128)(2,1)S(1)}, bf16[576,3584]{1,0:T(8,128)(2,1)S(1)}, u32[]{:S(2)}, u32[]{:S(2)}) collective-permute-start(bf16[576,3584]{1,0:T(8,128)(2,1)S(1)} %shard_map.106), channel_id=1, source_target_pairs={{0,8},{8,0},{16,24},{24,16},{32,40},{40,32},{48,56},{56,48},{64,72... | collective-permute-start | bytes 12386312 | tf_op jit(solution)/shard_map/ppermute | solution.py:383
  161.5 5.2 %collective-permute-start.5 = (bf16[128,448]{1,0:T(8,128)(2,1)S(1)}, bf16[128,448]{1,0:T(8,128)(2,1)S(1)}, u32[]{:S(2)}, u32[]{:S(2)}) collective-permute-start(bf16[128,448]{1,0:T(8,128)(2,1)S(1)} %shard_map.108.refs_0_), channel_id=1, source_target_pairs={{0,7},{1,0},{2,1},{3,2},{4,3},{5,4},{6,5},{7,6},{8,15},{9,8},{10,9... | collective-permute-start | bytes 344072 | tf_op jit(solution)/shard_map/ppermute | solution.py:355
  163.1 6.2 %collective-permute-start.4 = (bf16[128,448]{1,0:T(8,128)(2,1)S(1)}, bf16[128,448]{1,0:T(8,128)(2,1)S(1)}, u32[]{:S(2)}, u32[]{:S(2)}) collective-permute-start(bf16[128,448]{1,0:T(8,128)(2,1)S(1)} %shard_map.108.refs_0_), channel_id=1, source_target_pairs={{0,1},{1,2},{2,3},{3,4},{4,5},{5,6},{6,7},{7,0},{8,9},{9,10},{10,1... | collective-permute-start | bytes 344072 | tf_op jit(solution)/shard_map/ppermute | solution.py:354
  166.7 6.9 %collective-permute-start.7 = (bf16[128,448]{1,0:T(8,128)(2,1)S(1)}, bf16[128,448]{1,0:T(8,128)(2,1)S(1)}, u32[]{:S(2)}, u32[]{:S(2)}) collective-permute-start(bf16[128,448]{1,0:T(8,128)(2,1)S(1)} %collective-permute-done.5.refs_2_), channel_id=1, source_target_pairs={{0,7},{1,0},{2,1},{3,2},{4,3},{5,4},{6,5},{7,6},{8,15},{9,8},{10,9... | collective-permute-start | bytes 344072 | tf_op jit(solution)/shard_map/ppermute | solution.py:355
  169.3 10.3 %collective-permute-start.6 = (bf16[128,448]{1,0:T(8,128)(2,1)S(1)}, bf16[128,448]{1,0:T(8,128)(2,1)S(1)}, u32[]{:S(2)}, u32[]{:S(2)}) collective-permute-start(bf16[128,448]{1,0:T(8,128)(2,1)S(1)} %collective-permute-done.4.refs_1_), channel_id=1, source_target_pairs={{0,1},{1,2},{2,3},{3,4},{4,5},{5,6},{6,7},{7,0},{8,9},{9,10},{10,1... | collective-permute-start | bytes 344072 | tf_op jit(solution)/shard_map/ppermute | solution.py:354
  169.3 11.0 %collective-permute-start.10 = (bf16[128,448]{1,0:T(8,128)(2,1)S(1)}, bf16[128,448]{1,0:T(8,128)(2,1)S(1)}, u32[]{:S(2)}, u32[]{:S(2)}) collective-permute-start(bf16[128,448]{1,0:T(8,128)(2,1)S(1)} %shard_map.108.refs_0_), channel_id=1, source_target_pairs={{0,4},{1,5},{2,6},{3,7},{4,0},{5,1},{6,2},{7,3},{8,12},{9,13},{10,... | collective-permute-start | bytes 344072 | tf_op jit(solution)/shard_map/ppermute | solution.py:358
  173.6 6.8 %collective-permute-start.9 = (bf16[128,448]{1,0:T(8,128)(2,1)S(1)}, bf16[128,448]{1,0:T(8,128)(2,1)S(1)}, u32[]{:S(2)}, u32[]{:S(2)}) collective-permute-start(bf16[128,448]{1,0:T(8,128)(2,1)S(1)} %collective-permute-done.7.refs_4_), channel_id=1, source_target_pairs={{0,7},{1,0},{2,1},{3,2},{4,3},{5,4},{6,5},{7,6},{8,15},{9,8},{10,9... | collective-permute-start | bytes 344072 | tf_op jit(solution)/shard_map/ppermute | solution.py:355
  179.6 6.2 %collective-permute-start.8 = (bf16[128,448]{1,0:T(8,128)(2,1)S(1)}, bf16[128,448]{1,0:T(8,128)(2,1)S(1)}, u32[]{:S(2)}, u32[]{:S(2)}) collective-permute-start(bf16[128,448]{1,0:T(8,128)(2,1)S(1)} %collective-permute-done.6.refs_3_), channel_id=1, source_target_pairs={{0,1},{1,2},{2,3},{3,4},{4,5},{5,6},{6,7},{7,0},{8,9},{9,10},{10,1... | collective-permute-start | bytes 344072 | tf_op jit(solution)/shard_map/ppermute | solution.py:354
Sparse Core Ops, SparseCore 0:
  29.4 49.7 all-gather.2
  94.5 49.7 reduce-scatter.1
